TPU v7x, 32 devices: a whole 2x2x4 slice. The times are simulated.
32 devices in a mesh: pix: 8 (over z, x), rep: 4 (over y, core).
Axes of the slice: x: 2, y: 2, z: 4, core: 2. Of those that a mesh axis runs over, the one named last changes fastest.
Arguments:
- tokens: bfloat16 [4096, 24, 128], P(('pix', 'rep')), may hold values from -6 to 6
- lengths: int32 [4096], P(('pix', 'rep')), may hold values from 3 to 24, as said below
- masked: int32 [4096, 24], P(('pix', 'rep')), may hold values from 0 to 1, as said below
- route_dev: int32 [4096], P(('pix', 'rep')), may hold values from 0 to 7, as said below
- route_slot: int32 [4096], P(('pix', 'rep')), may hold values from 0 to 127, as said below
- norm_gain: float32 [2, 2, 128], replicated, may hold values from 0.5 to 1.5
- norm_bias: float32 [2, 2, 128], replicated, may hold values from -1.75 to 1.75
- w_qkv: bfloat16 [2, 128, 384], replicated, may hold values from -0.5 to 0.5
- w_out: bfloat16 [2, 128, 128], replicated, may hold values from -1 to 1
- w_up: bfloat16 [2, 128, 512], replicated, may hold values from -0.5 to 0.5
- b_up: float32 [2, 512], replicated, may hold values from -1.75 to 1.75
- w_down: bfloat16 [2, 512, 128], replicated, may hold values from -0.25 to 0.25
- b_down: float32 [2, 128], replicated, may hold values from -1.75 to 1.75
- mask_token: float32 [128], replicated, may hold values from -6 to 6
- pos_table: float32 [24, 128], replicated, may hold values from -3 to 3
- cotangent: bfloat16 [4096, 24, 128], P(('pix', 'rep')), may hold values from -6 to 6
Outputs:
- dec_output: float32 [4096, 24, 128], P(('pix', 'rep'))
- grad_tokens: float32 [4096, 24, 128], P(('pix', 'rep'))
- grad_norm_gain: float32 [2, 2, 128], replicated
- grad_norm_bias: float32 [2, 2, 128], replicated
- grad_w_qkv: float32 [2, 128, 384], replicated
- grad_w_out: float32 [2, 128, 128], replicated
- grad_w_up: float32 [2, 128, 512], replicated
- grad_b_up: float32 [2, 512], replicated
- grad_w_down: float32 [2, 512, 128], replicated
- grad_b_down: float32 [2, 128], replicated
- grad_mask_token: float32 [128], replicated
- grad_pos_table: float32 [24, 128], replicated
Inputs may be any that keep to these rules, and one draw needn't show every extreme that they name: `lengths`: the first series of every device has length 24. masked is 1 at and beyond the length; below it each series has 1 to 8 unmasked slots, exactly 8 in the first series of every device. Within each rep index the series form a one-to-one map onto decoder slots; route_dev minus the sender's pix index (modulo 8) and route_slot depend only on the series' slot and rep index; no device of pix sends more than 32 series to one device, and in each rep group some pair sends exactly 32. `route_slot`: every decoder slot of every device is named exactly once within its rep group.
All inputs are finite; a program needn't handle non-finite values.
Results may differ from a plain program's by a relative error of at most 0.014.
Values may be sent and summed in bfloat16 or wider, within the bound.
No kernel may reach another device: no remote copies, remote signals or barrier semaphores. Data moves between devices by JAX's collectives and lax.ppermute only.
A program may use at most 192 MiB of HBM per device.

v0:
```python
import math

import jax
import jax.numpy as jnp
from jax import lax
from jax.sharding import PartitionSpec as P

HEADS = 8
HEAD_DIM = 16
VIS = 8


def normalize(values):
    centre = jnp.mean(values, axis=-1, keepdims=True)
    centered = values - centre
    return centered * lax.rsqrt(jnp.mean(centered * centered, axis=-1, keepdims=True) + 1e-05)


def norm_affine(values, gains, shifts):
    return normalize(values) * gains + shifts


def gelu_exact(values):
    return jax.nn.gelu(values, approximate=False)


def matmul(left, right):
    return jnp.dot(left, right, preferred_element_type=jnp.float32)


def forward_layer(inputs, key_valid, gains, shifts, wqkv, wout, wup, bup, wdown, bdown):
    pixels, seq_slots, model_width = inputs.shape
    flat_rows = inputs.reshape(pixels * seq_slots, model_width)
    norm_one, first_back = jax.vjp(norm_affine, flat_rows, gains[0], shifts[0])
    first_low = norm_one.astype(jnp.bfloat16)
    projected = (
        matmul(first_low, wqkv).astype(jnp.bfloat16).reshape(pixels, seq_slots, 3, HEADS, HEAD_DIM)
    )
    queries = projected[:, :, 0]
    key_rows = projected[:, :, 1]
    value_rows = projected[:, :, 2]
    scaling = 1.0 / math.sqrt(HEAD_DIM)
    scores = (
        jnp.einsum("pshe,pthe->phst", queries, key_rows, preferred_element_type=jnp.float32)
        * scaling
    )
    scores = jnp.where(key_valid[:, None, None, :], scores, -1e30)
    attn_probs = jax.nn.softmax(scores, axis=-1)
    probs_low = attn_probs.astype(jnp.bfloat16)
    attended = jnp.einsum(
        "phst,pthe->pshe", probs_low, value_rows, preferred_element_type=jnp.float32
    )
    attended = attended.astype(jnp.bfloat16).reshape(pixels * seq_slots, model_width)
    middle = flat_rows + matmul(attended, wout)
    norm_two, second_back = jax.vjp(norm_affine, middle, gains[1], shifts[1])
    second_low = norm_two.astype(jnp.bfloat16)
    hidden = matmul(second_low, wup) + bup
    active, gelu_back = jax.vjp(gelu_exact, hidden)
    active_low = active.astype(jnp.bfloat16)
    output = middle + (matmul(active_low, wdown) + bdown)
    saved = (
        first_back,
        first_low,
        queries,
        key_rows,
        value_rows,
        attn_probs,
        probs_low,
        attended,
        second_back,
        second_low,
        gelu_back,
        active_low,
    )
    return (output.reshape(pixels, seq_slots, model_width), saved)


def backward_layer(grad_out, saved, wqkv, wout, wup, wdown):
    (
        first_back,
        first_low,
        queries,
        key_rows,
        value_rows,
        attn_probs,
        probs_low,
        attended,
        second_back,
        second_low,
        gelu_back,
        active_low,
    ) = saved
    pixels, seq_slots, model_width = grad_out.shape
    flat_grad = grad_out.reshape(pixels * seq_slots, model_width)
    grad_low = flat_grad.astype(jnp.bfloat16)
    d_wdown = matmul(active_low.T, grad_low)
    d_bdown = jnp.sum(grad_low.astype(jnp.float32), axis=0)
    d_active = matmul(grad_low, wdown.T)
    (d_hidden,) = gelu_back(d_active)
    hidden_low = d_hidden.astype(jnp.bfloat16)
    d_wup = matmul(second_low.T, hidden_low)
    d_bup = jnp.sum(hidden_low.astype(jnp.float32), axis=0)
    d_second = matmul(hidden_low, wup.T)
    d_middle, d_gain_two, d_shift_two = second_back(d_second)
    d_middle = flat_grad + d_middle
    middle_low = d_middle.astype(jnp.bfloat16)
    d_wout = matmul(attended.T, middle_low)
    d_attended = (
        matmul(middle_low, wout.T).astype(jnp.bfloat16).reshape(pixels, seq_slots, HEADS, HEAD_DIM)
    )
    d_probs = jnp.einsum(
        "pshe,pthe->phst", d_attended, value_rows, preferred_element_type=jnp.float32
    )
    d_values = jnp.einsum(
        "phst,pshe->pthe", probs_low, d_attended, preferred_element_type=jnp.float32
    )
    d_scores = attn_probs * (d_probs - jnp.sum(d_probs * attn_probs, axis=-1, keepdims=True))
    d_scores = d_scores.astype(jnp.bfloat16)
    scaling = 1.0 / math.sqrt(HEAD_DIM)
    d_queries = (
        jnp.einsum("phst,pthe->pshe", d_scores, key_rows, preferred_element_type=jnp.float32)
        * scaling
    )
    d_keys = (
        jnp.einsum("phst,pshe->pthe", d_scores, queries, preferred_element_type=jnp.float32)
        * scaling
    )
    d_mixed = jnp.stack([d_queries, d_keys, d_values], axis=2).reshape(
        pixels * seq_slots, 3 * model_width
    )
    d_mixed = d_mixed.astype(jnp.bfloat16)
    d_wqkv = matmul(first_low.T, d_mixed)
    d_first = matmul(d_mixed, wqkv.T)
    d_flat, d_gain_one, d_shift_one = first_back(d_first)
    grad_in = (d_middle + d_flat).reshape(pixels, seq_slots, model_width)
    gradients = (
        jnp.stack([d_gain_one, d_gain_two]),
        jnp.stack([d_shift_one, d_shift_two]),
        d_wqkv,
        d_wout,
        d_wup,
        d_bup,
        d_wdown,
        d_bdown,
    )
    return (grad_in, gradients)


def shards(
    tokens,
    lengths,
    masked,
    route_dev,
    route_slot,
    norm_gain,
    norm_bias,
    w_qkv,
    w_out,
    w_up,
    b_up,
    w_down,
    b_down,
    mask_token,
    pos_table,
    cotangent,
):
    pix_count = lax.axis_size("pix")
    pixels, seq_slots, model_width = tokens.shape
    capacity = max(2, (2 * pixels + pix_count - 1) // pix_count)
    slot_count = pix_count * capacity
    row_width = VIS * model_width
    positions = jnp.arange(seq_slots, dtype=jnp.int32)
    vis_slots = jnp.arange(VIS, dtype=jnp.int32)
    inside = positions[None, :] < lengths[:, None]
    visible = inside & (masked == 0)
    vis_int = visible.astype(jnp.int32)
    ranks = jnp.cumsum(vis_int, axis=1) - vis_int
    select = visible[:, None, :] & (ranks[:, None, :] == vis_slots[None, :, None])
    select_int = select.astype(jnp.int32)
    enc_in = jnp.einsum(
        "pvt,ptd->pvd", select.astype(jnp.bfloat16), tokens, preferred_element_type=jnp.float32
    )
    enc_valid = vis_slots[None, :] < jnp.sum(vis_int, axis=1)[:, None]
    slot_pos = jnp.sum(select_int * (positions[None, None, :] + 1), axis=-1)
    enc_out, enc_saved = forward_layer(
        enc_in,
        enc_valid,
        norm_gain[0],
        norm_bias[0],
        w_qkv[0],
        w_out[0],
        w_up[0],
        b_up[0],
        w_down[0],
        b_down[0],
    )
    sent = enc_out.astype(jnp.bfloat16).reshape(pixels, row_width)
    dest_hot = (route_dev[:, None] == jnp.arange(pix_count, dtype=jnp.int32)[None, :]).astype(
        jnp.int32
    )
    earlier = jnp.cumsum(dest_hot, axis=0) - dest_hot
    place_index = route_dev * capacity + jnp.sum(earlier * dest_hot, axis=1)
    placing = (jnp.arange(slot_count, dtype=jnp.int32)[:, None] == place_index[None, :]).astype(
        jnp.bfloat16
    )
    metadata = jnp.concatenate(
        [slot_pos, lengths[:, None], route_slot[:, None] + 1], axis=1
    ).astype(jnp.bfloat16)
    out_rows = matmul(placing, sent).astype(jnp.bfloat16).reshape(pix_count, capacity, row_width)
    out_meta = matmul(placing, metadata).astype(jnp.bfloat16).reshape(pix_count, capacity, VIS + 2)
    recv_rows, recv_meta = (
        lax.all_to_all(out_rows, "pix", split_axis=0, concat_axis=0, tiled=True),
        lax.all_to_all(out_meta, "pix", split_axis=0, concat_axis=0, tiled=True),
    )
    recv_meta = recv_meta.reshape(slot_count, VIS + 2)
    dest_slot = recv_meta.astype(jnp.float32).astype(jnp.int32)[:, VIS + 1] - 1
    collect = (jnp.arange(pixels, dtype=jnp.int32)[:, None] == dest_slot[None, :]).astype(
        jnp.bfloat16
    )
    dec_rows = (
        matmul(collect, recv_rows.reshape(slot_count, row_width))
        .astype(jnp.bfloat16)
        .reshape(pixels, VIS, model_width)
    )
    dec_meta = matmul(collect, recv_meta).astype(jnp.int32)
    dec_pos = dec_meta[:, :VIS] - 1
    dec_len = dec_meta[:, VIS]
    dec_select = dec_pos[:, :, None] == positions[None, None, :]
    dec_visible = jnp.any(dec_select, axis=1)
    dec_inside = positions[None, :] < dec_len[:, None]
    dec_hidden = 1.0 - dec_visible.astype(jnp.float32)
    dec_keep = dec_inside.astype(jnp.float32)
    dec_in = jnp.einsum(
        "pvt,pvd->ptd",
        dec_select.astype(jnp.bfloat16),
        dec_rows,
        preferred_element_type=jnp.float32,
    )
    dec_in = dec_in + dec_hidden[..., None] * mask_token + pos_table[None]
    dec_out, dec_saved = forward_layer(
        dec_in,
        dec_inside,
        norm_gain[1],
        norm_bias[1],
        w_qkv[1],
        w_out[1],
        w_up[1],
        b_up[1],
        w_down[1],
        b_down[1],
    )
    result = dec_out * dec_keep[..., None]
    grad_top = cotangent.astype(jnp.float32) * dec_keep[..., None]
    d_dec_in, dec_grads = backward_layer(
        grad_top, dec_saved, w_qkv[1], w_out[1], w_up[1], w_down[1]
    )
    dec_gain, dec_shift, dec_qkv, dec_outw, dec_upw, dec_upb, dec_downw, dec_downb = dec_grads
    d_mask = jnp.sum(dec_hidden[..., None] * d_dec_in, axis=(0, 1))
    d_pos = jnp.sum(d_dec_in, axis=0)
    d_rows = jnp.einsum(
        "pvt,ptd->pvd", dec_select.astype(jnp.float32), d_dec_in, precision=lax.Precision.HIGHEST
    )
    d_rows = d_rows.astype(jnp.bfloat16).reshape(pixels, row_width)
    back_rows = (
        matmul(collect.T, d_rows).astype(jnp.bfloat16).reshape(pix_count, capacity, row_width)
    )
    returned = lax.all_to_all(back_rows, "pix", split_axis=0, concat_axis=0, tiled=True)
    d_sent = matmul(placing.T, returned.reshape(slot_count, row_width)).reshape(
        pixels, VIS, model_width
    )
    d_enc_in, enc_grads = backward_layer(d_sent, enc_saved, w_qkv[0], w_out[0], w_up[0], w_down[0])
    enc_gain, enc_shift, enc_qkv, enc_outw, enc_upw, enc_upb, enc_downw, enc_downb = enc_grads
    (
        enc_gain,
        enc_shift,
        enc_qkv,
        enc_outw,
        enc_upw,
        enc_upb,
        enc_downw,
        enc_downb,
        dec_gain,
        dec_shift,
        dec_qkv,
        dec_outw,
        dec_upw,
        dec_upb,
        dec_downw,
        dec_downb,
        d_mask,
        d_pos,
    ) = lax.psum(
        (
            enc_gain,
            enc_shift,
            enc_qkv,
            enc_outw,
            enc_upw,
            enc_upb,
            enc_downw,
            enc_downb,
            dec_gain,
            dec_shift,
            dec_qkv,
            dec_outw,
            dec_upw,
            dec_upb,
            dec_downw,
            dec_downb,
            d_mask,
            d_pos,
        ),
        ("pix", "rep"),
    )
    d_tokens = jnp.einsum(
        "pvt,pvd->ptd", select.astype(jnp.float32), d_enc_in, precision=lax.Precision.HIGHEST
    )
    return (
        result,
        d_tokens,
        jnp.stack([enc_gain, dec_gain]),
        jnp.stack([enc_shift, dec_shift]),
        jnp.stack([enc_qkv, dec_qkv]),
        jnp.stack([enc_outw, dec_outw]),
        jnp.stack([enc_upw, dec_upw]),
        jnp.stack([enc_upb, dec_upb]),
        jnp.stack([enc_downw, dec_downw]),
        jnp.stack([enc_downb, dec_downb]),
        d_mask,
        d_pos,
    )


def solution(mesh):
    in_specs = (
        P(("pix", "rep"), None, None),
        P(("pix", "rep")),
        P(("pix", "rep"), None),
        P(("pix", "rep")),
        P(("pix", "rep")),
        P(),
        P(),
        P(),
        P(),
        P(),
        P(),
        P(),
        P(),
        P(),
        P(),
        P(("pix", "rep"), None, None),
    )
    out_specs = (
        P(("pix", "rep"), None, None),
        P(("pix", "rep"), None, None),
        P(),
        P(),
        P(),
        P(),
        P(),
        P(),
        P(),
        P(),
        P(),
        P(),
    )
    return jax.shard_map(shards, mesh=mesh, in_specs=in_specs, out_specs=out_specs, check_vma=False)
```

profile of v0, /device:TPU:0, one launch (start us, length us, event | category | flops | bytes accessed | tf_op | source)
XLA Modules:
  0.0 615.4 jit_solution(1078685818021360069)
XLA Ops:
  9.0 2.2 select_reduce_fusion
  15.1 7.3 %all-to-all-start = ((bf16[8,2,160]{2,1,0:T(2,128)(2,1)}), bf16[8,2,160]{2,1,0:T(2,128)(2,1)S(1)}, u32[]{:S(2)}, u32[]{:S(2)}) async-start(bf16[8,2,160]{2,1,0:T(2,128)(2,1)} %reshape.512), calls=%async_computation | async-start | bytes 16384 | tf_op jit(solution)/shard_map/all_to_all | solution.py:213
  27.7 6.1 reshape.487
  33.7 4.4 fusion.151
  40.0 14.1 %fusion.154 = (f32[128,8,8]{2,1,0:T(8,128)S(1)}, f32[128,8,8,8]{2,3,1,0:T(8,128)S(1)}) fusion(f32[128,8,8,8]{2,3,1,0:T(8,128)S(1)} %fusion.37, pred[128,8]{1,0:T(8,128)(4,1)S(1)} %iota_compare_fusion.12), kind=kOutput, calls=%fused_computation.304 | output fusion | flops 393223 | bytes 558080 | tf_op jit(solution)/shard_map/sub | solution.py:48
  59.8 7.4 %multiply_convert_fusion.7 = (bf16[1024,512]{1,0:T(8,128)(2,1)S(1)}, f32[1024,512]{1,0:T(8,128)}, f32[1024,512]{1,0:T(8,128)}) fusion(f32[512]{0:T(512)} %bitcast.311, bf16[2,128,512]{2,1,0:T(8,128)(2,1)} %param.25, f32[1024,128]{1,0:T(8,128)S(1)} %get-tuple-element.93, f32[128]{0:T(128)} %get-tuple-element.81, f32[128]{0:T(128)S(1)} %get-tuple-element.118, ...), kind=kOutput, calls=%fused_computation.67 | convolution fusion | flops 169476096 | bytes 5909504 | tf_op jit(solution)/shard_map/dot_general | solution.py:28
  71.3 6.2 %all-to-all-start.1 = ((bf16[8,32,1024]{2,1,0:T(8,128)(2,1)}), bf16[8,32,1024]{2,1,0:T(8,128)(2,1)S(1)}, u32[]{:S(2)}, u32[]{:S(2)}) async-start(bf16[8,32,1024]{2,1,0:T(8,128)(2,1)} %bitcast.19), calls=%async_computation.1 | async-start | bytes 1048576 | tf_op jit(solution)/shard_map/all_to_all | solution.py:212
  79.7 11.7 %all-to-all-done.1 = bf16[8,32,1024]{2,1,0:T(8,128)(2,1)S(1)} async-done(((bf16[8,32,1024]{2,1,0:T(8,128)(2,1)}), bf16[8,32,1024]{2,1,0:T(8,128)(2,1)S(1)}, u32[]{:S(2)}, u32[]{:S(2)}) %all-to-all-start.1) | async-done | bytes 524320 | tf_op jit(solution)/shard_map/all_to_all | solution.py:212
  91.8 2.1 fusion.156
  97.2 2.2 convolution_convert_fusion
  99.4 4.3 copy.214
  103.7 22.2 %reshape.493 = bf16[128,24,3,8,16]{1,0,4,3,2:T(8,128)(2,1)} reshape(bf16[3072,384]{0,1:T(8,128)(2,1)} %copy.214) | data formatting | bytes 4718592 | tf_op jit(solution)/shard_map/reshape | solution.py:37
  125.9 9.5 %fusion.150 = (bf16[128,24,1,8,16]{1,0,4,3,2:T(8,128)(2,1)}, bf16[128,24,1,8,16]{1,0,4,3,2:T(8,128)(2,1)S(1)}, bf16[128,24,1,8,16]{1,0,4,3,2:T(8,128)(2,1)S(1)}) fusion(bf16[128,24,3,8,16]{1,0,4,3,2:T(8,128)(2,1)} %reshape.493), kind=kLoop, calls=%fused_computation.300 | loop fusion | bytes 4718592 | tf_op jit(solution)/shard_map/slice | solution.py:41
  138.6 20.5 %fusion.15 = f32[128,8,24,24]{2,3,1,0:T(8,128)} fusion(bf16[128,24,1,8,16]{1,0,4,3,2:T(8,128)(2,1)S(1)} %get-tuple-element.61, bf16[128,24,1,8,16]{1,0,4,3,2:T(8,128)(2,1)S(1)} %get-tuple-element.62), kind=kOutput, calls=%fused_computation.45 | convolution fusion | flops 18874368 | bytes 3932160 | tf_op jit(solution)/shard_map/pshe,pthe->phst/dot_general | solution.py:44
  159.2 10.8 %copy.218 = f32[128,8,24,24]{0,3,2,1:T(8,128)} copy(f32[128,8,24,24]{2,3,1,0:T(8,128)} %fusion.15) | data formatting | bytes 4718592 | tf_op jit(solution)/shard_map/pshe,pthe->phst/dot_general | solution.py:44
  169.9 2.5 fusion.157
  174.2 9.4 %copy.219 = bf16[128,8,24,24]{3,2,1,0:T(8,128)(2,1)} copy(bf16[128,8,24,24]{0,3,2,1:T(8,128)(2,1)S(1)} %fusion.141) | data formatting | bytes 2359296 | tf_op jit(solution)/shard_map/convert_element_type | solution.py:49
  183.6 8.6 %convert_bitcast_fusion.1 = bf16[128,24,8,16]{1,3,2,0:T(8,128)(2,1)S(1)} fusion(bf16[128,8,24,24]{3,2,1,0:T(8,128)(2,1)} %copy.219, bf16[128,24,1,8,16]{1,0,4,3,2:T(8,128)(2,1)} %get-tuple-element.60), kind=kOutput, calls=%fused_computation.36 | convolution fusion | flops 19267584 | bytes 2752512 | tf_op jit(solution)/shard_map/phst,pthe->pshe/dot_general | solution.py:50
  192.2 4.8 copy.220
  197.0 7.5 %reshape.494 = bf16[3072,128]{0,1:T(8,128)(2,1)S(1)} reshape(bf16[128,24,8,16]{1,0,3,2:T(8,128)(2,1)} %copy.220) | data formatting | bytes 1572864 | tf_op jit(solution)/shard_map/reshape | solution.py:53
  206.3 14.4 %multiply_convert_fusion.2 = (bf16[3072,512]{1,0:T(8,128)(2,1)S(1)}, f32[3072,512]{1,0:T(8,128)S(1)}, f32[3072,512]{1,0:T(8,128)S(1)}) fusion(f32[512]{0:T(512)S(1)} %bitcast.313, bf16[2,128,512]{2,1,0:T(8,128)(2,1)S(1)} %copy-done.101, f32[3072,128]{1,0:T(8,128)S(1)} %get-tuple-element.100, f32[128]{0:T(128)S(1)} %copy-done.98, f32[128]{0:T(128)S(1)} %copy-done.87, ...), kind=kOutput, calls=%fused_computation.11 | convolution fusion | flops 508428288 | bytes 17460224 | tf_op jit(solution)/shard_map/dot_general | solution.py:28
  224.0 3.3 convert_reduce_fusion
  229.0 2.5 fusion.146
  234.8 8.0 %reshape.497 = bf16[128,24,8,16]{1,0,3,2:T(8,128)(2,1)} reshape(bf16[3072,128]{0,1:T(8,128)(2,1)S(1)} %copy.222) | data formatting | bytes 1572864 | tf_op jit(solution)/shard_map/reshape | solution.py:109
  242.8 11.8 %convert_bitcast_fusion = bf16[128,24,1,8,16]{1,4,3,0,2:T(8,128)(2,1)} fusion(bf16[128,8,24,24]{3,2,1,0:T(8,128)(2,1)} %copy.219, bf16[128,24,8,16]{1,0,3,2:T(8,128)(2,1)} %reshape.497), kind=kOutput, calls=%fused_computation.35 | convolution fusion | flops 19267584 | bytes 2752512 | tf_op jit(solution)/shard_map/phst,pshe->pthe/dot_general | solution.py:114
  254.6 20.1 %fusion.12 = f32[128,8,24,24]{2,3,1,0:T(8,128)} fusion(bf16[128,24,1,8,16]{1,0,4,3,2:T(8,128)(2,1)S(1)} %copy-done.10, bf16[128,24,8,16]{1,0,3,2:T(8,128)(2,1)S(1)} %copy-done.7), kind=kOutput, calls=%fused_computation.42 | convolution fusion | flops 18874368 | bytes 3932160 | tf_op jit(solution)/shard_map/pshe,pthe->phst/dot_general | solution.py:111
  274.7 11.0 %copy.225 = f32[128,8,24,24]{0,3,2,1:T(8,128)} copy(f32[128,8,24,24]{2,3,1,0:T(8,128)} %fusion.12) | data formatting | bytes 4718592 | tf_op jit(solution)/shard_map/pshe,pthe->phst/dot_general | solution.py:111
  285.7 4.1 multiply_convert_fusion.6
  289.8 10.4 %copy.226 = bf16[128,8,24,24]{3,2,1,0:T(8,128)(2,1)} copy(bf16[128,8,24,24]{0,3,2,1:T(8,128)(2,1)} %multiply_convert_fusion.6) | data formatting | bytes 2359296 | tf_op jit(solution)/shard_map/convert_element_type | solution.py:118
  300.2 11.9 %fusion.10 = bf16[128,24,1,8,16]{1,4,3,0,2:T(8,128)(2,1)} fusion(bf16[128,8,24,24]{3,2,1,0:T(8,128)(2,1)} %copy.226, bf16[128,24,1,8,16]{1,0,4,3,2:T(8,128)(2,1)} %copy-done.9), kind=kOutput, calls=%fused_computation.27 | convolution fusion | flops 19660800 | bytes 2752512 | tf_op jit(solution)/shard_map/phst,pshe->pthe/dot_general | solution.py:125
  312.1 9.0 %fusion.9 = bf16[128,24,1,8,16]{1,4,3,0,2:T(8,128)(2,1)} fusion(bf16[128,8,24,24]{3,2,1,0:T(8,128)(2,1)S(1)} %copy-done.2, bf16[128,24,1,8,16]{1,0,4,3,2:T(8,128)(2,1)} %copy-done.8), kind=kOutput, calls=%fused_computation.26 | convolution fusion | flops 19660800 | bytes 2752512 | tf_op jit(solution)/shard_map/phst,pthe->pshe/dot_general | solution.py:121
  321.2 7.2 %pad_maximum_fusion = bf16[128,24,3,8,16]{1,4,3,0,2:T(8,128)(2,1)S(1)} fusion(bf16[128,24,1,8,16]{1,4,3,0,2:T(8,128)(2,1)} %convert_bitcast_fusion, bf16[128,24,1,8,16]{1,4,3,0,2:T(8,128)(2,1)} %fusion.10, bf16[128,24,1,8,16]{1,4,3,0,2:T(8,128)(2,1)} %fusion.9), kind=kLoop, calls=%fused_computation.3 | loop fusion | flops 2359296 | bytes 4718592 | tf_op jit(solution)/shard_map/stack | solution.py:128
  328.4 9.4 %copy.230 = bf16[128,24,3,8,16]{1,0,4,3,2:T(8,128)(2,1)} copy(bf16[128,24,3,8,16]{1,4,3,0,2:T(8,128)(2,1)S(1)} %pad_maximum_fusion) | data formatting | bytes 4718592 | tf_op jit(solution)/shard_map/stack | solution.py:128
  337.9 20.1 %convert_element_type.231 = bf16[3072,384]{0,1:T(8,128)(2,1)} reshape(bf16[128,24,3,8,16]{1,0,4,3,2:T(8,128)(2,1)} %copy.230) | data formatting | bytes 4718592 | tf_op jit(solution)/shard_map/convert_element_type | solution.py:131
  358.0 3.7 multiply_reduce_fusion.4
  361.8 2.5 fusion.145
  369.2 4.1 all-to-all-start.2
  377.0 3.0 convolution_bitcast_fusion.2
  380.0 4.9 convolution_bitcast_fusion.3
  384.9 2.3 all-to-all-done.2
  388.7 3.4 convert_reduce_fusion.1
  398.9 3.7 convert_bitcast_fusion.2
  403.2 2.1 multiply_reduce_fusion
  412.1 4.6 copy.234
  416.8 7.4 %convert_element_type.240 = bf16[1024,384]{1,0:T(8,128)(2,1)S(1)} reshape(bf16[128,8,3,8,16]{4,3,2,1,0:T(8,128)(2,1)} %copy.234) | data formatting | bytes 1572864 | tf_op jit(solution)/shard_map/convert_element_type | solution.py:131
  426.3 39.0 %all-reduce = (f32[1,2,128]{2,1,0:T(2,128)S(1)}, f32[1,2,128]{2,1,0:T(2,128)S(1)}, f32[1,2,128]{2,1,0:T(2,128)S(1)}, f32[1,2,128]{2,1,0:T(2,128)S(1)}, f32[1,512...) all-reduce(f32[1,2,128]{2,1,0:T(2,128)S(1)} %maximum_bitcast_fusion, ...), channel_id=1, replica_groups=mesh['pix'=8,'rep'=4] {'pix','rep'}, use_global_device_ids=true, to_apply=%region_33.34 | all-reduce | flops 5504 | bytes 44032 | tf_op jit(solution)/shard_map/psum | solution.py:292
  468.3 2.9 fusion.50
  471.2 130.8 %all-reduce.4.cloned.1.call-done = (f32[1,128,384]{2,1,0:T(8,128)}, f32[1,128,384]{2,1,0:T(8,128)}, f32[1,128,128]{2,1,0:T(8,128)}, f32[1,128,128]{2,1,0:T(8,128...) async-done(((f32[1,128,384]{2,1,0:T(8,128)}, f32[1,128,384]{2,1,0:T(8,128)}, f32[1,128,128]{2,1,0:T(8,128)}, ...) | async-done | bytes 1572880 | tf_op jit(solution)/shard_map/psum | solution.py:292
  (332 shorter events, 78.0 us)
Async XLA Ops:
  7.2 17.9 %copy-start = (bf16[128,24,128]{2,1,0:T(8,128)(2,1)S(1)}, bf16[128,24,128]{2,1,0:T(8,128)(2,1)}, u32[]{:S(2)}) copy-start(bf16[128,24,128]{2,1,0:T(8,128)(2,1)} %param.16) | copy-start | bytes 2359300
  7.2 19.3 %copy-start.91 = (f32[2,2,128]{2,1,0:T(2,128)S(1)}, f32[2,2,128]{2,1,0:T(2,128)}, u32[]{:S(2)}) copy-start(f32[2,2,128]{2,1,0:T(2,128)} %param.22) | copy-start | bytes 6148
  7.2 19.3 %copy-start.92 = (f32[2,2,128]{2,1,0:T(2,128)S(1)}, f32[2,2,128]{2,1,0:T(2,128)}, u32[]{:S(2)}) copy-start(f32[2,2,128]{2,1,0:T(2,128)} %param.21) | copy-start | bytes 6148
  7.2 19.9 %copy-start.47 = (bf16[2,128,384]{2,1,0:T(8,128)(2,1)S(1)}, bf16[2,128,384]{2,1,0:T(8,128)(2,1)}, u32[]{:S(2)}) copy-start(bf16[2,128,384]{2,1,0:T(8,128)(2,1)} %param.23) | copy-start | bytes 589828
  8.2 19.5 %copy-start.55 = (pred[128,24]{1,0:T(8,128)(4,1)}, pred[128,24]{1,0:T(8,128)(4,1)S(1)}, u32[]{:S(2)}) copy-start(pred[128,24]{1,0:T(8,128)(4,1)S(1)} %copy.203) | copy-start | bytes 9220
  9.0 18.6 %copy-start.38 = (s32[128,24]{1,0:T(8,128)}, s32[128,24]{1,0:T(8,128)S(1)}, u32[]{:S(2)}) copy-start(s32[128,24]{1,0:T(8,128)S(1)} %copy.204) | copy-start | bytes 36868
  15.1 56.2 %all-to-all-start = ((bf16[8,2,160]{2,1,0:T(2,128)(2,1)}), bf16[8,2,160]{2,1,0:T(2,128)(2,1)S(1)}, u32[]{:S(2)}, u32[]{:S(2)}) async-start(bf16[8,2,160]{2,1,0:T(2,128)(2,1)} %reshape.512), calls=%async_computation | async-start | bytes 16384 | tf_op jit(solution)/shard_map/all_to_all | solution.py:213
  25.5 32.9 %copy-start.23 = (f32[128,8,128]{2,1,0:T(8,128)}, f32[128,8,128]{2,1,0:T(8,128)S(1)}, u32[]{:S(2)}) copy-start(f32[128,8,128]{2,1,0:T(8,128)S(1)} %get-tuple-element.89) | copy-start | bytes 1572868
  25.5 44.4 %copy-start.41 = (f32[128,8]{1,0:T(8,128)}, f32[128,8]{1,0:T(8,128)S(1)}, u32[]{:S(2)}) copy-start(f32[128,8]{1,0:T(8,128)S(1)} %broadcast_multiply_fusion.2) | copy-start | bytes 12292
  27.1 32.7 %copy-start.82 = (f32[128]{0:T(128)}, f32[128]{0:T(128)S(1)}, u32[]{:S(2)}) copy-start(f32[128]{0:T(128)S(1)} %get-tuple-element.118) | copy-start | bytes 1540
  27.1 69.1 %copy-start.80 = (f32[128]{0:T(128)}, f32[128]{0:T(128)S(1)}, u32[]{:S(2)}) copy-start(f32[128]{0:T(128)S(1)} %get-tuple-element.116) | copy-start | bytes 1540
  38.1 16.1 %copy-start.36 = (bf16[128,8,1,8,16]{4,3,2,1,0:T(8,128)(2,1)}, bf16[128,8,1,8,16]{4,3,2,1,0:T(8,128)(2,1)S(1)}, u32[]{:S(2)}) copy-start(bf16[128,8,1,8,16]{4,3,2,1,0:T(8,128)(2,1)S(1)} %get-tuple-element.65) | copy-start | bytes 786436
  58.4 8.8 %copy-start.34 = (bf16[1024,128]{1,0:T(8,128)(2,1)}, bf16[1024,128]{1,0:T(8,128)(2,1)S(1)}, u32[]{:S(2)}) copy-start(bf16[1024,128]{1,0:T(8,128)(2,1)S(1)} %reshape.488) | copy-start | bytes 786436
  58.8 8.5 %copy-start.21 = (f32[1024,128]{1,0:T(8,128)}, f32[1024,128]{1,0:T(8,128)S(1)}, u32[]{:S(2)}) copy-start(f32[1024,128]{1,0:T(8,128)S(1)} %get-tuple-element.93) | copy-start | bytes 1572868
  58.8 8.4 %copy-start.65 = (f32[1024]{0:T(1024)}, f32[1024]{0:T(1024)S(1)}, u32[]{:S(2)}) copy-start(f32[1024]{0:T(1024)S(1)} %broadcast_multiply_fusion.4) | copy-start | bytes 12292
  59.2 8.0 %copy-start.72 = (f32[1024]{0:T(1024)}, f32[1024]{0:T(1024)S(1)}, u32[]{:S(2)}) copy-start(f32[1024]{0:T(1024)S(1)} %fusion.128) | copy-start | bytes 12292
  59.8 8.4 %copy-start.53 = (bf16[2,512,128]{2,1,0:T(8,128)(2,1)S(1)}, bf16[2,512,128]{2,1,0:T(8,128)(2,1)}, u32[]{:S(2)}) copy-start(bf16[2,512,128]{2,1,0:T(8,128)(2,1)} %param.27) | copy-start | bytes 786436
  59.8 8.4 %copy-start.90 = (f32[128]{0:T(128)S(1)}, f32[128]{0:T(128)}, u32[]{:S(2)}) copy-start(f32[128]{0:T(128)} %get-tuple-element.85) | copy-start | bytes 1540
  68.6 23.1 %copy-start.103 = (f32[24,128]{1,0:T(8,128)S(1)}, f32[24,128]{1,0:T(8,128)}, u32[]{:S(2)}) copy-start(f32[24,128]{1,0:T(8,128)} %param.30) | copy-start | bytes 36868
  68.6 23.1 %copy-start.104 = (f32[128]{0:T(128)S(1)}, f32[128]{0:T(128)}, u32[]{:S(2)}) copy-start(f32[128]{0:T(128)} %param.29) | copy-start | bytes 1540
  71.3 20.2 %all-to-all-start.1 = ((bf16[8,32,1024]{2,1,0:T(8,128)(2,1)}), bf16[8,32,1024]{2,1,0:T(8,128)(2,1)S(1)}, u32[]{:S(2)}, u32[]{:S(2)}) async-start(bf16[8,32,1024]{2,1,0:T(8,128)(2,1)} %bitcast.19), calls=%async_computation.1 | async-start | bytes 1048576 | tf_op jit(solution)/shard_map/all_to_all | solution.py:212
  77.7 14.0 %copy-start.78 = (s32[256,1]{0,1:T(1,128)}, s32[256,1]{0,1:T(1,128)S(1)}, u32[]{:S(2)}) copy-start(s32[256,1]{0,1:T(1,128)S(1)} %fusion.130) | copy-start | bytes 3076
  78.8 15.1 %copy-start.43 = (s32[128,8]{1,0:T(8,128)}, s32[128,8]{1,0:T(8,128)S(1)}, u32[]{:S(2)}) copy-start(s32[128,8]{1,0:T(8,128)S(1)} %copy.208) | copy-start | bytes 12292
  93.9 110.6 %copy-start.5 = (f32[128,24,128]{2,1,0:T(8,128)}, f32[128,24,128]{2,1,0:T(8,128)S(1)}, u32[]{:S(2)}) copy-start(f32[128,24,128]{2,1,0:T(8,128)S(1)} %get-tuple-element.96) | copy-start | bytes 4718596
  172.4 11.1 %copy-start.51 = (f32[128,8,24]{0,2,1:T(8,128)}, f32[128,8,24]{0,2,1:T(8,128)S(1)}, u32[]{:S(2)}) copy-start(f32[128,8,24]{0,2,1:T(8,128)S(1)} %get-tuple-element.97) | copy-start | bytes 294916
  197.0 7.5 %copy-start.59 = (bf16[2,128,128]{2,1,0:T(8,128)(2,1)S(1)}, bf16[2,128,128]{2,1,0:T(8,128)(2,1)}, u32[]{:S(2)}) copy-start(bf16[2,128,128]{2,1,0:T(8,128)(2,1)} %param.24) | copy-start | bytes 196612
  205.3 23.7 %copy-start.3 = (f32[3072,128]{1,0:T(8,128)}, f32[3072,128]{1,0:T(8,128)S(1)}, u32[]{:S(2)}) copy-start(f32[3072,128]{1,0:T(8,128)S(1)} %get-tuple-element.100) | copy-start | bytes 4718596
  206.2 14.4 %copy-start.54 = (bf16[2,512,128]{2,1,0:T(8,128)(2,1)S(1)}, bf16[2,512,128]{2,1,0:T(8,128)(2,1)}, u32[]{:S(2)}) copy-start(bf16[2,512,128]{2,1,0:T(8,128)(2,1)} %param.27) | copy-start | bytes 786436
  206.2 14.4 %copy-start.84 = (f32[128]{0:T(128)S(1)}, f32[128]{0:T(128)}, u32[]{:S(2)}) copy-start(f32[128]{0:T(128)} %get-tuple-element.84) | copy-start | bytes 1540
  242.8 11.8 %copy-start.7 = (bf16[128,24,8,16]{1,0,3,2:T(8,128)(2,1)S(1)}, bf16[128,24,8,16]{1,0,3,2:T(8,128)(2,1)}, u32[]{:S(2)}) copy-start(bf16[128,24,8,16]{1,0,3,2:T(8,128)(2,1)} %reshape.497) | copy-start | bytes 2359300
  242.8 11.8 %copy-start.10 = (bf16[128,24,1,8,16]{1,0,4,3,2:T(8,128)(2,1)S(1)}, bf16[128,24,1,8,16]{1,0,4,3,2:T(8,128)(2,1)}, u32[]{:S(2)}) copy-start(bf16[128,24,1,8,16]{1,0,4,3,2:T(8,128)(2,1)} %get-tuple-element.60) | copy-start | bytes 2359300
  274.7 11.0 %copy-start.26 = (f32[128,8,24,24]{0,3,2,1:T(8,128)S(1)}, f32[128,8,24,24]{0,3,2,1:T(8,128)}, u32[]{:S(2)}) copy-start(f32[128,8,24,24]{0,3,2,1:T(8,128)} %copy-done.25) | copy-start | bytes 7077892
  274.7 11.0 %copy-start.52 = (f32[128,8,24]{0,2,1:T(8,128)S(1)}, f32[128,8,24]{0,2,1:T(8,128)}, u32[]{:S(2)}) copy-start(f32[128,8,24]{0,2,1:T(8,128)} %copy-done.51) | copy-start | bytes 294916
  300.2 11.9 %copy-start.2 = (bf16[128,8,24,24]{3,2,1,0:T(8,128)(2,1)S(1)}, bf16[128,8,24,24]{3,2,1,0:T(8,128)(2,1)}, u32[]{:S(2)}) copy-start(bf16[128,8,24,24]{3,2,1,0:T(8,128)(2,1)} %copy.226) | copy-start | bytes 3538948
  312.1 9.0 %copy-start.60 = (f32[128,24]{1,0:T(8,128)S(1)}, f32[128,24]{1,0:T(8,128)}, u32[]{:S(2)}) copy-start(f32[128,24]{1,0:T(8,128)} %get-tuple-element.71) | copy-start | bytes 36868
  337.9 20.1 %copy-start.6 = (f32[128,24,128]{2,1,0:T(8,128)S(1)}, f32[128,24,128]{2,1,0:T(8,128)}, u32[]{:S(2)}) copy-start(f32[128,24,128]{2,1,0:T(8,128)} %copy-done.5) | copy-start | bytes 4718596
  337.9 20.1 %copy-start.49 = (bf16[2,128,384]{2,1,0:T(8,128)(2,1)S(1)}, bf16[2,128,384]{2,1,0:T(8,128)(2,1)}, u32[]{:S(2)}) copy-start(bf16[2,128,384]{2,1,0:T(8,128)(2,1)} %param.23) | copy-start | bytes 589828
  337.9 20.1 %copy-start.64 = (f32[3072]{0:T(1024)S(1)}, f32[3072]{0:T(1024)}, u32[]{:S(2)}) copy-start(f32[3072]{0:T(1024)} %div.107) | copy-start | bytes 36868
  337.9 20.1 %copy-start.81 = (f32[128]{0:T(128)S(1)}, f32[128]{0:T(128)}, u32[]{:S(2)}) copy-start(f32[128]{0:T(128)} %copy-done.80) | copy-start | bytes 1540
  369.2 18.0 %all-to-all-start.2 = ((bf16[8,32,1024]{2,1,0:T(8,128)(2,1)}), bf16[8,32,1024]{2,1,0:T(8,128)(2,1)}, u32[]{:S(2)}, u32[]{:S(2)}) async-start(bf16[8,32,1024]{2,1,0:T(8,128)(2,1)} %bitcast.298), calls=%async_computation.2 | async-start | bytes 1048576 | tf_op jit(solution)/shard_map/all_to_all | solution.py:267
  373.4 228.6 %all-reduce.4.cloned.1.call-start = ((), (), s32[]{:S(2)}) async-start(), calls=%async_computation.3 | async-start | bytes 3145728 | tf_op jit(solution)/shard_map/psum | solution.py:292
  380.0 8.7 %copy-start.93 = (f32[1,512]{1,0:T(1,128)S(1)}, f32[1,512]{1,0:T(1,128)}, u32[]{:S(2)}) copy-start(f32[1,512]{1,0:T(1,128)} %get-tuple-element.75) | copy-start | bytes 6148
  416.8 8.9 %copy-start.50 = (bf16[2,128,384]{2,1,0:T(8,128)(2,1)S(1)}, bf16[2,128,384]{2,1,0:T(8,128)(2,1)}, u32[]{:S(2)}) copy-start(bf16[2,128,384]{2,1,0:T(8,128)(2,1)} %param.23) | copy-start | bytes 589828
  416.8 8.9 %copy-start.70 = (f32[1024]{0:T(1024)S(1)}, f32[1024]{0:T(1024)}, u32[]{:S(2)}) copy-start(f32[1024]{0:T(1024)} %div.114) | copy-start | bytes 12292
  416.8 8.9 %copy-start.71 = (f32[1024]{0:T(1024)S(1)}, f32[1024]{0:T(1024)}, u32[]{:S(2)}) copy-start(f32[1024]{0:T(1024)} %rsqrt.51) | copy-start | bytes 12292
  426.2 42.1 %copy-start.39 = (s32[128,24]{1,0:T(8,128)S(1)}, s32[128,24]{1,0:T(8,128)}, u32[]{:S(2)}) copy-start(s32[128,24]{1,0:T(8,128)} %copy-done.38) | copy-start | bytes 36868
  426.2 42.1 %copy-start.56 = (pred[128,24]{1,0:T(8,128)(4,1)S(1)}, pred[128,24]{1,0:T(8,128)(4,1)}, u32[]{:S(2)}) copy-start(pred[128,24]{1,0:T(8,128)(4,1)} %copy-done.55) | copy-start | bytes 9220
  468.3 139.8 %copy-start.1 = (bf16[128,24,128]{2,1,0:T(8,128)(2,1)S(1)}, bf16[128,24,128]{2,1,0:T(8,128)(2,1)}, u32[]{:S(2)}) copy-start(bf16[128,24,128]{2,1,0:T(8,128)(2,1)} %param.16) | copy-start | bytes 2359300
  (61 other events, 203.1 us)
Sparse Core Ops, SparseCore 0:
  467.2 134.7 all-reduce.3
where the time goes:
time: 626 us; the launch traced here: 615 us
  local copies, waits for them, and re-layouts  174 us (28%)
  matrix products  160 us (26%)
  waiting for transfers between devices  145 us (23%)
  other arithmetic  64.3 us (10%)
  blocking collectives  39 us (6%)
  starting transfers between devices  17.7 us (3%)
  between operations  16.1 us (3%)
    psum x1, waiting for transfers between devices, shards(): lax.psum((enc_gain, enc_shift, enc_qkv, enc_outw, enc_upw, enc_upb, enc_d...  131 us
    dot_general x30, matrix products, matmul(): return jnp.dot(left, right, preferred_element_type=jnp.float32)  60.1 us
    psum x1, blocking collectives, shards(): lax.psum((enc_gain, enc_shift, enc_qkv, enc_outw, enc_upw, enc_upb, enc_d...  39 us
    reshape x2, local copies, waits for them, and re-layouts, forward_layer(): matmul(first_low, wqkv).astype(jnp.bfloat16)  28.3 us
    convert_element_type x2, local copies, waits for them, and re-layouts, backward_layer(): d_mixed = d_mixed.astype(jnp.bfloat16)  27.5 us
    dot_general x2, matrix products, backward_layer(): jnp.einsum('pshe,pthe->phst', d_attended, value_rows, preferred_element_t...  22.3 us
    dot_general x2, matrix products, forward_layer(): jnp.einsum('pshe,pthe->phst', queries, key_rows, preferred_element_type=j...  21.7 us
    sub x2, other arithmetic, forward_layer(): attn_probs = jax.nn.softmax(scores, axis=-1)  16.6 us
  transfers between devices with their start and end apart: 4, of which 3 were waited for; matrix products, arithmetic and copies ran while one was open for 10% of the time, Pallas kernels for 0%

commit v1 on v0

v1 whole, which is shorter than its diff:
```python
import functools

import jax
import jax.numpy as jnp
from jax import lax
from jax.experimental import pallas as pl
from jax.experimental.pallas import tpu as pltpu
from jax.sharding import PartitionSpec as P

HEADS = 8
HEAD_DIM = 16
VIS = 8
GROUP = 16
PAD = 32
CHUNK = 48
EPS = 1e-05
NEG = -1e30
BF = jnp.bfloat16
F32 = jnp.float32
VMEM_LIMIT = 56 * 1024 * 1024


def nn(left, right):
    return jnp.dot(left, right, preferred_element_type=F32)


def nt(left, right):
    return lax.dot_general(left, right, (((1,), (1,)), ((), ())), preferred_element_type=F32)


def tn(left, right):
    return lax.dot_general(left, right, (((0,), (0,)), ((), ())), preferred_element_type=F32)


def iota(shape, dim):
    return lax.broadcasted_iota(jnp.int32, shape, dim)


def fold_rows(values):
    rows = values.shape[0]
    return jnp.sum(values.reshape(rows // 8, 8, values.shape[1]), axis=0)


def erf_parts(hidden):
    size = jnp.abs(hidden)
    base = 1.0 + size * (0.3275911 * 0.7071067811865476)
    t = 1.0 / base
    bell = jnp.exp(hidden * hidden * -0.5)
    poly = t * (
        0.5 * 0.254829592
        + t * (0.5 * -0.284496736 + t * (0.5 * 1.421413741 + t * (0.5 * -1.453152027 + t * (0.5 * 1.061405429))))
    )
    tail = poly * bell
    return jnp.where(hidden >= 0, 1.0 - tail, tail), bell


def expand(rows, masks):
    count = rows.shape[0]
    return jnp.concatenate([rows * masks[h, :count, :] for h in range(HEADS)], axis=0)


def fold_heads(rows, step, count):
    lane = iota((count, 128), 1)
    picked = rows[0:count]
    for head in range(1, HEADS):
        picked = jnp.where(lane >= head * HEAD_DIM, rows[head * step : head * step + count], picked)
    return picked


def ln_fwd(values, gain, bias, hat, inv, low, where):
    centred = values - jnp.mean(values, axis=-1, keepdims=True)
    scale = lax.rsqrt(jnp.mean(centred * centred, axis=-1, keepdims=True) + EPS)
    unit = centred * scale
    hat[where] = unit
    inv[where] = jnp.broadcast_to(scale, unit.shape)
    low[where] = (unit * gain + bias).astype(BF)


def ln_bwd(grad, gain, hat, inv, where):
    unit = hat[where]
    inner = grad * gain
    lean = jnp.mean(inner, axis=-1, keepdims=True)
    tilt = jnp.mean(inner * unit, axis=-1, keepdims=True)
    return inv[where] * (inner - lean - unit * tilt), fold_rows(grad * unit), fold_rows(grad)


def prep_kernel(
    cap, extra, count, me_ref, dest_ref, tokens_ref, len_ref, masked_ref, dest_row_ref,
    payload_ref, pos_ref, place_ref, take_ref, back_ref, tally,
):
    pixels, slots = masked_ref.shape
    groups = pixels // GROUP
    block = cap + extra
    wide = GROUP * slots
    len_col = jnp.broadcast_to(len_ref[...].astype(F32), (pixels, pixels)).T
    dest_col = jnp.broadcast_to(dest_row_ref[...].astype(F32), (pixels, pixels)).T
    seen = (masked_ref[...] == 0) & (iota((pixels, slots), 1).astype(F32) < len_col[:, :slots])
    seen_low = jnp.where(seen, 1.0, 0.0).astype(BF)
    earlier = jnp.where(iota((slots, slots), 0) < iota((slots, slots), 1), 1.0, 0.0).astype(BF)
    member = iota((pixels, slots), 0) % GROUP
    code = jnp.where(seen, nn(seen_low, earlier) + (member * VIS).astype(F32), -1.0)
    spread = jnp.where(iota((slots, wide), 0) == iota((slots, wide), 1) % slots, 1.0, 0.0).astype(BF)
    code_wide = nn(code.astype(BF), spread)
    own = iota((pixels, wide), 0) % GROUP == iota((pixels, wide), 1) // slots
    code_row = jnp.sum(jnp.where(own, code_wide, 0.0).reshape(groups, GROUP, wide), axis=1)
    lanes = GROUP * VIS
    own_low = iota((pixels, lanes), 0) % GROUP == iota((pixels, lanes), 1) // VIS
    len_rows = jnp.sum(jnp.where(own_low, len_col, 0.0).reshape(groups, GROUP, lanes), axis=1)
    dest_rows = jnp.sum(jnp.where(own_low, dest_col, 0.0).reshape(groups, GROUP, lanes), axis=1)
    me = me_ref[0]
    for dev in range(count):
        tally[dev] = 0
    order = iota((lanes, wide), 0).astype(F32)
    steps = (iota((GROUP, wide), 1) % slots + 1).astype(F32).astype(BF)
    found = []
    for group in range(groups):
        select = jnp.where(order == code_row[group : group + 1, :], 1.0, 0.0).astype(BF)
        rows = nn(select, tokens_ref[group * wide : (group + 1) * wide, :]).reshape(GROUP, VIS, 128)
        found.append(nt(steps, select)[0:1, :])
        for member_id in range(GROUP):
            series = group * GROUP + member_id
            dest = dest_ref[series]
            rank = tally[dest]
            tally[dest] = rank + 1
            sender = lax.rem(2 * me - dest + 2 * count, count)
            place_ref[series] = dest * cap + rank
            take_ref[series] = sender * block + rank
            back_ref[series] = sender * cap + rank
            payload_ref[dest * block + rank] = rows[member_id].astype(BF)
    pos_rows = jnp.concatenate(found, axis=0)
    pos_ref[...] = pos_rows

    def label(dev, carry):
        mine = dest_rows == dev.astype(F32)
        payload_ref[dev * block + cap] = jnp.where(mine, pos_rows, 0.0).astype(BF)
        payload_ref[dev * block + cap + 1] = jnp.where(mine, len_rows, 0.0).astype(BF)
        return carry

    lax.fori_loop(0, count, label, 0)


def prep(tokens, lengths, masked, route_dev, count, cap, extra, me):
    pixels, slots, width = tokens.shape
    smem = pl.BlockSpec(memory_space=pltpu.SMEM)
    vmem = pl.BlockSpec(memory_space=pltpu.VMEM)
    index = jax.ShapeDtypeStruct((pixels,), jnp.int32)
    return pl.pallas_call(
        functools.partial(prep_kernel, cap, extra, count),
        out_shape=(
            jax.ShapeDtypeStruct((count * (cap + extra), VIS, width), BF),
            jax.ShapeDtypeStruct((pixels // GROUP, GROUP * VIS), F32),
            index,
            index,
            index,
        ),
        in_specs=[smem, smem, vmem, vmem, vmem, vmem],
        out_specs=(vmem, vmem, smem, smem, smem),
        scratch_shapes=[pltpu.SMEM((count,), jnp.int32)],
        compiler_params=pltpu.CompilerParams(vmem_limit_bytes=VMEM_LIMIT),
        name="prep",
    )(
        me, route_dev, tokens.reshape(pixels * slots, width), lengths.reshape(1, pixels), masked,
        route_dev.reshape(1, pixels),
    )


class Box:
    pass


def gelu_stage(hidden, b_up, act, slope, base, rows):
    for start in range(0, rows, 16):
        value = hidden[start : start + 16] + b_up
        cdf, bell = erf_parts(value)
        where = pl.ds(base + start, 16)
        act[where] = (value * cdf).astype(BF)
        slope[where] = cdf + value * bell * 0.3989422804014327


def slope_stage(grad_act, slope, out, base, rows):
    total = None
    for start in range(0, rows, 16):
        part = (grad_act[start : start + 16] * slope[pl.ds(base + start, 16)]).astype(BF)
        out[pl.ds(start, 16)] = part
        summed = fold_rows(part.astype(F32))
        total = summed if total is None else total + summed
    return total


def softmax_rows(scores, keep):
    scores = jnp.where(keep, scores, NEG)
    powers = jnp.exp(scores - jnp.max(scores, axis=0, keepdims=True))
    return powers / jnp.sum(powers, axis=0, keepdims=True)


def soft_bwd(probs, grad):
    return (probs * (grad - jnp.sum(grad * probs, axis=0, keepdims=True))).astype(BF)


def encoder_fwd(b, base, rows):
    w = b.w
    for start in range(0, rows, 32):
        where = pl.ds(base + start, 32)
        ln_fwd(b.e_x[where], w.gain[0:1], w.bias[0:1], b.e_hat1, b.e_inv1, b.e_n1, where)
    whole = pl.ds(base, rows)
    qkv = nn(b.e_n1[whole], w.qkv[0])
    for start in range(0, rows, 32):
        where = pl.ds(base + start, 32)
        part = qkv[start : start + 32]
        b.e_qkv[where, 0:128] = (part[:, 0:128] * 0.25).astype(BF)
        b.e_qkv[where, 128:384] = part[:, 128:384].astype(BF)
    same = iota((16, 128), 0) // VIS == (iota((16, 128), 1) % 16) // VIS
    for start in range(0, rows, 16):
        where = pl.ds(base + start, 16)
        query = expand(b.e_qkv[where, 0:128], b.masks)
        keep = same & (b.pos_col[where] > 0)
        probs = softmax_rows(nt(b.e_qkv[where, 128:256], query), keep)
        b.e_probs[where] = probs
        mixed = tn(probs.astype(BF), b.e_qkv[where, 256:384])
        b.e_att[where] = fold_heads(mixed, 16, 16).astype(BF)
    proj = nn(b.e_att[whole], w.out[0])
    for start in range(0, rows, 32):
        where = pl.ds(base + start, 32)
        middle = b.e_x[where] + proj[start : start + 32]
        b.e_x[where] = middle
        ln_fwd(middle, w.gain[1:2], w.bias[1:2], b.e_hat2, b.e_inv2, b.e_n2, where)
    hidden = nn(b.e_n2[whole], w.up[0])
    gelu_stage(hidden, w.b_up[0:1], b.e_act, b.e_slope, base, rows)
    down = nn(b.e_act[whole], w.down[0])
    for start in range(0, rows, 32):
        where = pl.ds(base + start, 32)
        b.sent[where] = (b.e_x[where] + down[start : start + 32] + w.b_down[0:1]).astype(BF)


def encoder_bwd(b, base, rows):
    w = b.w
    whole = pl.ds(base, rows)
    grad_low = b.g_sent[whole]
    b.d_down[0] += tn(grad_low, b.e_act[whole])
    b.d_b_down[0] += fold_rows(grad_low.astype(F32))
    grad_act = nn(grad_low, b.down_t[0])
    b.d_b_up[0] += slope_stage(grad_act, b.e_slope, b.e_gh, base, rows)
    b.d_up[0] += tn(b.e_n2[whole], b.e_gh[...])
    grad_n2 = nn(b.e_gh[...], b.up_t[0])
    for start in range(0, rows, 32):
        where = pl.ds(base + start, 32)
        grad, gain_part, bias_part = ln_bwd(
            grad_n2[start : start + 32], w.gain[1:2], b.e_hat2, b.e_inv2, where
        )
        b.d_gain[1] += gain_part
        b.d_bias[1] += bias_part
        grad = grad + b.g_sent[where].astype(F32)
        b.e_gm[pl.ds(start, 32)] = grad
        b.e_gml[pl.ds(start, 32)] = grad.astype(BF)
    b.d_out[0] += tn(b.e_att[whole], b.e_gml[...])
    b.e_ga[...] = nn(b.e_gml[...], b.out_t[0]).astype(BF)
    for start in range(0, rows, 16):
        where = pl.ds(base + start, 16)
        query = expand(b.e_qkv[where, 0:128], b.masks)
        grad_out = expand(b.e_ga[start : start + 16], b.masks)
        probs = b.e_probs[where]
        grad_s = soft_bwd(probs, nt(b.e_qkv[where, 256:384], grad_out))
        here = pl.ds(start, 16)
        b.e_gqkv[here, 256:384] = nn(probs.astype(BF), grad_out).astype(BF)
        b.e_gqkv[here, 128:256] = nn(grad_s, query).astype(BF)
        grad_q = fold_heads(tn(grad_s, b.e_qkv[where, 128:256]), 16, 16)
        b.e_gqkv[here, 0:128] = (grad_q * 0.25).astype(BF)
    b.d_qkv[0] += tn(b.e_n1[whole], b.e_gqkv[...])
    grad_n1 = nn(b.e_gqkv[...], b.qkv_t[0])
    for start in range(0, rows, 32):
        where = pl.ds(base + start, 32)
        grad, gain_part, bias_part = ln_bwd(
            grad_n1[start : start + 32], w.gain[0:1], b.e_hat1, b.e_inv1, where
        )
        b.d_gain[0] += gain_part
        b.d_bias[0] += bias_part
        b.g_enc[where] = grad + b.e_gm[pl.ds(start, 32)]


def decoder_group(b, group):
    w = b.w
    slots = b.slots
    rows = GROUP * slots
    first = group * GROUP
    lane = iota((1, 128), 1)
    pos_row = b.pos_row[group]
    target = jnp.where(pos_row > 0, (lane // VIS * slots).astype(F32) + pos_row - 1.0, -1.0)
    for start in range(0, rows, CHUNK):
        spot = (iota((CHUNK, 128), 0) + start).astype(F32)
        b.hot[pl.ds(start, CHUNK)] = jnp.where(spot == target, 1.0, 0.0).astype(BF)
    sent_rows = pl.ds(pl.multiple_of(group * 128, 128), 128)
    placed = nn(b.hot[...], b.sent[sent_rows])
    shown = nn(b.hot[...], jnp.ones((128, 128), BF))
    step = iota((slots, 128), 0).astype(F32)

    def span(member):
        return pl.ds(member * slots, slots)

    def inside(member):
        lens = b.len_col[pl.ds(pl.multiple_of(group * 128, 128) + member * VIS, VIS)]
        return step < jnp.concatenate([lens] * (slots // VIS), axis=0)

    for member in range(GROUP):
        at = slice(member * slots, (member + 1) * slots)
        hidden_part = 1.0 - shown[at]
        b.unseen[span(member)] = hidden_part
        b.d_x[span(member)] = placed[at] + hidden_part * w.mask[...] + w.pos[...]
        cot = b.cot[b.slot[first + member]].astype(F32)
        b.d_g[span(member)] = jnp.where(inside(member), cot, 0.0)
    for start in range(0, rows, CHUNK):
        where = pl.ds(start, CHUNK)
        ln_fwd(b.d_x[where], w.gain[2:3], w.bias[2:3], b.d_hat1, b.d_inv1, b.d_n1, where)
    qkv = nn(b.d_n1[...], w.qkv[1])
    zeros = jnp.zeros((PAD - slots, 128), F32)

    def padded(values):
        return jnp.concatenate([values, zeros], axis=0).astype(BF)

    wide_zero = jnp.zeros((PAD - slots, HEADS * PAD), F32)

    def padded_wide(values):
        return jnp.concatenate([values, wide_zero], axis=0).astype(BF)

    for member in range(GROUP):
        at = slice(member * slots, (member + 1) * slots)
        query_low = padded(qkv[at, 0:128] * 0.25)
        key_low = padded(qkv[at, 128:256])
        value_low = padded(qkv[at, 256:384])
        b.d_q[member] = query_low
        b.d_k[member] = key_low
        b.d_v[member] = value_low
        scores = nt(key_low, expand(query_low, b.masks))[:slots]
        ok = inside(member)
        probs = softmax_rows(scores, jnp.concatenate([ok, ok], axis=1))
        b.d_probs[member] = probs
        mixed = tn(padded_wide(probs), value_low)
        b.d_att32[span(member)] = fold_heads(mixed, PAD, slots)
    for start in range(0, rows, CHUNK):
        where = pl.ds(start, CHUNK)
        b.d_att[where] = b.d_att32[where].astype(BF)
    proj = nn(b.d_att[...], w.out[1])
    for start in range(0, rows, CHUNK):
        where = pl.ds(start, CHUNK)
        middle = b.d_x[where] + proj[start : start + CHUNK]
        b.d_x[where] = middle
        ln_fwd(middle, w.gain[3:4], w.bias[3:4], b.d_hat2, b.d_inv2, b.d_n2, where)
    hidden = nn(b.d_n2[...], w.up[1])
    gelu_stage(hidden, w.b_up[1:2], b.d_act, b.d_slope, 0, rows)
    down = nn(b.d_act[...], w.down[1])
    for member in range(GROUP):
        at = slice(member * slots, (member + 1) * slots)
        value = b.d_x[span(member)] + down[at] + w.b_down[1:2]
        b.dec[b.slot[first + member]] = jnp.where(inside(member), value, 0.0)
    for start in range(0, rows, CHUNK):
        where = pl.ds(start, CHUNK)
        b.d_gl[where] = b.d_g[where].astype(BF)
    b.d_down[1] += tn(b.d_gl[...], b.d_act[...])
    b.d_b_down[1] += fold_rows(b.d_g[...])
    grad_act = nn(b.d_gl[...], b.down_t[1])
    b.d_b_up[1] += slope_stage(grad_act, b.d_slope, b.d_gh, 0, rows)
    b.d_up[1] += tn(b.d_n2[...], b.d_gh[...])
    grad_n2 = nn(b.d_gh[...], b.up_t[1])
    for start in range(0, rows, CHUNK):
        where = pl.ds(start, CHUNK)
        grad, gain_part, bias_part = ln_bwd(
            grad_n2[start : start + CHUNK], w.gain[3:4], b.d_hat2, b.d_inv2, where
        )
        b.d_gain[3] += gain_part
        b.d_bias[3] += bias_part
        grad = grad + b.d_g[where]
        b.d_g[where] = grad
        b.d_gl[where] = grad.astype(BF)
    b.d_out[1] += tn(b.d_att[...], b.d_gl[...])
    grad_att = nn(b.d_gl[...], b.out_t[1])
    for member in range(GROUP):
        at = slice(member * slots, (member + 1) * slots)
        query = expand(b.d_q[member], b.masks)
        grad_out = expand(padded(grad_att[at]), b.masks)
        probs = b.d_probs[member]
        grad_s = soft_bwd(probs, nt(b.d_v[member], grad_out)[:slots])
        grad_s = jnp.concatenate([grad_s.astype(F32), wide_zero], axis=0).astype(BF)
        b.d_gqkv32[span(member), 256:384] = nn(padded_wide(probs), grad_out)[:slots]
        b.d_gqkv32[span(member), 128:256] = nn(grad_s, query)[:slots]
        b.d_gqkv32[span(member), 0:128] = fold_heads(tn(grad_s, b.d_k[member]), PAD, slots) * 0.25
    for start in range(0, rows, CHUNK):
        where = pl.ds(start, CHUNK)
        b.d_gqkv[where] = b.d_gqkv32[where].astype(BF)
    b.d_qkv[1] += tn(b.d_n1[...], b.d_gqkv[...])
    grad_n1 = nn(b.d_gqkv[...], b.qkv_t[1])
    pos_total = None
    for start in range(0, rows, CHUNK):
        where = pl.ds(start, CHUNK)
        grad, gain_part, bias_part = ln_bwd(
            grad_n1[start : start + CHUNK], w.gain[2:3], b.d_hat1, b.d_inv1, where
        )
        b.d_gain[2] += gain_part
        b.d_bias[2] += bias_part
        grad = grad + b.d_g[where]
        b.d_gl[where] = grad.astype(BF)
        part = jnp.sum(grad.reshape(CHUNK // slots, slots, 128), axis=0)
        pos_total = part if pos_total is None else pos_total + part
        b.d_mask[...] += fold_rows(grad * b.unseen[where])
    b.d_pos[...] += pos_total
    b.g_sent[sent_rows] = tn(b.hot[...], b.d_gl[...]).astype(BF)


IN_NAMES = (
    "take", "back_at", "slot", "recv", "cot", "w_qkv", "w_out", "w_up", "w_down", "b_up", "b_down", "gain",
    "bias", "mask", "pos",
)
OUT_NAMES = ("dec", "back", "grads")


def small_rows(slots):
    return 18 + 1 + slots


def main_kernel(names, cap, extra, count, *refs):
    b = Box()
    for name, ref in zip(names, refs, strict=True):
        setattr(b, name, ref)
    b.w = Box()
    for name in ("qkv", "out", "up", "down"):
        setattr(b.w, name, getattr(b, "w_" + name))
    for name in ("b_up", "b_down", "gain", "bias", "mask", "pos"):
        setattr(b.w, name, getattr(b, name))
    b.slots = b.cot.shape[1]
    pixels = b.cot.shape[0]
    groups = pixels // GROUP
    block = cap + extra
    for head in range(HEADS):
        lane = iota((PAD, 128), 1) // HEAD_DIM
        b.masks[head] = jnp.where(lane == head, 1.0, 0.0).astype(BF)
    for layer in range(2):
        b.qkv_t[layer] = b.w_qkv[layer].T
        b.out_t[layer] = b.w_out[layer].T
        b.up_t[layer] = b.w_up[layer].T
        b.down_t[layer] = b.w_down[layer].T
    for ref in (b.d_qkv, b.d_out, b.d_up, b.d_down, b.d_gain, b.d_bias, b.d_b_up, b.d_b_down, b.d_mask, b.d_pos):
        ref[...] = jnp.zeros(ref.shape, F32)

    def gather(dev, carry):
        pos, lens = carry
        return (
            pos + b.recv[dev * block + cap].astype(F32),
            lens + b.recv[dev * block + cap + 1].astype(F32),
        )

    empty = jnp.zeros((groups, 128), F32)
    pos, lens = lax.fori_loop(0, count, gather, (empty, empty))
    for group in range(groups):
        where = pl.ds(group * 128, 128)
        b.pos_row[group] = pos[group : group + 1]
        b.pos_col[where] = jnp.broadcast_to(pos[group : group + 1], (128, 128)).T
        b.len_col[where] = jnp.broadcast_to(lens[group : group + 1], (128, 128)).T

    enc_rows = 256
    per = enc_rows // VIS

    def enc_forward(step, carry):
        base = pl.multiple_of(step * enc_rows, enc_rows)
        for member in range(per):
            b.e_x[pl.ds(base + member * VIS, VIS)] = b.recv[b.take[step * per + member]].astype(F32)
        encoder_fwd(b, base, enc_rows)
        return carry

    lax.fori_loop(0, pixels // per, enc_forward, 0)

    def dec_both(group, carry):
        decoder_group(b, group)
        return carry

    lax.fori_loop(0, groups, dec_both, 0)

    def enc_backward(step, carry):
        base = pl.multiple_of(step * enc_rows, enc_rows)
        encoder_bwd(b, base, enc_rows)
        for member in range(per):
            rows = b.g_enc[pl.ds(base + member * VIS, VIS)]
            b.back[b.back_at[step * per + member]] = rows.astype(BF)
        return carry

    lax.fori_loop(0, pixels // per, enc_backward, 0)

    offset = 0
    for layer in range(2):
        for start in range(0, 384, 128):
            b.grads[offset : offset + 128] = b.d_qkv[layer, :, start : start + 128].astype(BF)
            offset += 128
        b.grads[offset : offset + 128] = b.d_out[layer].astype(BF)
        offset += 128
        for start in range(0, 512, 128):
            b.grads[offset : offset + 128] = b.d_up[layer, :, start : start + 128].astype(BF)
            offset += 128
        for start in range(0, 512, 128):
            b.grads[offset : offset + 128] = b.d_down[layer, :, start : start + 128].T.astype(BF)
            offset += 128

    def total(ref, index):
        return jnp.sum(ref[index], axis=0, keepdims=True)

    small = [total(b.d_gain, i) for i in range(4)] + [total(b.d_bias, i) for i in range(4)]
    for layer in range(2):
        row = total(b.d_b_up, layer)
        small += [row[:, start : start + 128] for start in range(0, 512, 128)]
    small += [total(b.d_b_down, layer) for layer in range(2)]
    small.append(jnp.sum(b.d_mask[...], axis=0, keepdims=True))
    small.append(b.d_pos[...])
    tail = jnp.concatenate(small, axis=0)
    fill = -tail.shape[0] % 16
    tail = jnp.concatenate([tail, jnp.zeros((fill, 128), F32)], axis=0)
    b.grads[offset : offset + tail.shape[0]] = tail.astype(BF)


def main_call(args, cap, extra, count, grad_rows):
    recv, cot = args[3], args[4]
    pixels, slots, width = cot.shape
    enc = pixels * VIS
    rows = GROUP * slots
    smem = pl.BlockSpec(memory_space=pltpu.SMEM)
    vmem = pl.BlockSpec(memory_space=pltpu.VMEM)
    enc_rows = 256
    scratch = {
        "masks": ((HEADS, PAD, 128), BF),
        "qkv_t": ((2, 384, 128), BF),
        "out_t": ((2, 128, 128), BF),
        "up_t": ((2, 512, 128), BF),
        "down_t": ((2, 128, 512), BF),
        "d_qkv": ((2, 128, 384), F32),
        "d_out": ((2, 128, 128), F32),
        "d_up": ((2, 128, 512), F32),
        "d_down": ((2, 128, 512), F32),
        "d_gain": ((4, 8, 128), F32),
        "d_bias": ((4, 8, 128), F32),
        "d_b_up": ((2, 8, 512), F32),
        "d_b_down": ((2, 8, 128), F32),
        "d_mask": ((8, 128), F32),
        "d_pos": ((slots, 128), F32),
        "pos_row": ((pixels // GROUP, 1, 128), F32),
        "pos_col": ((enc, 128), F32),
        "len_col": ((enc, 128), F32),
        "sent": ((enc, 128), BF),
        "g_sent": ((enc, 128), BF),
        "g_enc": ((enc, 128), F32),
        "e_x": ((enc, 128), F32),
        "e_hat1": ((enc, 128), F32),
        "e_inv1": ((enc, 128), F32),
        "e_n1": ((enc, 128), BF),
        "e_qkv": ((enc, 384), BF),
        "e_probs": ((enc, 128), F32),
        "e_att": ((enc, 128), BF),
        "e_hat2": ((enc, 128), F32),
        "e_inv2": ((enc, 128), F32),
        "e_n2": ((enc, 128), BF),
        "e_act": ((enc, 512), BF),
        "e_slope": ((enc, 512), F32),
        "e_gh": ((enc_rows, 512), BF),
        "e_gm": ((enc_rows, 128), F32),
        "e_gml": ((enc_rows, 128), BF),
        "e_ga": ((enc_rows, 128), BF),
        "e_gqkv": ((enc_rows, 384), BF),
        "hot": ((rows, 128), BF),
        "unseen": ((rows, 128), F32),
        "d_x": ((rows, 128), F32),
        "d_g": ((rows, 128), F32),
        "d_gl": ((rows, 128), BF),
        "d_hat1": ((rows, 128), F32),
        "d_inv1": ((rows, 128), F32),
        "d_n1": ((rows, 128), BF),
        "d_q": ((GROUP, PAD, 128), BF),
        "d_k": ((GROUP, PAD, 128), BF),
        "d_v": ((GROUP, PAD, 128), BF),
        "d_probs": ((GROUP, slots, HEADS * PAD), F32),
        "d_att32": ((rows, 128), F32),
        "d_att": ((rows, 128), BF),
        "d_hat2": ((rows, 128), F32),
        "d_inv2": ((rows, 128), F32),
        "d_n2": ((rows, 128), BF),
        "d_act": ((rows, 512), BF),
        "d_slope": ((rows, 512), F32),
        "d_gh": ((rows, 512), BF),
        "d_gqkv32": ((rows, 384), F32),
        "d_gqkv": ((rows, 384), BF),
    }
    names = IN_NAMES + OUT_NAMES + tuple(scratch)
    return pl.pallas_call(
        functools.partial(main_kernel, names, cap, extra, count),
        out_shape=(
            jax.ShapeDtypeStruct((pixels, slots, width), F32),
            jax.ShapeDtypeStruct((count * cap, VIS, width), BF),
            jax.ShapeDtypeStruct((grad_rows, 128), BF),
        ),
        in_specs=[smem] * 3 + [vmem] * (len(IN_NAMES) - 3),
        out_specs=(vmem, vmem, vmem),
        scratch_shapes=[pltpu.VMEM(shape, kind) for shape, kind in scratch.values()],
        compiler_params=pltpu.CompilerParams(vmem_limit_bytes=VMEM_LIMIT),
        name="layers",
    )(*args)


def pair_sum_kernel(core_ref, mine_ref, theirs_ref, out_ref):
    core = core_ref[0]
    out_ref[...] = (mine_ref[core].astype(F32) + theirs_ref[core].astype(F32)).astype(BF)


def chunk_sum_kernel(parts_ref, out_ref):
    total = parts_ref[0].astype(F32)
    for part in range(1, parts_ref.shape[0]):
        total = total + parts_ref[part].astype(F32)
    low = total.astype(BF)
    for part in range(parts_ref.shape[0]):
        out_ref[part] = low


def unpack_kernel(
    slots, core_ref, mine_ref, theirs_ref, gain_ref, bias_ref, qkv_ref, out_ref, up_ref, b_up_ref, down_ref,
    b_down_ref, mask_ref, pos_ref, full,
):
    core = core_ref[0]
    full[core] = mine_ref[...]
    full[1 - core] = theirs_ref[...]
    half = full.shape[1]

    def rows(start, size):
        side, at = start // half, start % half
        if at + size <= half:
            return full[side, at : at + size].astype(F32)
        cut = half - at
        return jnp.concatenate(
            [full[side, at:half].astype(F32), full[side + 1, 0 : size - cut].astype(F32)], axis=0
        )

    offset = 0
    for layer in range(2):
        for start in range(0, 384, 128):
            qkv_ref[layer, :, start : start + 128] = rows(offset, 128)
            offset += 128
        out_ref[layer] = rows(offset, 128)
        offset += 128
        for start in range(0, 512, 128):
            up_ref[layer, :, start : start + 128] = rows(offset, 128)
            offset += 128
        for start in range(0, 512, 128):
            down_ref[layer, start : start + 128, :] = rows(offset, 128)
            offset += 128
    count = small_rows(slots)
    small = rows(offset, count + (-count % 16))
    gain_ref[...] = small[0:4]
    bias_ref[...] = small[4:8]
    for layer in range(2):
        for part in range(4):
            at = 8 + 4 * layer + part
            b_up_ref[layer : layer + 1, part * 128 : (part + 1) * 128] = small[at : at + 1]
    b_down_ref[...] = small[16:18]
    mask_ref[...] = small[18:19]
    pos_ref[...] = small[19 : 19 + slots]


def restore_kernel(place_ref, pos_ref, rows_ref, out_ref, held):
    groups = pos_ref.shape[0]
    wide = out_ref.shape[0] // groups
    slots = wide // GROUP
    lane = iota((1, 128), 1)
    for group in range(groups):
        for member in range(GROUP):
            block = rows_ref[place_ref[group * GROUP + member]]
            held[pl.ds(member * VIS, VIS)] = block.astype(F32)
        pos_row = pos_ref[group : group + 1]
        target = jnp.where(pos_row > 0, (lane // VIS * slots).astype(F32) + pos_row - 1.0, -1.0)
        hot = jnp.where(iota((wide, 128), 0).astype(F32) == target, 1.0, 0.0).astype(BF)
        out_ref[group * wide : (group + 1) * wide, :] = nn(hot, held[...].astype(BF))


def shards(
    tokens, lengths, masked, route_dev, route_slot, norm_gain, norm_bias, w_qkv, w_out, w_up, b_up, w_down,
    b_down, mask_token, pos_table, cotangent,
):
    count = lax.axis_size("pix")
    reps = lax.axis_size("rep")
    devices = count * reps
    pixels, slots, width = tokens.shape
    cap = max(2, (2 * pixels + count - 1) // count)
    extra = 2
    smem = pl.BlockSpec(memory_space=pltpu.SMEM)
    vmem = pl.BlockSpec(memory_space=pltpu.VMEM)
    params = pltpu.CompilerParams(vmem_limit_bytes=VMEM_LIMIT)
    pix = lax.axis_index("pix")
    me = pix.reshape(1).astype(jnp.int32)
    flat = pix * reps + lax.axis_index("rep")
    core = (flat % 2).reshape(1).astype(jnp.int32)
    payload, pos_rows, place, take, back_at = prep(
        tokens, lengths, masked, route_dev, count, cap, extra, me
    )
    block = cap + extra
    recv = lax.all_to_all(
        payload.reshape(count, block, VIS, width), "pix", split_axis=0, concat_axis=0, tiled=True
    ).reshape(count * block, VIS, width)
    chunk = -(-(3072 + small_rows(slots)) // devices)
    chunk += -chunk % 8
    half = devices // 2
    dec, back, grads = main_call(
        (
            take, back_at, route_slot, recv, cotangent, w_qkv, w_out, w_up, w_down, b_up, b_down,
            norm_gain.reshape(4, width), norm_bias.reshape(4, width), mask_token.reshape(1, width), pos_table,
        ),
        cap,
        extra,
        count,
        devices * chunk,
    )
    returned = lax.all_to_all(
        back.reshape(count, cap, VIS, width), "pix", split_axis=0, concat_axis=0, tiled=True
    ).reshape(count * cap, VIS, width)
    axes = ("pix", "rep")
    swap = [(i, i ^ 1) for i in range(devices)]
    groups = [[2 * i + side for i in range(half)] for side in range(2)]

    def exchange(values):
        return lax.all_to_all(
            values, axes, split_axis=0, concat_axis=0, axis_index_groups=groups, tiled=True
        )

    grads = grads.reshape(2, half, chunk, 128)
    theirs = lax.ppermute(grads, axes, swap)
    paired = pl.pallas_call(
        pair_sum_kernel,
        out_shape=jax.ShapeDtypeStruct((half, chunk, 128), BF),
        in_specs=[smem, vmem, vmem],
        out_specs=vmem,
        compiler_params=params,
        name="pair_sum",
    )(core, grads, theirs)
    spread = pl.pallas_call(
        chunk_sum_kernel,
        out_shape=jax.ShapeDtypeStruct((half, chunk, 128), BF),
        in_specs=[vmem],
        out_specs=vmem,
        compiler_params=params,
        name="chunk_sum",
    )(exchange(paired))
    summed = exchange(spread).reshape(half * chunk, 128)
    other = lax.ppermute(summed, axes, swap)
    gain, bias, qkv, out, up, bup, down, bdown, mask, pos = pl.pallas_call(
        functools.partial(unpack_kernel, slots),
        out_shape=tuple(
            jax.ShapeDtypeStruct(shape, F32)
            for shape in (
                (4, width), (4, width), w_qkv.shape, w_out.shape, w_up.shape, b_up.shape, w_down.shape,
                b_down.shape, (1, width), pos_table.shape,
            )
        ),
        in_specs=[smem, vmem, vmem],
        out_specs=(vmem,) * 10,
        scratch_shapes=[pltpu.VMEM((2, half * chunk, 128), BF)],
        compiler_params=params,
        name="unpack",
    )(core, summed, other)
    grad_tokens = pl.pallas_call(
        restore_kernel,
        out_shape=jax.ShapeDtypeStruct((pixels * slots, width), F32),
        in_specs=[smem, vmem, vmem],
        out_specs=vmem,
        scratch_shapes=[pltpu.VMEM((GROUP * VIS, width), F32)],
        compiler_params=params,
        name="restore",
    )(place, pos_rows, returned)
    return (
        dec,
        grad_tokens.reshape(pixels, slots, width),
        gain.reshape(norm_gain.shape),
        bias.reshape(norm_bias.shape),
        qkv,
        out,
        up,
        bup,
        down,
        bdown,
        mask.reshape(width),
        pos,
    )


def solution(mesh):
    rows = P(("pix", "rep"))
    in_specs = (rows,) * 5 + (P(),) * 10 + (rows,)
    out_specs = (rows, rows) + (P(),) * 10
    return jax.shard_map(shards, mesh=mesh, in_specs=in_specs, out_specs=out_specs, check_vma=False)
```

time: 626 us -> 191 us (0.31); the launches traced: 615 us -> 190 us
  local copies, waits for them, and re-layouts: 174 us -> 3.93 us
  matrix products: 160 us -> 0 us
  waiting for transfers between devices: 145 us -> 16 us
  Pallas kernels: 0 us -> 108 us
  other arithmetic: 64.3 us -> 0 us
  blocking collectives: 39 us -> 57.7 us
  between operations: 16.1 us -> 0.7 us
  starting transfers between devices: 17.7 us -> 3.62 us
    dot_general x46 -> x0, matrix products: 160 us -> none  [the longest x30 60.1 us: matmul(): return jnp.dot(left, right, preferred_element_type=jnp.float32)]
    psum x1 -> x0, waiting for transfers between devices: 131 us -> none  [shards(): lax.psum((enc_gain, enc_shift, enc_qkv, enc_outw, enc_upw, enc_upb, enc_d...]
    pallas_call x0 -> x6, Pallas kernels: none -> 108 us  [the longest x1 95.5 us: main_call(): pl.pallas_call(functools.partial(main_kernel, names, cap, extra, count),...]
    convert_element_type x11 -> x0, local copies, waits for them, and re-layouts: 58.2 us -> none  [the longest x2 27.5 us: backward_layer(): d_mixed = d_mixed.astype(jnp.bfloat16)]
    all_to_all x0 -> x3, blocking collectives: none -> 57.7 us  [the longest x2 34.3 us: exchange(): lax.all_to_all(values, axes, split_axis=0, concat_axis=0, axis_index_grou...]
    reshape x9 -> x0, local copies, waits for them, and re-layouts: 46.7 us -> none  [the longest x2 28.3 us: forward_layer(): matmul(first_low, wqkv).astype(jnp.bfloat16)]
    psum x1 -> x0, blocking collectives: 39 us -> none  [shards(): lax.psum((enc_gain, enc_shift, enc_qkv, enc_outw, enc_upw, enc_upb, enc_d...]
    dot_general x2 -> x0, local copies, waits for them, and re-layouts: 21.7 us -> none  [the longest x1 11 us: backward_layer(): jnp.einsum('pshe,pthe->phst', d_attended, value_rows, preferred_element_t...]
  transfers between devices with their start and end apart: 4 -> 3, of which waited for: 3 -> 2; matrix products, arithmetic and copies ran while one was open for 10% -> 0% of each run, Pallas kernels for 0% -> 1%
where the time goes in v1:
time: 191 us; the launch traced here: 190 us
  Pallas kernels  108 us (57%)
  blocking collectives  57.7 us (30%)
  waiting for transfers between devices  16 us (8%)
  local copies, waits for them, and re-layouts  3.93 us (2%)
  starting transfers between devices  3.62 us (2%)
    pallas_call x1, Pallas kernels, main_call(): pl.pallas_call(functools.partial(main_kernel, names, cap, extra, count),...  95.5 us
    all_to_all x2, blocking collectives, exchange(): lax.all_to_all(values, axes, split_axis=0, concat_axis=0, axis_index_grou...  34.3 us
    all_to_all x1, blocking collectives, shards(): lax.all_to_all(payload.reshape(count, block, VIS, width), 'pix', split_ax...  23.4 us
    all_to_all x1, waiting for transfers between devices, shards(): lax.all_to_all(back.reshape(count, cap, VIS, width), 'pix', split_axis=0,...  13.4 us
    unnamed x9, local copies, waits for them, and re-layouts  3.93 us
  transfers between devices with their start and end apart: 3, of which 2 were waited for; matrix products, arithmetic and copies ran while one was open for 0% of the time, Pallas kernels for 1%

profile of v1, /device:TPU:0, one launch (start us, length us, event | category | flops | bytes accessed | tf_op | source)
XLA Modules:
  0.0 190.1 jit_solution(7222288144329143516)
XLA Ops:
  0.6 1.4 copy.28.masked_ref
  2.1 3.6 %prep.1 = (bf16[272,8,128]{2,1,0:T(8,128)(2,1)}, f32[8,128]{1,0:T(8,128)}, s32[128]{0:T(128)}, s32[128]{0:T(128)}, s32[128]{0:T(128)}) custom-call(s32[1]{0:T(128)} %bitcast.me_ref, s32[128]{0:T(128)} %dest_ref.1, bf16[3072,128]{1,0:T(8,128)(2,1)} %bitcast.25, s32[1,128]{1,0:T(1,128)} %bitcast.31, s32[128,24]{1,0:T(8,128)} %copy.28.masked_ref, s32[1,128]{1,0:T(1,128)} %bitcast.29), custom_call_target="tpu_custom_call" | custom-call | tf_op jit(solution)/shard_map/prep/pallas_call | solution.py:147
  5.7 23.4 %all_to_all.20 = bf16[8,34,8,128]{3,2,1,0:T(8,128)(2,1)} all-to-all(bf16[8,34,8,128]{3,2,1,0:T(8,128)(2,1)} %bitcast.26), channel_id=1, replica_groups=mesh['pix'=8,'rep'=4] {'pix'}, dimensions={0} | all-to-all | bytes 1114112 | tf_op jit(solution)/shard_map/all_to_all | solution.py:695
  29.1 95.5 %layers.1 = (f32[128,24,128]{2,1,0:T(8,128)}, bf16[256,8,128]{2,1,0:T(8,128)(2,1)}, bf16[3328,128]{1,0:T(8,128)(2,1)}) custom-call(s32[128]{0:T(128)} %get-tuple-element.30.refs_0_, s32[128]{0:T(128)} %get-tuple-element.31.refs_1_, s32[128]{0:T(128)} %refs_2_.1, bf16[272,8,128]{2,1,0:T(8,128)(2,1)} %bitcast.18, bf16[128,24,128]{2,1,0:T(8,128)(2,1)} %refs_4_.1, ...), custom_call_target="tpu_custom_call" | custom-call | tf_op jit(solution)/shard_map/layers/pallas_call | solution.py:586
  124.6 0.0 collective-permute-start
  124.6 2.6 %collective-permute-done.theirs_ref = bf16[2,16,104,128]{3,2,1,0:T(8,128)(2,1)S(1)} collective-permute-done((bf16[2,16,104,128]{3,2,1,0:T(8,128)(2,1)}, bf16[2,16,104,128]{3,2,1,0:T(8,128)(2,1)S(1)}, u32[]{:S(2)}, u32[]{:S(2)}) %collective-permute-start) | collective-permute-done | bytes 852000 | tf_op jit(solution)/shard_map/ppermute | solution.py:724
  127.2 0.0 copy-start.2
  127.2 0.9 copy-done.2
  128.1 2.3 %pair_sum.1 = bf16[16,104,128]{2,1,0:T(8,128)(2,1)} custom-call(s32[1]{0:T(128)} %bitcast.12.core_ref, bf16[2,16,104,128]{3,2,1,0:T(8,128)(2,1)} %bitcast.24, bf16[2,16,104,128]{3,2,1,0:T(8,128)(2,1)} %copy-done.2), custom_call_target="tpu_custom_call" | custom-call | tf_op jit(solution)/shard_map/pair_sum/pallas_call | solution.py:725
  130.4 18.0 %all_to_all.21.parts_ref = bf16[16,104,128]{2,1,0:T(8,128)(2,1)} all-to-all(bf16[16,104,128]{2,1,0:T(8,128)(2,1)} %pair_sum.1), channel_id=1, replica_groups={{0,2,4,6,8,10,12,14,16,18,20,22,24,26,28,30},{1,3,5,7,9,11,13,15,17,19,..., dimensions={0} | all-to-all | bytes 851968 | tf_op jit(solution)/shard_map/all_to_all | solution.py:719
  148.3 1.8 chunk_sum.1
  150.2 16.3 %all_to_all.22 = bf16[16,104,128]{2,1,0:T(8,128)(2,1)S(1)} all-to-all(bf16[16,104,128]{2,1,0:T(8,128)(2,1)} %chunk_sum.1), channel_id=1, replica_groups={{0,2,4,6,8,10,12,14,16,18,20,22,24,26,28,30},{1,3,5,7,9,11,13,15,17,19,..., dimensions={0} | all-to-all | bytes 851968 | tf_op jit(solution)/shard_map/all_to_all | solution.py:719
  166.5 0.0 copy-start.1
  166.5 3.6 %all-to-all-start.1 = ((bf16[8,32,8,128]{3,2,1,0:T(8,128)(2,1)}), bf16[8,32,8,128]{3,2,1,0:T(8,128)(2,1)S(1)}, u32[]{:S(2)}, u32[]{:S(2)}) async-start(bf16[8,32,8,128]{3,2,1,0:T(8,128)(2,1)} %bitcast.9), calls=%async_computation.1 | async-start | bytes 1048576 | tf_op jit(solution)/shard_map/all_to_all | solution.py:711
  170.1 0.0 collective-permute-start.1
  170.1 13.4 %all-to-all-done.1 = bf16[8,32,8,128]{3,2,1,0:T(8,128)(2,1)S(1)} async-done(((bf16[8,32,8,128]{3,2,1,0:T(8,128)(2,1)}), bf16[8,32,8,128]{3,2,1,0:T(8,128)(2,1)S(1)}, u32[]{:S(2)}, u32[]{:S(2)}) %all-to-all-start.1) | async-done | bytes 524320 | tf_op jit(solution)/shard_map/all_to_all | solution.py:711
  183.5 0.0 copy-start
  183.5 0.8 copy-done
  184.3 2.6 %restore.1 = f32[3072,128]{1,0:T(8,128)} custom-call(s32[128]{0:T(128)} %get-tuple-element.34.place_ref, f32[8,128]{1,0:T(8,128)} %get-tuple-element.35.pos_ref, bf16[256,8,128]{2,1,0:T(8,128)(2,1)} %bitcast.19), custom_call_target="tpu_custom_call" | custom-call | tf_op jit(solution)/shard_map/restore/pallas_call | solution.py:758
  186.9 0.0 copy-done.1
  186.9 0.0 collective-permute-done.1.theirs_ref
  186.9 0.0 copy-start.3
  186.9 0.8 copy-done.3
  187.7 2.4 %unpack.1 = (f32[4,128]{1,0:T(4,128)}, f32[4,128]{1,0:T(4,128)}, f32[2,128,384]{2,1,0:T(8,128)}, f32[2,128,128]{2,1,0:T(8,128)}, f32[2,128,512]{2,1,0:T(8,128)},...) custom-call(s32[1]{0:T(128)} %bitcast.12.core_ref, ...), custom_call_target="tpu_custom_call" | custom-call | tf_op jit(solution)/shard_map/unpack/pallas_call | solution.py:743
Async XLA Ops:
  124.6 2.6 %collective-permute-start = (bf16[2,16,104,128]{3,2,1,0:T(8,128)(2,1)}, bf16[2,16,104,128]{3,2,1,0:T(8,128)(2,1)S(1)}, u32[]{:S(2)}, u32[]{:S(2)}) collective-permute-start(bf16[2,16,104,128]{3,2,1,0:T(8,128)(2,1)} %bitcast.23), channel_id=1, source_target_pairs={{0,1},{1,0},{2,3},{3,2},{4,5},{5,4},{6,7},{7,6},{8,9},{9,8},{10,11... | collective-permute-start | bytes 2555912 | tf_op jit(solution)/shard_map/ppermute | solution.py:724
  127.2 0.9 copy-start.2
  166.5 20.4 %copy-start.1 = (bf16[16,104,128]{2,1,0:T(8,128)(2,1)}, bf16[16,104,128]{2,1,0:T(8,128)(2,1)S(1)}, u32[]{:S(2)}) copy-start(bf16[16,104,128]{2,1,0:T(8,128)(2,1)S(1)} %all_to_all.22) | copy-start | bytes 1277956
  166.5 17.0 %all-to-all-start.1 = ((bf16[8,32,8,128]{3,2,1,0:T(8,128)(2,1)}), bf16[8,32,8,128]{3,2,1,0:T(8,128)(2,1)S(1)}, u32[]{:S(2)}, u32[]{:S(2)}) async-start(bf16[8,32,8,128]{3,2,1,0:T(8,128)(2,1)} %bitcast.9), calls=%async_computation.1 | async-start | bytes 1048576 | tf_op jit(solution)/shard_map/all_to_all | solution.py:711
  170.1 16.8 %collective-permute-start.1 = (bf16[1664,128]{1,0:T(8,128)(2,1)S(1)}, bf16[1664,128]{1,0:T(8,128)(2,1)S(1)}, u32[]{:S(2)}, u32[]{:S(2)}) collective-permute-start(bf16[1664,128]{1,0:T(8,128)(2,1)S(1)} %bitcast.20), channel_id=1, source_target_pairs={{0,1},{1,0},{2,3},{3,2},{4,5},{5,4},{6,7},{7,6},{8,9},{9,8},{10,11... | collective-permute-start | bytes 1277960 | tf_op jit(solution)/shard_map/ppermute | solution.py:742
  183.5 0.8 copy-start
  186.9 0.8 copy-start.3

commit v2 on v1

--- a/solution.py
+++ b/solution.py
@@ -9,6 +9,10 @@
 
 HEADS = 8
 HEAD_DIM = 16
+FOLD = 4
+BATCH = 16
+PAIRS = 16
+ENC_ROWS = 512
 VIS = 8
 GROUP = 16
 PAD = 32
@@ -65,6 +69,67 @@
     for head in range(1, HEADS):
         picked = jnp.where(lane >= head * HEAD_DIM, rows[head * step : head * step + count], picked)
     return picked
+
+
+def fold_halves(rows, step, count):
+    lane = iota((count, 128), 1) // HEAD_DIM % FOLD
+    picked = rows[0:count]
+    for head in range(1, FOLD):
+        picked = jnp.where(lane == head, rows[head * step : head * step + count], picked)
+    return picked
+
+
+def expand_halves(rows, masks):
+    return jnp.concatenate([rows * masks[h] for h in range(FOLD)], axis=0)
+
+
+def stack_halves(values):
+    low = iota(values.shape, 1) < 64
+    return jnp.concatenate([jnp.where(low, values, 0.0), jnp.where(low, 0.0, values)], axis=0).astype(BF)
+
+
+def join_halves(values):
+    count = values.shape[0] // 2
+    return jnp.where(iota((count, 128), 1) < 64, values[:count], values[count:])
+
+
+def both_diagonals(values, rows):
+    return values[:rows, :128], values[rows:, 128:]
+
+
+def block_diagonal(first, second):
+    low = jnp.concatenate([first, jnp.zeros_like(first)], axis=1)
+    return jnp.concatenate([low, jnp.concatenate([jnp.zeros_like(second), second], axis=1)], axis=0)
+
+
+def pair_nt(rows, columns):
+    full = nt(jnp.concatenate(rows, axis=0), jnp.concatenate(columns, axis=0))
+    return both_diagonals(full, rows[0].shape[0])
+
+
+def pair_nn(rows, columns):
+    full = nn(jnp.concatenate(rows, axis=0), jnp.concatenate(columns, axis=1))
+    return both_diagonals(full, rows[0].shape[0])
+
+
+def pair_tn(rows, columns):
+    full = tn(jnp.concatenate(rows, axis=0), block_diagonal(*columns))
+    return full[:, :128], full[:, 128:]
+
+
+def softmax_halves(scores, keep):
+    count = scores.shape[0] // 2
+    scores = jnp.where(keep[None], scores.reshape(2, count, 128), NEG)
+    powers = jnp.exp(scores - jnp.max(scores, axis=1, keepdims=True))
+    probs = powers * (1.0 / jnp.sum(powers, axis=1, keepdims=True))
+    return probs.reshape(2 * count, 128)
+
+
+def soft_bwd_halves(probs, grad):
+    count = probs.shape[0] // 2
+    both = (grad * probs).reshape(2, count, 128)
+    lean = jnp.sum(both, axis=1, keepdims=True)
+    return (probs.reshape(2, count, 128) * (grad.reshape(2, count, 128) - lean)).reshape(2 * count, 128).astype(BF)
 
 
 def ln_fwd(values, gain, bias, hat, inv, low, where):
@@ -197,211 +262,514 @@
     return (probs * (grad - jnp.sum(grad * probs, axis=0, keepdims=True))).astype(BF)
 
 
-def encoder_fwd(b, base, rows):
-    w = b.w
-    for start in range(0, rows, 32):
-        where = pl.ds(base + start, 32)
-        ln_fwd(b.e_x[where], w.gain[0:1], w.bias[0:1], b.e_hat1, b.e_inv1, b.e_n1, where)
-    whole = pl.ds(base, rows)
-    qkv = nn(b.e_n1[whole], w.qkv[0])
-    for start in range(0, rows, 32):
-        where = pl.ds(base + start, 32)
-        part = qkv[start : start + 32]
-        b.e_qkv[where, 0:128] = (part[:, 0:128] * 0.25).astype(BF)
-        b.e_qkv[where, 128:384] = part[:, 128:384].astype(BF)
-    same = iota((16, 128), 0) // VIS == (iota((16, 128), 1) % 16) // VIS
-    for start in range(0, rows, 16):
-        where = pl.ds(base + start, 16)
-        query = expand(b.e_qkv[where, 0:128], b.masks)
-        keep = same & (b.pos_col[where] > 0)
-        probs = softmax_rows(nt(b.e_qkv[where, 128:256], query), keep)
-        b.e_probs[where] = probs
-        mixed = tn(probs.astype(BF), b.e_qkv[where, 256:384])
-        b.e_att[where] = fold_heads(mixed, 16, 16).astype(BF)
-    proj = nn(b.e_att[whole], w.out[0])
-    for start in range(0, rows, 32):
-        where = pl.ds(base + start, 32)
-        middle = b.e_x[where] + proj[start : start + 32]
-        b.e_x[where] = middle
-        ln_fwd(middle, w.gain[1:2], w.bias[1:2], b.e_hat2, b.e_inv2, b.e_n2, where)
-    hidden = nn(b.e_n2[whole], w.up[0])
-    gelu_stage(hidden, w.b_up[0:1], b.e_act, b.e_slope, base, rows)
-    down = nn(b.e_act[whole], w.down[0])
-    for start in range(0, rows, 32):
-        where = pl.ds(base + start, 32)
-        b.sent[where] = (b.e_x[where] + down[start : start + 32] + w.b_down[0:1]).astype(BF)
-
-
-def encoder_bwd(b, base, rows):
-    w = b.w
-    whole = pl.ds(base, rows)
-    grad_low = b.g_sent[whole]
-    b.d_down[0] += tn(grad_low, b.e_act[whole])
-    b.d_b_down[0] += fold_rows(grad_low.astype(F32))
-    grad_act = nn(grad_low, b.down_t[0])
-    b.d_b_up[0] += slope_stage(grad_act, b.e_slope, b.e_gh, base, rows)
-    b.d_up[0] += tn(b.e_n2[whole], b.e_gh[...])
-    grad_n2 = nn(b.e_gh[...], b.up_t[0])
-    for start in range(0, rows, 32):
-        where = pl.ds(base + start, 32)
-        grad, gain_part, bias_part = ln_bwd(
-            grad_n2[start : start + 32], w.gain[1:2], b.e_hat2, b.e_inv2, where
+class Encoder:
+    def __init__(self, b, base, rows):
+        self.b, self.base, self.rows = b, base, rows
+        self.whole = slice(base, base + rows)
+
+    def chunks(self):
+        return [slice(start, start + 32) for start in range(self.base, self.base + self.rows, 32)]
+
+    def part(self, values, where):
+        return values[where.start - self.base : where.stop - self.base]
+
+    def attend(self):
+        b, w, whole = self.b, self.b.w, self.whole
+        v = Box()
+        same = iota((16, 128), 0) // VIS == (iota((16, 128), 1) % 16) // VIS
+
+        def load(series):
+            b.e_x[series * VIS : (series + 1) * VIS] = b.recv[b.take[series]].astype(F32)
+
+        steps = [functools.partial(load, series) for series in range(self.base // VIS, (self.base + self.rows) // VIS)]
+
+        def norm(where):
+            ln_fwd(b.e_x[where], w.gain[0:1], w.bias[0:1], b.e_hat1, b.e_inv1, b.e_n1, where)
+
+        steps += [functools.partial(norm, where) for where in self.chunks()]
+
+        def project():
+            v.qkv = nn(b.e_n1[whole], w.qkv[0])
+            v.score, v.prob, v.mixed = {}, {}, {}
+
+        steps.append(project)
+
+        def split(where):
+            part = self.part(v.qkv, where)
+            b.e_qkv[where, 0:128] = (part[:, 0:128] * 0.25).astype(BF)
+            b.e_qkv[where, 128:384] = part[:, 128:384].astype(BF)
+
+        steps += [functools.partial(split, where) for where in self.chunks()]
+
+        def score(at):
+            pair = (at, at + 16)
+            queries = [expand(b.e_qkv[one : one + 16, 0:128], b.masks) for one in pair]
+            keys = [b.e_qkv[one : one + 16, 128:256] for one in pair]
+            v.score[at], v.score[at + 16] = pair_nt(keys, queries)
+
+        def soft(at):
+            v.prob[at] = softmax_rows(v.score[at], same & (b.pos_col[at : at + 16] > 0))
+            b.e_probs[at : at + 16] = v.prob[at]
+
+        def mix(at):
+            pair = (at, at + 16)
+            values = [b.e_qkv[one : one + 16, 256:384] for one in pair]
+            v.mixed[at], v.mixed[at + 16] = pair_tn([v.prob[one].astype(BF) for one in pair], values)
+
+        def gather(at):
+            b.e_att[at : at + 16] = fold_heads(v.mixed[at], 16, 16).astype(BF)
+
+        for first in range(self.base, self.base + self.rows, 16 * PAIRS):
+            for stage, stride in ((score, 32), (soft, 16), (mix, 32), (gather, 16)):
+                steps += [functools.partial(stage, at) for at in range(first, first + 16 * PAIRS, stride)]
+
+        def out():
+            v.proj = nn(b.e_att[whole], w.out[0])
+
+        steps.append(out)
+
+        def second(where):
+            middle = b.e_x[where] + self.part(v.proj, where)
+            b.e_x[where] = middle
+            ln_fwd(middle, w.gain[1:2], w.bias[1:2], b.e_hat2, b.e_inv2, b.e_n2, where)
+
+        steps += [functools.partial(second, where) for where in self.chunks()]
+        return steps
+
+    def bend(self):
+        b, w, whole = self.b, self.b.w, self.whole
+        v = Box()
+
+        def up():
+            v.hidden = nn(b.e_n2[whole], w.up[0])
+
+        def curve(start):
+            value = v.hidden[start : start + 16] + w.b_up[0:1]
+            cdf, bell = erf_parts(value)
+            where = slice(self.base + start, self.base + start + 16)
+            b.e_act[where] = (value * cdf).astype(BF)
+            b.e_slope[where] = cdf + value * bell * 0.3989422804014327
+
+        def down():
+            v.down = nn(b.e_act[whole], w.down[0])
+
+        def finish(where):
+            b.sent[where] = (b.e_x[where] + self.part(v.down, where) + w.b_down[0:1]).astype(BF)
+
+        return (
+            [up]
+            + [functools.partial(curve, start) for start in range(0, self.rows, 16)]
+            + [down]
+            + [functools.partial(finish, where) for where in self.chunks()]
         )
-        b.d_gain[1] += gain_part
-        b.d_bias[1] += bias_part
-        grad = grad + b.g_sent[where].astype(F32)
-        b.e_gm[pl.ds(start, 32)] = grad
-        b.e_gml[pl.ds(start, 32)] = grad.astype(BF)
-    b.d_out[0] += tn(b.e_att[whole], b.e_gml[...])
-    b.e_ga[...] = nn(b.e_gml[...], b.out_t[0]).astype(BF)
-    for start in range(0, rows, 16):
-        where = pl.ds(base + start, 16)
-        query = expand(b.e_qkv[where, 0:128], b.masks)
-        grad_out = expand(b.e_ga[start : start + 16], b.masks)
-        probs = b.e_probs[where]
-        grad_s = soft_bwd(probs, nt(b.e_qkv[where, 256:384], grad_out))
-        here = pl.ds(start, 16)
-        b.e_gqkv[here, 256:384] = nn(probs.astype(BF), grad_out).astype(BF)
-        b.e_gqkv[here, 128:256] = nn(grad_s, query).astype(BF)
-        grad_q = fold_heads(tn(grad_s, b.e_qkv[where, 128:256]), 16, 16)
-        b.e_gqkv[here, 0:128] = (grad_q * 0.25).astype(BF)
-    b.d_qkv[0] += tn(b.e_n1[whole], b.e_gqkv[...])
-    grad_n1 = nn(b.e_gqkv[...], b.qkv_t[0])
-    for start in range(0, rows, 32):
-        where = pl.ds(base + start, 32)
-        grad, gain_part, bias_part = ln_bwd(
-            grad_n1[start : start + 32], w.gain[0:1], b.e_hat1, b.e_inv1, where
-        )
-        b.d_gain[0] += gain_part
-        b.d_bias[0] += bias_part
-        b.g_enc[where] = grad + b.e_gm[pl.ds(start, 32)]
-
-
-def decoder_group(b, group):
-    w = b.w
-    slots = b.slots
-    rows = GROUP * slots
-    first = group * GROUP
-    lane = iota((1, 128), 1)
-    pos_row = b.pos_row[group]
-    target = jnp.where(pos_row > 0, (lane // VIS * slots).astype(F32) + pos_row - 1.0, -1.0)
-    for start in range(0, rows, CHUNK):
-        spot = (iota((CHUNK, 128), 0) + start).astype(F32)
-        b.hot[pl.ds(start, CHUNK)] = jnp.where(spot == target, 1.0, 0.0).astype(BF)
-    sent_rows = pl.ds(pl.multiple_of(group * 128, 128), 128)
-    placed = nn(b.hot[...], b.sent[sent_rows])
-    shown = nn(b.hot[...], jnp.ones((128, 128), BF))
-    step = iota((slots, 128), 0).astype(F32)
-
-    def span(member):
-        return pl.ds(member * slots, slots)
-
-    def inside(member):
-        lens = b.len_col[pl.ds(pl.multiple_of(group * 128, 128) + member * VIS, VIS)]
-        return step < jnp.concatenate([lens] * (slots // VIS), axis=0)
-
-    for member in range(GROUP):
-        at = slice(member * slots, (member + 1) * slots)
-        hidden_part = 1.0 - shown[at]
-        b.unseen[span(member)] = hidden_part
-        b.d_x[span(member)] = placed[at] + hidden_part * w.mask[...] + w.pos[...]
-        cot = b.cot[b.slot[first + member]].astype(F32)
-        b.d_g[span(member)] = jnp.where(inside(member), cot, 0.0)
-    for start in range(0, rows, CHUNK):
-        where = pl.ds(start, CHUNK)
-        ln_fwd(b.d_x[where], w.gain[2:3], w.bias[2:3], b.d_hat1, b.d_inv1, b.d_n1, where)
-    qkv = nn(b.d_n1[...], w.qkv[1])
-    zeros = jnp.zeros((PAD - slots, 128), F32)
-
-    def padded(values):
-        return jnp.concatenate([values, zeros], axis=0).astype(BF)
-
-    wide_zero = jnp.zeros((PAD - slots, HEADS * PAD), F32)
-
-    def padded_wide(values):
-        return jnp.concatenate([values, wide_zero], axis=0).astype(BF)
-
-    for member in range(GROUP):
-        at = slice(member * slots, (member + 1) * slots)
-        query_low = padded(qkv[at, 0:128] * 0.25)
-        key_low = padded(qkv[at, 128:256])
-        value_low = padded(qkv[at, 256:384])
-        b.d_q[member] = query_low
-        b.d_k[member] = key_low
-        b.d_v[member] = value_low
-        scores = nt(key_low, expand(query_low, b.masks))[:slots]
-        ok = inside(member)
-        probs = softmax_rows(scores, jnp.concatenate([ok, ok], axis=1))
-        b.d_probs[member] = probs
-        mixed = tn(padded_wide(probs), value_low)
-        b.d_att32[span(member)] = fold_heads(mixed, PAD, slots)
-    for start in range(0, rows, CHUNK):
-        where = pl.ds(start, CHUNK)
-        b.d_att[where] = b.d_att32[where].astype(BF)
-    proj = nn(b.d_att[...], w.out[1])
-    for start in range(0, rows, CHUNK):
-        where = pl.ds(start, CHUNK)
-        middle = b.d_x[where] + proj[start : start + CHUNK]
-        b.d_x[where] = middle
-        ln_fwd(middle, w.gain[3:4], w.bias[3:4], b.d_hat2, b.d_inv2, b.d_n2, where)
-    hidden = nn(b.d_n2[...], w.up[1])
-    gelu_stage(hidden, w.b_up[1:2], b.d_act, b.d_slope, 0, rows)
-    down = nn(b.d_act[...], w.down[1])
-    for member in range(GROUP):
-        at = slice(member * slots, (member + 1) * slots)
-        value = b.d_x[span(member)] + down[at] + w.b_down[1:2]
-        b.dec[b.slot[first + member]] = jnp.where(inside(member), value, 0.0)
-    for start in range(0, rows, CHUNK):
-        where = pl.ds(start, CHUNK)
-        b.d_gl[where] = b.d_g[where].astype(BF)
-    b.d_down[1] += tn(b.d_gl[...], b.d_act[...])
-    b.d_b_down[1] += fold_rows(b.d_g[...])
-    grad_act = nn(b.d_gl[...], b.down_t[1])
-    b.d_b_up[1] += slope_stage(grad_act, b.d_slope, b.d_gh, 0, rows)
-    b.d_up[1] += tn(b.d_n2[...], b.d_gh[...])
-    grad_n2 = nn(b.d_gh[...], b.up_t[1])
-    for start in range(0, rows, CHUNK):
-        where = pl.ds(start, CHUNK)
-        grad, gain_part, bias_part = ln_bwd(
-            grad_n2[start : start + CHUNK], w.gain[3:4], b.d_hat2, b.d_inv2, where
-        )
-        b.d_gain[3] += gain_part
-        b.d_bias[3] += bias_part
-        grad = grad + b.d_g[where]
-        b.d_g[where] = grad
-        b.d_gl[where] = grad.astype(BF)
-    b.d_out[1] += tn(b.d_att[...], b.d_gl[...])
-    grad_att = nn(b.d_gl[...], b.out_t[1])
-    for member in range(GROUP):
-        at = slice(member * slots, (member + 1) * slots)
-        query = expand(b.d_q[member], b.masks)
-        grad_out = expand(padded(grad_att[at]), b.masks)
-        probs = b.d_probs[member]
-        grad_s = soft_bwd(probs, nt(b.d_v[member], grad_out)[:slots])
-        grad_s = jnp.concatenate([grad_s.astype(F32), wide_zero], axis=0).astype(BF)
-        b.d_gqkv32[span(member), 256:384] = nn(padded_wide(probs), grad_out)[:slots]
-        b.d_gqkv32[span(member), 128:256] = nn(grad_s, query)[:slots]
-        b.d_gqkv32[span(member), 0:128] = fold_heads(tn(grad_s, b.d_k[member]), PAD, slots) * 0.25
-    for start in range(0, rows, CHUNK):
-        where = pl.ds(start, CHUNK)
-        b.d_gqkv[where] = b.d_gqkv32[where].astype(BF)
-    b.d_qkv[1] += tn(b.d_n1[...], b.d_gqkv[...])
-    grad_n1 = nn(b.d_gqkv[...], b.qkv_t[1])
-    pos_total = None
-    for start in range(0, rows, CHUNK):
-        where = pl.ds(start, CHUNK)
-        grad, gain_part, bias_part = ln_bwd(
-            grad_n1[start : start + CHUNK], w.gain[2:3], b.d_hat1, b.d_inv1, where
-        )
-        b.d_gain[2] += gain_part
-        b.d_bias[2] += bias_part
-        grad = grad + b.d_g[where]
-        b.d_gl[where] = grad.astype(BF)
-        part = jnp.sum(grad.reshape(CHUNK // slots, slots, 128), axis=0)
-        pos_total = part if pos_total is None else pos_total + part
-        b.d_mask[...] += fold_rows(grad * b.unseen[where])
-    b.d_pos[...] += pos_total
-    b.g_sent[sent_rows] = tn(b.hot[...], b.d_gl[...]).astype(BF)
+
+    def feed(self):
+        b, whole = self.b, self.whole
+        v = Box()
+
+        def back():
+            grad_low = b.g_sent[whole]
+            b.d_down[0] += tn(grad_low, b.e_act[whole])
+            b.d_b_down[0] += fold_rows(grad_low.astype(F32))
+            v.grad_act = nn(grad_low, b.down_t[0])
+            v.total = None
+
+        def unbend(start):
+            where = slice(self.base + start, self.base + start + 16)
+            part = (v.grad_act[start : start + 16] * b.e_slope[where]).astype(BF)
+            b.e_gh[where] = part
+            summed = fold_rows(part.astype(F32))
+            v.total = summed if v.total is None else v.total + summed
+
+        def end():
+            b.d_b_up[0] += v.total
+            b.d_up[0] += tn(b.e_n2[whole], b.e_gh[whole])
+            b.e_gn2[whole] = nn(b.e_gh[whole], b.up_t[0])
+
+        return [back] + [functools.partial(unbend, start) for start in range(0, self.rows, 16)] + [end]
+
+    def retreat(self):
+        b, w, whole = self.b, self.b.w, self.whole
+        v = Box()
+
+        def norm(where):
+            grad, gain_part, bias_part = ln_bwd(b.e_gn2[where], w.gain[1:2], b.e_hat2, b.e_inv2, where)
+            b.d_gain[1] += gain_part
+            b.d_bias[1] += bias_part
+            grad = grad + b.g_sent[where].astype(F32)
+            b.e_gm[where] = grad
+            b.e_gml[where] = grad.astype(BF)
+
+        steps = [functools.partial(norm, where) for where in self.chunks()]
+
+        def out():
+            b.d_out[0] += tn(b.e_att[whole], b.e_gml[whole])
+            v.grad_att = nn(b.e_gml[whole], b.out_t[0])
+            v.grad, v.grad_p, v.grad_s, v.grad_v, v.grad_k, v.grad_q = ({} for _ in range(6))
+
+        steps.append(out)
+
+        def spread(at):
+            pair = (at, at + 16)
+            for one in pair:
+                low = v.grad_att[one - self.base : one - self.base + 16].astype(BF)
+                v.grad[one] = expand(low, b.masks)
+            values = [b.e_qkv[one : one + 16, 256:384] for one in pair]
+            v.grad_p[at], v.grad_p[at + 16] = pair_nt(values, [v.grad[one] for one in pair])
+
+        def values(at):
+            pair = (at, at + 16)
+            probs = [b.e_probs[one : one + 16].astype(BF) for one in pair]
+            v.grad_v[at], v.grad_v[at + 16] = pair_nn(probs, [v.grad[one] for one in pair])
+
+        def soft(at):
+            v.grad_s[at] = soft_bwd(b.e_probs[at : at + 16], v.grad_p[at])
+
+        def keys(at):
+            pair = (at, at + 16)
+            columns = [expand(b.e_qkv[one : one + 16, 0:128], b.masks) for one in pair]
+            v.grad_k[at], v.grad_k[at + 16] = pair_nn([v.grad_s[one] for one in pair], columns)
+
+        def queries(at):
+            pair = (at, at + 16)
+            keys = [b.e_qkv[one : one + 16, 128:256] for one in pair]
+            v.grad_q[at], v.grad_q[at + 16] = pair_tn([v.grad_s[one] for one in pair], keys)
+
+        def gather(at):
+            b.e_gqkv[at : at + 16, 256:384] = v.grad_v[at].astype(BF)
+            b.e_gqkv[at : at + 16, 128:256] = v.grad_k[at].astype(BF)
+            b.e_gqkv[at : at + 16, 0:128] = (fold_heads(v.grad_q[at], 16, 16) * 0.25).astype(BF)
+
+        for first in range(self.base, self.base + self.rows, 16 * PAIRS):
+            for stage, stride in ((spread, 32), (values, 32), (soft, 16), (keys, 32), (queries, 32), (gather, 16)):
+                steps += [functools.partial(stage, at) for at in range(first, first + 16 * PAIRS, stride)]
+
+        def project():
+            b.d_qkv[0] += tn(b.e_n1[whole], b.e_gqkv[whole])
+            v.grad_n1 = nn(b.e_gqkv[whole], b.qkv_t[0])
+
+        steps.append(project)
+
+        def first_norm(where):
+            grad, gain_part, bias_part = ln_bwd(
+                self.part(v.grad_n1, where), w.gain[0:1], b.e_hat1, b.e_inv1, where
+            )
+            b.d_gain[0] += gain_part
+            b.d_bias[0] += bias_part
+            grad = grad + b.e_gm[where]
+            for series in range(where.start // VIS, where.stop // VIS):
+                at = series * VIS - where.start
+                b.back[b.back_at[series]] = grad[at : at + VIS].astype(BF)
+
+        steps += [functools.partial(first_norm, where) for where in self.chunks()]
+        return steps
+
+
+def weave(*streams):
+    lists = [list(stream) for stream in streams]
+    order = []
+    for which, steps in enumerate(lists):
+        order += [((index + 0.5) / len(steps), which, step) for index, step in enumerate(steps)]
+    for _, _, step in sorted(order, key=lambda entry: entry[:2]):
+        step()
+
+
+class Decoder:
+    def __init__(self, b, d, group):
+        self.b, self.d, self.group = b, d, group
+        self.slots = b.slots
+        self.rows = GROUP * b.slots
+        self.sent_rows = pl.ds(pl.multiple_of(group * 128, 128), 128)
+        self.zeros = jnp.zeros((PAD - b.slots, 128), F32)
+        self.step = iota((b.slots, 128), 0).astype(F32)
+
+    def span(self, member):
+        return pl.ds(member * self.slots, self.slots)
+
+    def cut(self, member):
+        return slice(member * self.slots, (member + 1) * self.slots)
+
+    def inside(self, member):
+        lens = self.b.len_col[pl.ds(pl.multiple_of(self.group * 128, 128) + member * VIS, VIS)]
+        return self.step < jnp.concatenate([lens] * (self.slots // VIS), axis=0)
+
+    def padded(self, values):
+        return jnp.concatenate([values, self.zeros], axis=0).astype(BF)
+
+    def chunks(self):
+        return range(0, self.rows, CHUNK)
+
+    def attend(self):
+        b, d, w, slots = self.b, self.d, self.b.w, self.slots
+        v = Box()
+        steps = []
+
+        def begin():
+            pos_row = b.pos_row[self.group]
+            lane = iota((1, 128), 1)
+            target = jnp.where(pos_row > 0, (lane // VIS * slots).astype(F32) + pos_row - 1.0, -1.0)
+            for start in self.chunks():
+                spot = (iota((CHUNK, 128), 0) + start).astype(F32)
+                d.hot[pl.ds(start, CHUNK)] = jnp.where(spot == target, 1.0, 0.0).astype(BF)
+            v.placed = nn(d.hot[...], b.sent[self.sent_rows])
+            v.shown = nn(d.hot[...], jnp.ones((128, 128), BF))
+
+        steps.append(begin)
+
+        def assemble(member):
+            at = self.cut(member)
+            hidden_part = 1.0 - v.shown[at]
+            d.unseen[self.span(member)] = hidden_part
+            d.x[self.span(member)] = v.placed[at] + hidden_part * w.mask[...] + w.pos[...]
+            cot = b.cot[b.slot[self.group * GROUP + member]].astype(F32)
+            d.g[self.span(member)] = jnp.where(self.inside(member), cot, 0.0)
+
+        steps += [functools.partial(assemble, member) for member in range(GROUP)]
+
+        def norm(start):
+            where = pl.ds(start, CHUNK)
+            ln_fwd(d.x[where], w.gain[2:3], w.bias[2:3], d.hat1, d.inv1, d.n1, where)
+
+        steps += [functools.partial(norm, start) for start in self.chunks()]
+
+        def project():
+            v.qkv = nn(d.n1[...], w.qkv[1])
+            v.score, v.prob, v.mixed = {}, {}, {}
+
+        steps.append(project)
+
+        def split(member):
+            at = self.cut(member)
+            d.q[member] = self.padded(v.qkv[at, 0:128] * 0.25)
+            d.k[member] = stack_halves(v.qkv[at, 128:256])
+            d.v[member] = stack_halves(v.qkv[at, 256:384])
+
+        def score(member):
+            pair = (member, member + 1)
+            queries = [expand_halves(d.q[one], b.masks_half) for one in pair]
+            v.score[member], v.score[member + 1] = pair_nt([d.k[one] for one in pair], queries)
+
+        def soft(member):
+            v.prob[member] = softmax_halves(v.score[member], self.inside(member))
+            d.probs[member] = v.prob[member]
+
+        def mix(member):
+            pair = (member, member + 1)
+            mixed = pair_tn([v.prob[one].astype(BF) for one in pair], [d.v[one] for one in pair])
+            v.mixed[member], v.mixed[member + 1] = mixed
+
+        def gather(member):
+            d.att32[self.span(member)] = fold_halves(v.mixed[member], PAD, slots)
+
+        for first in range(0, GROUP, BATCH):
+            for stage, stride in ((split, 1), (score, 2), (soft, 1), (mix, 2), (gather, 1)):
+                steps += [functools.partial(stage, member) for member in range(first, first + BATCH, stride)]
+
+        def low(start):
+            where = pl.ds(start, CHUNK)
+            d.att[where] = d.att32[where].astype(BF)
+
+        steps += [functools.partial(low, start) for start in self.chunks()]
+
+        def out():
+            v.proj = nn(d.att[...], w.out[1])
+
+        steps.append(out)
+
+        def second(start):
+            where = pl.ds(start, CHUNK)
+            middle = d.x[where] + v.proj[start : start + CHUNK]
+            d.x[where] = middle
+            ln_fwd(middle, w.gain[3:4], w.bias[3:4], d.hat2, d.inv2, d.n2, where)
+
+        steps += [functools.partial(second, start) for start in self.chunks()]
+        return steps
+
+    def bend(self):
+        b, d, w = self.b, self.d, self.b.w
+        v = Box()
+        steps = []
+
+        def up():
+            v.hidden = nn(d.n2[...], w.up[1])
+
+        steps.append(up)
+
+        def curve(start):
+            value = v.hidden[start : start + 16] + w.b_up[1:2]
+            cdf, bell = erf_parts(value)
+            where = pl.ds(start, 16)
+            d.act[where] = (value * cdf).astype(BF)
+            d.slope[where] = cdf + value * bell * 0.3989422804014327
+
+        steps += [functools.partial(curve, start) for start in range(0, self.rows, 16)]
+        return steps
+
+    def feed(self):
+        b, d, w = self.b, self.d, self.b.w
+        v = Box()
+        steps = []
+
+        def down():
+            v.down = nn(d.act[...], w.down[1])
+
+        steps.append(down)
+
+        def finish(member):
+            value = d.x[self.span(member)] + v.down[self.cut(member)] + w.b_down[1:2]
+            b.dec[b.slot[self.group * GROUP + member]] = jnp.where(self.inside(member), value, 0.0)
+
+        steps += [functools.partial(finish, member) for member in range(GROUP)]
+
+        def low(start):
+            where = pl.ds(start, CHUNK)
+            d.gl[where] = d.g[where].astype(BF)
+
+        steps += [functools.partial(low, start) for start in self.chunks()]
+
+        def back():
+            b.d_down[1] += tn(d.gl[...], d.act[...])
+            b.d_b_down[1] += fold_rows(d.g[...])
+            v.grad_act = nn(d.gl[...], b.down_t[1])
+            v.total = None
+
+        steps.append(back)
+
+        def unbend(start):
+            part = (v.grad_act[start : start + 16] * d.slope[pl.ds(start, 16)]).astype(BF)
+            d.gh[pl.ds(start, 16)] = part
+            summed = fold_rows(part.astype(F32))
+            v.total = summed if v.total is None else v.total + summed
+
+        steps += [functools.partial(unbend, start) for start in range(0, self.rows, 16)]
+
+        def end():
+            b.d_b_up[1] += v.total
+            b.d_up[1] += tn(d.n2[...], d.gh[...])
+            d.gn2[...] = nn(d.gh[...], b.up_t[1])
+
+        steps.append(end)
+        return steps
+
+    def retreat(self):
+        b, d, w, slots = self.b, self.d, self.b.w, self.slots
+        v = Box()
+        steps = []
+
+        def norm(start):
+            where = pl.ds(start, CHUNK)
+            grad, gain_part, bias_part = ln_bwd(d.gn2[where], w.gain[3:4], d.hat2, d.inv2, where)
+            b.d_gain[3] += gain_part
+            b.d_bias[3] += bias_part
+            grad = grad + d.g[where]
+            d.g[where] = grad
+            d.gl[where] = grad.astype(BF)
+
+        steps += [functools.partial(norm, start) for start in self.chunks()]
+
+        def out():
+            b.d_out[1] += tn(d.att[...], d.gl[...])
+            v.grad_att = nn(d.gl[...], b.out_t[1])
+            v.grad, v.prob, v.grad_p, v.grad_s, v.grad_v, v.grad_k, v.grad_q = ({} for _ in range(7))
+
+        steps.append(out)
+
+        def spread(member):
+            pair = (member, member + 1)
+            for one in pair:
+                v.grad[one] = expand_halves(self.padded(v.grad_att[self.cut(one)]), b.masks_half)
+            grads = [v.grad[one] for one in pair]
+            v.grad_p[member], v.grad_p[member + 1] = pair_nt([d.v[one] for one in pair], grads)
+
+        def values(member):
+            pair = (member, member + 1)
+            probs = [d.probs[one].astype(BF) for one in pair]
+            v.grad_v[member], v.grad_v[member + 1] = pair_nn(probs, [v.grad[one] for one in pair])
+
+        def soft(member):
+            v.grad_s[member] = soft_bwd_halves(d.probs[member], v.grad_p[member])
+
+        def keys(member):
+            pair = (member, member + 1)
+            columns = [expand_halves(d.q[one], b.masks_half) for one in pair]
+            v.grad_k[member], v.grad_k[member + 1] = pair_nn([v.grad_s[one] for one in pair], columns)
+
+        def queries(member):
+            pair = (member, member + 1)
+            grads = pair_tn([v.grad_s[one] for one in pair], [d.k[one] for one in pair])
+            v.grad_q[member], v.grad_q[member + 1] = grads
+
+        def gather(member):
+            d.gqkv32[self.span(member), 256:384] = join_halves(v.grad_v[member])
+            d.gqkv32[self.span(member), 128:256] = join_halves(v.grad_k[member])
+            d.gqkv32[self.span(member), 0:128] = fold_halves(v.grad_q[member], PAD, slots) * 0.25
+
+        for first in range(0, GROUP, BATCH):
+            for stage, stride in ((spread, 2), (values, 2), (soft, 1), (keys, 2), (queries, 2), (gather, 1)):
+                steps += [functools.partial(stage, member) for member in range(first, first + BATCH, stride)]
+
+        def low(start):
+            where = pl.ds(start, CHUNK)
+            d.gqkv[where] = d.gqkv32[where].astype(BF)
+
+        steps += [functools.partial(low, start) for start in self.chunks()]
+
+        def project():
+            b.d_qkv[1] += tn(d.n1[...], d.gqkv[...])
+            v.grad_n1 = nn(d.gqkv[...], b.qkv_t[1])
+            v.pos = None
+
+        steps.append(project)
+
+        def first_norm(start):
+            where = pl.ds(start, CHUNK)
+            grad, gain_part, bias_part = ln_bwd(
+                v.grad_n1[start : start + CHUNK], w.gain[2:3], d.hat1, d.inv1, where
+            )
+            b.d_gain[2] += gain_part
+            b.d_bias[2] += bias_part
+            grad = grad + d.g[where]
+            d.gl[where] = grad.astype(BF)
+            part = jnp.sum(grad.reshape(CHUNK // slots, slots, 128), axis=0)
+            v.pos = part if v.pos is None else v.pos + part
+            b.d_mask[...] += fold_rows(grad * d.unseen[where])
+
+        steps += [functools.partial(first_norm, start) for start in self.chunks()]
+
+        def end():
+            b.d_pos[...] += v.pos
+            b.g_sent[self.sent_rows] = tn(d.hot[...], d.gl[...]).astype(BF)
+
+        steps.append(end)
+        return steps
+
+
+def decoder_all(b, groups, before, after):
+    first, second = b.sets
+    pairs = groups // 2
+    here = Decoder(b, first, 0)
+    there = Decoder(b, second, 1)
+    weave(before, here.attend())
+    weave(here.bend())
+    weave(here.feed(), there.attend())
+
+    def pair(index, carry):
+        here = Decoder(b, first, 2 * index)
+        there = Decoder(b, second, 2 * index + 1)
+        later = Decoder(b, first, 2 * index + 2)
+        latest = Decoder(b, second, 2 * index + 3)
+        weave(there.bend(), here.retreat())
+        weave(there.feed(), later.attend())
+        weave(later.bend(), there.retreat())
+        weave(later.feed(), latest.attend())
+        return carry
+
+    lax.fori_loop(0, pairs - 1, pair, 0)
+    here = Decoder(b, first, groups - 2)
+    there = Decoder(b, second, groups - 1)
+    weave(there.bend(), here.retreat())
+    weave(there.feed())
+    weave(there.retreat(), after)
 
 
 IN_NAMES = (
@@ -417,8 +785,10 @@
 
 def main_kernel(names, cap, extra, count, *refs):
     b = Box()
+    b.sets = (Box(), Box())
     for name, ref in zip(names, refs, strict=True):
-        setattr(b, name, ref)
+        name, _, side = name.partition("@")
+        setattr(b.sets[int(side)] if side else b, name, ref)
     b.w = Box()
     for name in ("qkv", "out", "up", "down"):
         setattr(b.w, name, getattr(b, "w_" + name))
@@ -431,6 +801,9 @@
     for head in range(HEADS):
         lane = iota((PAD, 128), 1) // HEAD_DIM
         b.masks[head] = jnp.where(lane == head, 1.0, 0.0).astype(BF)
+    for head in range(FOLD):
+        lane = iota((PAD, 128), 1) // HEAD_DIM % FOLD
+        b.masks_half[head] = jnp.where(lane == head, 1.0, 0.0).astype(BF)
     for layer in range(2):
         b.qkv_t[layer] = b.w_qkv[layer].T
         b.out_t[layer] = b.w_out[layer].T
@@ -454,33 +827,14 @@
         b.pos_col[where] = jnp.broadcast_to(pos[group : group + 1], (128, 128)).T
         b.len_col[where] = jnp.broadcast_to(lens[group : group + 1], (128, 128)).T
 
-    enc_rows = 256
-    per = enc_rows // VIS
-
-    def enc_forward(step, carry):
-        base = pl.multiple_of(step * enc_rows, enc_rows)
-        for member in range(per):
-            b.e_x[pl.ds(base + member * VIS, VIS)] = b.recv[b.take[step * per + member]].astype(F32)
-        encoder_fwd(b, base, enc_rows)
-        return carry
-
-    lax.fori_loop(0, pixels // per, enc_forward, 0)
-
-    def dec_both(group, carry):
-        decoder_group(b, group)
-        return carry
-
-    lax.fori_loop(0, groups, dec_both, 0)
-
-    def enc_backward(step, carry):
-        base = pl.multiple_of(step * enc_rows, enc_rows)
-        encoder_bwd(b, base, enc_rows)
-        for member in range(per):
-            rows = b.g_enc[pl.ds(base + member * VIS, VIS)]
-            b.back[b.back_at[step * per + member]] = rows.astype(BF)
-        return carry
-
-    lax.fori_loop(0, pixels // per, enc_backward, 0)
+    encoders = [Encoder(b, base, ENC_ROWS) for base in range(0, pixels * VIS, ENC_ROWS)]
+    weave(encoders[0].attend())
+    for now, later in zip(encoders, encoders[1:]):
+        weave(now.bend(), later.attend())
+    decoder_all(b, groups, encoders[-1].bend(), encoders[0].feed())
+    for now, later in zip(encoders, encoders[1:]):
+        weave(now.retreat(), later.feed())
+    weave(encoders[-1].retreat())
 
     offset = 0
     for layer in range(2):
@@ -512,6 +866,34 @@
     b.grads[offset : offset + tail.shape[0]] = tail.astype(BF)
 
 
+def decoder_scratch(rows, slots):
+    return {
+        "hot": ((rows, 128), BF),
+        "unseen": ((rows, 128), F32),
+        "x": ((rows, 128), F32),
+        "g": ((rows, 128), F32),
+        "gl": ((rows, 128), BF),
+        "hat1": ((rows, 128), F32),
+        "inv1": ((rows, 128), F32),
+        "n1": ((rows, 128), BF),
+        "q": ((GROUP, PAD, 128), BF),
+        "k": ((GROUP, 2 * slots, 128), BF),
+        "v": ((GROUP, 2 * slots, 128), BF),
+        "probs": ((GROUP, 2 * slots, 128), F32),
+        "att32": ((rows, 128), F32),
+        "att": ((rows, 128), BF),
+        "hat2": ((rows, 128), F32),
+        "inv2": ((rows, 128), F32),
+        "n2": ((rows, 128), BF),
+        "act": ((rows, 512), BF),
+        "slope": ((rows, 512), F32),
+        "gh": ((rows, 512), BF),
+        "gn2": ((rows, 128), F32),
+        "gqkv32": ((rows, 384), F32),
+        "gqkv": ((rows, 384), BF),
+    }
+
+
 def main_call(args, cap, extra, count, grad_rows):
     recv, cot = args[3], args[4]
     pixels, slots, width = cot.shape
@@ -519,9 +901,9 @@
     rows = GROUP * slots
     smem = pl.BlockSpec(memory_space=pltpu.SMEM)
     vmem = pl.BlockSpec(memory_space=pltpu.VMEM)
-    enc_rows = 256
     scratch = {
         "masks": ((HEADS, PAD, 128), BF),
+        "masks_half": ((FOLD, PAD, 128), BF),
         "qkv_t": ((2, 384, 128), BF),
         "out_t": ((2, 128, 128), BF),
         "up_t": ((2, 512, 128), BF),
@@ -541,7 +923,6 @@
         "len_col": ((enc, 128), F32),
         "sent": ((enc, 128), BF),
         "g_sent": ((enc, 128), BF),
-        "g_enc": ((enc, 128), F32),
         "e_x": ((enc, 128), F32),
         "e_hat1": ((enc, 128), F32),
         "e_inv1": ((enc, 128), F32),
@@ -554,34 +935,15 @@
         "e_n2": ((enc, 128), BF),
         "e_act": ((enc, 512), BF),
         "e_slope": ((enc, 512), F32),
-        "e_gh": ((enc_rows, 512), BF),
-        "e_gm": ((enc_rows, 128), F32),
-        "e_gml": ((enc_rows, 128), BF),
-        "e_ga": ((enc_rows, 128), BF),
-        "e_gqkv": ((enc_rows, 384), BF),
-        "hot": ((rows, 128), BF),
-        "unseen": ((rows, 128), F32),
-        "d_x": ((rows, 128), F32),
-        "d_g": ((rows, 128), F32),
-        "d_gl": ((rows, 128), BF),
-        "d_hat1": ((rows, 128), F32),
-        "d_inv1": ((rows, 128), F32),
-        "d_n1": ((rows, 128), BF),
-        "d_q": ((GROUP, PAD, 128), BF),
-        "d_k": ((GROUP, PAD, 128), BF),
-        "d_v": ((GROUP, PAD, 128), BF),
-        "d_probs": ((GROUP, slots, HEADS * PAD), F32),
-        "d_att32": ((rows, 128), F32),
-        "d_att": ((rows, 128), BF),
-        "d_hat2": ((rows, 128), F32),
-        "d_inv2": ((rows, 128), F32),
-        "d_n2": ((rows, 128), BF),
-        "d_act": ((rows, 512), BF),
-        "d_slope": ((rows, 512), F32),
-        "d_gh": ((rows, 512), BF),
-        "d_gqkv32": ((rows, 384), F32),
-        "d_gqkv": ((rows, 384), BF),
+        "e_gh": ((enc, 512), BF),
+        "e_gn2": ((enc, 128), F32),
+        "e_gm": ((enc, 128), F32),
+        "e_gml": ((enc, 128), BF),
+        "e_gqkv": ((enc, 384), BF),
     }
+    for side in range(2):
+        for name, entry in decoder_scratch(rows, slots).items():
+            scratch[f"{name}@{side}"] = entry
     names = IN_NAMES + OUT_NAMES + tuple(scratch)
     return pl.pallas_call(
         functools.partial(main_kernel, names, cap, extra, count),

time: 191 us -> 136 us (0.71)
  Pallas kernels: 108 us -> 53.5 us
    pallas_call x1, Pallas kernels: 95.5 us -> 40.8 us  [main_call(): pl.pallas_call(functools.partial(main_kernel, names, cap, extra, count),...]
  transfers between devices with their start and end apart: 3 -> 3, of which waited for: 2 -> 2; matrix products, arithmetic and copies ran while one was open for 0% -> 0% of each run, Pallas kernels for 1% -> 2%
where the time goes in v2:
time: 136 us; the launch traced here: 135 us
  blocking collectives  57.7 us (42%)
  Pallas kernels  53.5 us (39%)
  waiting for transfers between devices  16 us (12%)
  local copies, waits for them, and re-layouts  3.93 us (3%)
  starting transfers between devices  3.62 us (3%)
    pallas_call x1, Pallas kernels, main_call(): pl.pallas_call(functools.partial(main_kernel, names, cap, extra, count),...  40.8 us
    all_to_all x2, blocking collectives, exchange(): lax.all_to_all(values, axes, split_axis=0, concat_axis=0, axis_index_grou...  34.3 us
    all_to_all x1, blocking collectives, shards(): lax.all_to_all(payload.reshape(count, block, VIS, width), 'pix', split_ax...  23.4 us
    all_to_all x1, waiting for transfers between devices, shards(): lax.all_to_all(back.reshape(count, cap, VIS, width), 'pix', split_axis=0,...  13.4 us
    unnamed x9, local copies, waits for them, and re-layouts  3.93 us
    pallas_call x1, Pallas kernels, prep(): pl.pallas_call(functools.partial(prep_kernel, cap, extra, count), out_sha...  3.63 us
    all_to_all x1, starting transfers between devices, shards(): lax.all_to_all(back.reshape(count, cap, VIS, width), 'pix', split_axis=0,...  3.59 us
  transfers between devices with their start and end apart: 3, of which 2 were waited for; matrix products, arithmetic and copies ran while one was open for 0% of the time, Pallas kernels for 2%

profile of v2, /device:TPU:0, one launch (start us, length us, event | category | flops | bytes accessed | tf_op | source)
XLA Modules:
  0.0 135.4 jit_solution(12592028445326236143)
XLA Ops:
  0.6 1.4 %copy.28.masked_ref = s32[128,24]{1,0:T(8,128)} copy(s32[128,24]{0,1:T(8,128)} %param.18) | data formatting | bytes 24576 | tf_op args[2]
  2.1 3.6 %prep.1 = (bf16[272,8,128]{2,1,0:T(8,128)(2,1)}, f32[8,128]{1,0:T(8,128)}, s32[128]{0:T(128)}, s32[128]{0:T(128)}, s32[128]{0:T(128)}) custom-call(s32[1]{0:T(128)} %bitcast.me_ref, s32[128]{0:T(128)} %dest_ref.1, bf16[3072,128]{1,0:T(8,128)(2,1)} %bitcast.25, s32[1,128]{1,0:T(1,128)} %bitcast.31, s32[128,24]{1,0:T(8,128)} %copy.28.masked_ref, s32[1,128]{1,0:T(1,128)} %bitcast.29), custom_call_target="tpu_custom_call" | custom-call | tf_op jit(solution)/shard_map/prep/pallas_call | solution.py:212
  5.7 23.4 %all_to_all.20 = bf16[8,34,8,128]{3,2,1,0:T(8,128)(2,1)} all-to-all(bf16[8,34,8,128]{3,2,1,0:T(8,128)(2,1)} %bitcast.26), channel_id=1, replica_groups=mesh['pix'=8,'rep'=4] {'pix'}, dimensions={0} | all-to-all | bytes 1114112 | tf_op jit(solution)/shard_map/all_to_all | solution.py:1057
  29.1 40.8 %layers.1 = (f32[128,24,128]{2,1,0:T(8,128)}, bf16[256,8,128]{2,1,0:T(8,128)(2,1)}, bf16[3328,128]{1,0:T(8,128)(2,1)}) custom-call(s32[128]{0:T(128)} %get-tuple-element.30.refs_0_, s32[128]{0:T(128)} %get-tuple-element.31.refs_1_, s32[128]{0:T(128)} %refs_2_.1, bf16[272,8,128]{2,1,0:T(8,128)(2,1)} %bitcast.18, bf16[128,24,128]{2,1,0:T(8,128)(2,1)} %refs_4_.1, ...), custom_call_target="tpu_custom_call" | custom-call | tf_op jit(solution)/shard_map/layers/pallas_call | solution.py:948
  69.9 0.0 collective-permute-start
  69.9 2.6 %collective-permute-done.theirs_ref = bf16[2,16,104,128]{3,2,1,0:T(8,128)(2,1)S(1)} collective-permute-done((bf16[2,16,104,128]{3,2,1,0:T(8,128)(2,1)}, bf16[2,16,104,128]{3,2,1,0:T(8,128)(2,1)S(1)}, u32[]{:S(2)}, u32[]{:S(2)}) %collective-permute-start) | collective-permute-done | bytes 852000 | tf_op jit(solution)/shard_map/ppermute | solution.py:1086
  72.5 0.0 copy-start.2
  72.5 0.9 copy-done.2
  73.4 2.3 %pair_sum.1 = bf16[16,104,128]{2,1,0:T(8,128)(2,1)} custom-call(s32[1]{0:T(128)} %bitcast.12.core_ref, bf16[2,16,104,128]{3,2,1,0:T(8,128)(2,1)} %bitcast.24, bf16[2,16,104,128]{3,2,1,0:T(8,128)(2,1)} %copy-done.2), custom_call_target="tpu_custom_call" | custom-call | tf_op jit(solution)/shard_map/pair_sum/pallas_call | solution.py:1087
  75.7 18.0 %all_to_all.21.parts_ref = bf16[16,104,128]{2,1,0:T(8,128)(2,1)} all-to-all(bf16[16,104,128]{2,1,0:T(8,128)(2,1)} %pair_sum.1), channel_id=1, replica_groups={{0,2,4,6,8,10,12,14,16,18,20,22,24,26,28,30},{1,3,5,7,9,11,13,15,17,19,..., dimensions={0} | all-to-all | bytes 851968 | tf_op jit(solution)/shard_map/all_to_all | solution.py:1081
  93.7 1.8 %chunk_sum.1 = bf16[16,104,128]{2,1,0:T(8,128)(2,1)} custom-call(bf16[16,104,128]{2,1,0:T(8,128)(2,1)} %all_to_all.21.parts_ref), custom_call_target="tpu_custom_call" | custom-call | tf_op jit(solution)/shard_map/chunk_sum/pallas_call | solution.py:1095
  95.5 16.3 %all_to_all.22 = bf16[16,104,128]{2,1,0:T(8,128)(2,1)S(1)} all-to-all(bf16[16,104,128]{2,1,0:T(8,128)(2,1)} %chunk_sum.1), channel_id=1, replica_groups={{0,2,4,6,8,10,12,14,16,18,20,22,24,26,28,30},{1,3,5,7,9,11,13,15,17,19,..., dimensions={0} | all-to-all | bytes 851968 | tf_op jit(solution)/shard_map/all_to_all | solution.py:1081
  111.9 0.0 copy-start.1
  111.9 3.6 %all-to-all-start.1 = ((bf16[8,32,8,128]{3,2,1,0:T(8,128)(2,1)}), bf16[8,32,8,128]{3,2,1,0:T(8,128)(2,1)S(1)}, u32[]{:S(2)}, u32[]{:S(2)}) async-start(bf16[8,32,8,128]{3,2,1,0:T(8,128)(2,1)} %bitcast.9), calls=%async_computation.1 | async-start | bytes 1048576 | tf_op jit(solution)/shard_map/all_to_all | solution.py:1073
  115.4 0.0 collective-permute-start.1
  115.5 13.4 %all-to-all-done.1 = bf16[8,32,8,128]{3,2,1,0:T(8,128)(2,1)S(1)} async-done(((bf16[8,32,8,128]{3,2,1,0:T(8,128)(2,1)}), bf16[8,32,8,128]{3,2,1,0:T(8,128)(2,1)S(1)}, u32[]{:S(2)}, u32[]{:S(2)}) %all-to-all-start.1) | async-done | bytes 524320 | tf_op jit(solution)/shard_map/all_to_all | solution.py:1073
  128.9 0.0 copy-start
  128.9 0.8 copy-done
  129.7 2.6 %restore.1 = f32[3072,128]{1,0:T(8,128)} custom-call(s32[128]{0:T(128)} %get-tuple-element.34.place_ref, f32[8,128]{1,0:T(8,128)} %get-tuple-element.35.pos_ref, bf16[256,8,128]{2,1,0:T(8,128)(2,1)} %bitcast.19), custom_call_target="tpu_custom_call" | custom-call | tf_op jit(solution)/shard_map/restore/pallas_call | solution.py:1120
  132.3 0.0 copy-done.1
  132.3 0.0 collective-permute-done.1.theirs_ref
  132.3 0.0 copy-start.3
  132.3 0.8 copy-done.3
  133.0 2.4 %unpack.1 = (f32[4,128]{1,0:T(4,128)}, f32[4,128]{1,0:T(4,128)}, f32[2,128,384]{2,1,0:T(8,128)}, f32[2,128,128]{2,1,0:T(8,128)}, f32[2,128,512]{2,1,0:T(8,128)},...) custom-call(s32[1]{0:T(128)} %bitcast.12.core_ref, ...), custom_call_target="tpu_custom_call" | custom-call | tf_op jit(solution)/shard_map/unpack/pallas_call | solution.py:1105
Async XLA Ops:
  69.9 2.6 %collective-permute-start = (bf16[2,16,104,128]{3,2,1,0:T(8,128)(2,1)}, bf16[2,16,104,128]{3,2,1,0:T(8,128)(2,1)S(1)}, u32[]{:S(2)}, u32[]{:S(2)}) collective-permute-start(bf16[2,16,104,128]{3,2,1,0:T(8,128)(2,1)} %bitcast.23), channel_id=1, source_target_pairs={{0,1},{1,0},{2,3},{3,2},{4,5},{5,4},{6,7},{7,6},{8,9},{9,8},{10,11... | collective-permute-start | bytes 2555912 | tf_op jit(solution)/shard_map/ppermute | solution.py:1086
  72.5 0.9 copy-start.2
  111.9 20.4 %copy-start.1 = (bf16[16,104,128]{2,1,0:T(8,128)(2,1)}, bf16[16,104,128]{2,1,0:T(8,128)(2,1)S(1)}, u32[]{:S(2)}) copy-start(bf16[16,104,128]{2,1,0:T(8,128)(2,1)S(1)} %all_to_all.22) | copy-start | bytes 1277956
  111.9 17.0 %all-to-all-start.1 = ((bf16[8,32,8,128]{3,2,1,0:T(8,128)(2,1)}), bf16[8,32,8,128]{3,2,1,0:T(8,128)(2,1)S(1)}, u32[]{:S(2)}, u32[]{:S(2)}) async-start(bf16[8,32,8,128]{3,2,1,0:T(8,128)(2,1)} %bitcast.9), calls=%async_computation.1 | async-start | bytes 1048576 | tf_op jit(solution)/shard_map/all_to_all | solution.py:1073
  115.4 16.8 %collective-permute-start.1 = (bf16[1664,128]{1,0:T(8,128)(2,1)S(1)}, bf16[1664,128]{1,0:T(8,128)(2,1)S(1)}, u32[]{:S(2)}, u32[]{:S(2)}) collective-permute-start(bf16[1664,128]{1,0:T(8,128)(2,1)S(1)} %bitcast.20), channel_id=1, source_target_pairs={{0,1},{1,0},{2,3},{3,2},{4,5},{5,4},{6,7},{7,6},{8,9},{9,8},{10,11... | collective-permute-start | bytes 1277960 | tf_op jit(solution)/shard_map/ppermute | solution.py:1104
  128.9 0.8 copy-start
  132.3 0.8 copy-start.3

commit v3 on v2

--- a/solution.py
+++ b/solution.py
@@ -11,7 +11,7 @@
 HEAD_DIM = 16
 FOLD = 4
 BATCH = 16
-PAIRS = 16
+PAIRS = 32
 ENC_ROWS = 512
 VIS = 8
 GROUP = 16
@@ -21,7 +21,7 @@
 NEG = -1e30
 BF = jnp.bfloat16
 F32 = jnp.float32
-VMEM_LIMIT = 56 * 1024 * 1024
+MIB = 1024 * 1024
 
 
 def nn(left, right):
@@ -151,27 +151,28 @@
 
 def prep_kernel(
     cap, extra, count, me_ref, dest_ref, tokens_ref, len_ref, masked_ref, dest_row_ref,
-    payload_ref, pos_ref, place_ref, take_ref, back_ref, tally,
+    payload_ref, pos_ref, take_ref, back_ref, tally,
 ):
-    pixels, slots = masked_ref.shape
+    slots, pixels = masked_ref.shape
     groups = pixels // GROUP
     block = cap + extra
     wide = GROUP * slots
-    len_col = jnp.broadcast_to(len_ref[...].astype(F32), (pixels, pixels)).T
-    dest_col = jnp.broadcast_to(dest_row_ref[...].astype(F32), (pixels, pixels)).T
-    seen = (masked_ref[...] == 0) & (iota((pixels, slots), 1).astype(F32) < len_col[:, :slots])
+    lanes = GROUP * VIS
+    lens = len_ref[...].astype(F32)
+    seen = (masked_ref[...] == 0) & (iota((slots, pixels), 0).astype(F32) < lens)
     seen_low = jnp.where(seen, 1.0, 0.0).astype(BF)
-    earlier = jnp.where(iota((slots, slots), 0) < iota((slots, slots), 1), 1.0, 0.0).astype(BF)
-    member = iota((pixels, slots), 0) % GROUP
-    code = jnp.where(seen, nn(seen_low, earlier) + (member * VIS).astype(F32), -1.0)
+    earlier = jnp.where(iota((slots, slots), 1) < iota((slots, slots), 0), 1.0, 0.0).astype(BF)
+    member = iota((slots, pixels), 1) % GROUP
+    code = jnp.where(seen, nn(earlier, seen_low) + (member * VIS).astype(F32), -1.0)
     spread = jnp.where(iota((slots, wide), 0) == iota((slots, wide), 1) % slots, 1.0, 0.0).astype(BF)
-    code_wide = nn(code.astype(BF), spread)
+    code_wide = tn(code.astype(BF), spread)
     own = iota((pixels, wide), 0) % GROUP == iota((pixels, wide), 1) // slots
     code_row = jnp.sum(jnp.where(own, code_wide, 0.0).reshape(groups, GROUP, wide), axis=1)
-    lanes = GROUP * VIS
-    own_low = iota((pixels, lanes), 0) % GROUP == iota((pixels, lanes), 1) // VIS
-    len_rows = jnp.sum(jnp.where(own_low, len_col, 0.0).reshape(groups, GROUP, lanes), axis=1)
-    dest_rows = jnp.sum(jnp.where(own_low, dest_col, 0.0).reshape(groups, GROUP, lanes), axis=1)
+    in_group = iota((groups, pixels), 1) // GROUP == iota((groups, pixels), 0)
+    fan = iota((pixels, lanes), 0) % GROUP == iota((pixels, lanes), 1) // VIS
+    fan = jnp.where(fan, 1.0, 0.0).astype(BF)
+    len_rows = nn(jnp.where(in_group, lens, 0.0).astype(BF), fan)
+    dest_rows = nn(jnp.where(in_group, dest_row_ref[...].astype(F32), 0.0).astype(BF), fan)
     me = me_ref[0]
     for dev in range(count):
         tally[dev] = 0
@@ -188,9 +189,8 @@
             rank = tally[dest]
             tally[dest] = rank + 1
             sender = lax.rem(2 * me - dest + 2 * count, count)
-            place_ref[series] = dest * cap + rank
             take_ref[series] = sender * block + rank
-            back_ref[series] = sender * cap + rank
+            back_ref[series] = lax.rem(dest - me + count, count) * cap + rank
             payload_ref[dest * block + rank] = rows[member_id].astype(BF)
     pos_rows = jnp.concatenate(found, axis=0)
     pos_ref[...] = pos_rows
@@ -216,15 +216,14 @@
             jax.ShapeDtypeStruct((pixels // GROUP, GROUP * VIS), F32),
             index,
             index,
-            index,
         ),
         in_specs=[smem, smem, vmem, vmem, vmem, vmem],
-        out_specs=(vmem, vmem, smem, smem, smem),
+        out_specs=(vmem, vmem, smem, smem),
         scratch_shapes=[pltpu.SMEM((count,), jnp.int32)],
-        compiler_params=pltpu.CompilerParams(vmem_limit_bytes=VMEM_LIMIT),
+        compiler_params=pltpu.CompilerParams(vmem_limit_bytes=6 * MIB),
         name="prep",
     )(
-        me, route_dev, tokens.reshape(pixels * slots, width), lengths.reshape(1, pixels), masked,
+        me, route_dev, tokens.reshape(pixels * slots, width), lengths.reshape(1, pixels), masked.T,
         route_dev.reshape(1, pixels),
     )
 
@@ -617,7 +616,9 @@
 
         def finish(member):
             value = d.x[self.span(member)] + v.down[self.cut(member)] + w.b_down[1:2]
-            b.dec[b.slot[self.group * GROUP + member]] = jnp.where(self.inside(member), value, 0.0)
+            slot = b.slot[self.group * GROUP + member]
+            b.dec[slot] = jnp.where(self.inside(member), value, 0.0)
+            pltpu.make_async_copy(b.dec.at[slot], b.dec_out.at[slot], b.sems.at[1]).start()
 
         steps += [functools.partial(finish, member) for member in range(GROUP)]
 
@@ -773,19 +774,21 @@
 
 
 IN_NAMES = (
-    "take", "back_at", "slot", "recv", "cot", "w_qkv", "w_out", "w_up", "w_down", "b_up", "b_down", "gain",
-    "bias", "mask", "pos",
+    "core", "take", "back_at", "slot", "recv_in", "cot_in", "w_qkv", "w_out", "w_up", "w_down", "b_up", "b_down",
+    "gain", "bias", "mask", "pos",
 )
-OUT_NAMES = ("dec", "back", "grads")
+OUT_NAMES = ("dec_out", "keep", "send")
 
 
 def small_rows(slots):
     return 18 + 1 + slots
 
 
-def main_kernel(names, cap, extra, count, *refs):
+def main_kernel(names, cap, extra, count, outs, *refs):
     b = Box()
     b.sets = (Box(), Box())
+    b.back_out = refs[len(IN_NAMES) + len(OUT_NAMES) : len(IN_NAMES) + len(OUT_NAMES) + outs]
+    refs = refs[: len(IN_NAMES) + len(OUT_NAMES)] + refs[len(IN_NAMES) + len(OUT_NAMES) + outs :]
     for name, ref in zip(names, refs, strict=True):
         name, _, side = name.partition("@")
         setattr(b.sets[int(side)] if side else b, name, ref)
@@ -798,6 +801,10 @@
     pixels = b.cot.shape[0]
     groups = pixels // GROUP
     block = cap + extra
+    recv_copy = pltpu.make_async_copy(b.recv_in, b.recv, b.sems.at[0])
+    recv_copy.start()
+    cot_copy = pltpu.make_async_copy(b.cot_in, b.cot, b.sems.at[2])
+    cot_copy.start()
     for head in range(HEADS):
         lane = iota((PAD, 128), 1) // HEAD_DIM
         b.masks[head] = jnp.where(lane == head, 1.0, 0.0).astype(BF)
@@ -820,6 +827,7 @@
         )
 
     empty = jnp.zeros((groups, 128), F32)
+    recv_copy.wait()
     pos, lens = lax.fori_loop(0, count, gather, (empty, empty))
     for group in range(groups):
         where = pl.ds(group * 128, 128)
@@ -831,10 +839,16 @@
     weave(encoders[0].attend())
     for now, later in zip(encoders, encoders[1:]):
         weave(now.bend(), later.attend())
+    cot_copy.wait()
     decoder_all(b, groups, encoders[-1].bend(), encoders[0].feed())
     for now, later in zip(encoders, encoders[1:]):
         weave(now.retreat(), later.feed())
     weave(encoders[-1].retreat())
+    copies = []
+    size = b.back.shape[0] // outs
+    for index, ref in enumerate(b.back_out):
+        copies.append(pltpu.make_async_copy(b.back.at[pl.ds(index * size, size)], ref, b.sems.at[5 + index]))
+        copies[-1].start()
 
     offset = 0
     for layer in range(2):
@@ -864,6 +878,15 @@
     fill = -tail.shape[0] % 16
     tail = jnp.concatenate([tail, jnp.zeros((fill, 128), F32)], axis=0)
     b.grads[offset : offset + tail.shape[0]] = tail.astype(BF)
+    half = b.grads.shape[0] // 2
+    mine = b.core[0]
+    for side, ref, sem in ((mine, b.keep, 3), (1 - mine, b.send, 4)):
+        rows = pl.ds(pl.multiple_of(side * half, half), half)
+        copies.append(pltpu.make_async_copy(b.grads.at[rows], ref, b.sems.at[sem]))
+        copies[-1].start()
+    for copy in copies:
+        copy.wait()
+    pltpu.make_async_copy(b.dec, b.dec_out, b.sems.at[1]).wait()
 
 
 def decoder_scratch(rows, slots):
@@ -894,14 +917,20 @@
     }
 
 
-def main_call(args, cap, extra, count, grad_rows):
-    recv, cot = args[3], args[4]
+def main_call(args, cap, extra, count, grad_rows, outs):
+    recv, cot = args[4], args[5]
     pixels, slots, width = cot.shape
     enc = pixels * VIS
     rows = GROUP * slots
     smem = pl.BlockSpec(memory_space=pltpu.SMEM)
     vmem = pl.BlockSpec(memory_space=pltpu.VMEM)
+    anywhere = pl.BlockSpec(memory_space=pl.ANY)
     scratch = {
+        "recv": (recv.shape, BF),
+        "cot": (cot.shape, BF),
+        "dec": (cot.shape, F32),
+        "back": ((count * cap, VIS, width), BF),
+        "grads": ((grad_rows, 128), BF),
         "masks": ((HEADS, PAD, 128), BF),
         "masks_half": ((FOLD, PAD, 128), BF),
         "qkv_t": ((2, 384, 128), BF),
@@ -944,43 +973,57 @@
     for side in range(2):
         for name, entry in decoder_scratch(rows, slots).items():
             scratch[f"{name}@{side}"] = entry
-    names = IN_NAMES + OUT_NAMES + tuple(scratch)
+    names = IN_NAMES + OUT_NAMES + tuple(scratch) + ("sems",)
+    half = jax.ShapeDtypeStruct((grad_rows // 2, 128), BF)
     return pl.pallas_call(
-        functools.partial(main_kernel, names, cap, extra, count),
-        out_shape=(
-            jax.ShapeDtypeStruct((pixels, slots, width), F32),
-            jax.ShapeDtypeStruct((count * cap, VIS, width), BF),
-            jax.ShapeDtypeStruct((grad_rows, 128), BF),
-        ),
-        in_specs=[smem] * 3 + [vmem] * (len(IN_NAMES) - 3),
-        out_specs=(vmem, vmem, vmem),
-        scratch_shapes=[pltpu.VMEM(shape, kind) for shape, kind in scratch.values()],
-        compiler_params=pltpu.CompilerParams(vmem_limit_bytes=VMEM_LIMIT),
+        functools.partial(main_kernel, names, cap, extra, count, outs),
+        out_shape=(jax.ShapeDtypeStruct((pixels, slots, width), F32), half, half)
+        + (jax.ShapeDtypeStruct((count * cap // outs, VIS, width), BF),) * outs,
+        in_specs=[smem] * 4 + [anywhere] * 2 + [vmem] * (len(IN_NAMES) - 6),
+        out_specs=(anywhere,) * (3 + outs),
+        scratch_shapes=[pltpu.VMEM(shape, kind) for shape, kind in scratch.values()]
+        + [pltpu.SemaphoreType.DMA((5 + outs,))],
+        compiler_params=pltpu.CompilerParams(vmem_limit_bytes=32 * MIB),
         name="layers",
     )(*args)
 
 
-def pair_sum_kernel(core_ref, mine_ref, theirs_ref, out_ref):
+def fetch(pairs, sems):
+    copies = [pltpu.make_async_copy(src, dst, sems.at[index]) for index, (src, dst) in enumerate(pairs)]
+    for copy in copies:
+        copy.start()
+    return copies
+
+
+def pair_sum_kernel(mine_ref, theirs_ref, out_ref, mine, theirs, sems):
+    for copy in fetch([(mine_ref, mine), (theirs_ref, theirs)], sems):
+        copy.wait()
+    out_ref[...] = (mine[...].astype(F32) + theirs[...].astype(F32)).astype(BF)
+
+
+def chunk_sum_kernel(parts_ref, out_ref, parts, low, sems):
+    count = parts_ref.shape[0]
+    (copy,) = fetch([(parts_ref, parts)], sems)
+    copy.wait()
+    total = parts[0].astype(F32)
+    for part in range(1, count):
+        total = total + parts[part].astype(F32)
+    low[...] = total.astype(BF)
+    for copy in fetch([(low, out_ref.at[part]) for part in range(count)], sems):
+        copy.wait()
+
+
+BIG = ("qkv", "out", "up", "down")
+
+
+def unpack_kernel(slots, *refs):
+    (core_ref, mine_ref, theirs_ref, gain_ref, bias_ref, b_up_ref, b_down_ref, mask_ref, pos_ref) = refs[:9]
+    outs = dict(zip(BIG, refs[9:13]))
+    held = dict(zip(BIG, refs[13:17]))
+    full, sems = refs[17:]
     core = core_ref[0]
-    out_ref[...] = (mine_ref[core].astype(F32) + theirs_ref[core].astype(F32)).astype(BF)
-
-
-def chunk_sum_kernel(parts_ref, out_ref):
-    total = parts_ref[0].astype(F32)
-    for part in range(1, parts_ref.shape[0]):
-        total = total + parts_ref[part].astype(F32)
-    low = total.astype(BF)
-    for part in range(parts_ref.shape[0]):
-        out_ref[part] = low
-
-
-def unpack_kernel(
-    slots, core_ref, mine_ref, theirs_ref, gain_ref, bias_ref, qkv_ref, out_ref, up_ref, b_up_ref, down_ref,
-    b_down_ref, mask_ref, pos_ref, full,
-):
-    core = core_ref[0]
-    full[core] = mine_ref[...]
-    full[1 - core] = theirs_ref[...]
+    for copy in fetch([(mine_ref, full.at[core]), (theirs_ref, full.at[1 - core])], sems):
+        copy.wait()
     half = full.shape[1]
 
     def rows(start, size):
@@ -993,18 +1036,29 @@
         )
 
     offset = 0
+    copies = []
+
+    def leave(name, layer):
+        copy = pltpu.make_async_copy(held[name].at[layer], outs[name].at[layer], sems.at[2 + len(copies)])
+        copy.start()
+        copies.append(copy)
+
     for layer in range(2):
         for start in range(0, 384, 128):
-            qkv_ref[layer, :, start : start + 128] = rows(offset, 128)
+            held["qkv"][layer, :, start : start + 128] = rows(offset, 128)
             offset += 128
-        out_ref[layer] = rows(offset, 128)
+        leave("qkv", layer)
+        held["out"][layer] = rows(offset, 128)
         offset += 128
+        leave("out", layer)
         for start in range(0, 512, 128):
-            up_ref[layer, :, start : start + 128] = rows(offset, 128)
+            held["up"][layer, :, start : start + 128] = rows(offset, 128)
             offset += 128
+        leave("up", layer)
         for start in range(0, 512, 128):
-            down_ref[layer, start : start + 128, :] = rows(offset, 128)
+            held["down"][layer, start : start + 128, :] = rows(offset, 128)
             offset += 128
+        leave("down", layer)
     count = small_rows(slots)
     small = rows(offset, count + (-count % 16))
     gain_ref[...] = small[0:4]
@@ -1016,21 +1070,31 @@
     b_down_ref[...] = small[16:18]
     mask_ref[...] = small[18:19]
     pos_ref[...] = small[19 : 19 + slots]
-
-
-def restore_kernel(place_ref, pos_ref, rows_ref, out_ref, held):
+    for copy in copies:
+        copy.wait()
+
+
+def restore_kernel(cap, count, place_ref, pos_ref, *refs):
+    blocks, (out_ref, rows, held, out, sems) = refs[:count], refs[count:]
+    size = rows.shape[0] // count
+    copies = fetch([(ref, rows.at[pl.ds(index * size, size)]) for index, ref in enumerate(blocks)], sems)
     groups = pos_ref.shape[0]
-    wide = out_ref.shape[0] // groups
+    wide = out.shape[0] // groups
     slots = wide // GROUP
     lane = iota((1, 128), 1)
+    for copy in copies:
+        copy.wait()
     for group in range(groups):
         for member in range(GROUP):
-            block = rows_ref[place_ref[group * GROUP + member]]
-            held[pl.ds(member * VIS, VIS)] = block.astype(F32)
+            block = rows[place_ref[group * GROUP + member]]
+            held[pl.ds((group % 2) * 128 + member * VIS, VIS)] = block.astype(F32)
         pos_row = pos_ref[group : group + 1]
         target = jnp.where(pos_row > 0, (lane // VIS * slots).astype(F32) + pos_row - 1.0, -1.0)
         hot = jnp.where(iota((wide, 128), 0).astype(F32) == target, 1.0, 0.0).astype(BF)
-        out_ref[group * wide : (group + 1) * wide, :] = nn(hot, held[...].astype(BF))
+        where = pl.ds(group * wide, wide)
+        out[where] = nn(hot, held[pl.ds((group % 2) * 128, 128)].astype(BF))
+        pltpu.make_async_copy(out.at[where], out_ref.at[where], sems.at[count]).start()
+    pltpu.make_async_copy(out, out_ref, sems.at[count]).wait()
 
 
 def shards(
@@ -1045,14 +1109,12 @@
     extra = 2
     smem = pl.BlockSpec(memory_space=pltpu.SMEM)
     vmem = pl.BlockSpec(memory_space=pltpu.VMEM)
-    params = pltpu.CompilerParams(vmem_limit_bytes=VMEM_LIMIT)
+    anywhere = pl.BlockSpec(memory_space=pl.ANY)
     pix = lax.axis_index("pix")
     me = pix.reshape(1).astype(jnp.int32)
     flat = pix * reps + lax.axis_index("rep")
     core = (flat % 2).reshape(1).astype(jnp.int32)
-    payload, pos_rows, place, take, back_at = prep(
-        tokens, lengths, masked, route_dev, count, cap, extra, me
-    )
+    payload, pos_rows, take, back_at = prep(tokens, lengths, masked, route_dev, count, cap, extra, me)
     block = cap + extra
     recv = lax.all_to_all(
         payload.reshape(count, block, VIS, width), "pix", split_axis=0, concat_axis=0, tiled=True
@@ -1060,19 +1122,18 @@
     chunk = -(-(3072 + small_rows(slots)) // devices)
     chunk += -chunk % 8
     half = devices // 2
-    dec, back, grads = main_call(
+    direct = count <= 8
+    dec, keep, send, *back = main_call(
         (
-            take, back_at, route_slot, recv, cotangent, w_qkv, w_out, w_up, w_down, b_up, b_down,
+            core, take, back_at, route_slot, recv, cotangent, w_qkv, w_out, w_up, w_down, b_up, b_down,
             norm_gain.reshape(4, width), norm_bias.reshape(4, width), mask_token.reshape(1, width), pos_table,
         ),
         cap,
         extra,
         count,
         devices * chunk,
+        count if direct else 1,
     )
-    returned = lax.all_to_all(
-        back.reshape(count, cap, VIS, width), "pix", split_axis=0, concat_axis=0, tiled=True
-    ).reshape(count * cap, VIS, width)
     axes = ("pix", "rep")
     swap = [(i, i ^ 1) for i in range(devices)]
     groups = [[2 * i + side for i in range(half)] for side in range(2)]
@@ -1082,50 +1143,66 @@
             values, axes, split_axis=0, concat_axis=0, axis_index_groups=groups, tiled=True
         )
 
-    grads = grads.reshape(2, half, chunk, 128)
-    theirs = lax.ppermute(grads, axes, swap)
+    theirs = lax.ppermute(send, axes, swap)
+    piece = jax.ShapeDtypeStruct((half, chunk, 128), BF)
+    line = pltpu.VMEM((half, chunk, 128), BF)
     paired = pl.pallas_call(
         pair_sum_kernel,
-        out_shape=jax.ShapeDtypeStruct((half, chunk, 128), BF),
-        in_specs=[smem, vmem, vmem],
+        out_shape=piece,
+        in_specs=[anywhere, anywhere],
         out_specs=vmem,
-        compiler_params=params,
+        scratch_shapes=[line, line, pltpu.SemaphoreType.DMA((2,))],
+        compiler_params=pltpu.CompilerParams(vmem_limit_bytes=4 * MIB),
         name="pair_sum",
-    )(core, grads, theirs)
+    )(keep.reshape(half, chunk, 128), theirs.reshape(half, chunk, 128))
+    if direct:
+        returned = back[:1]
+        for step in range(1, count):
+            returned.append(lax.ppermute(back[step], "pix", [(i, (i - step) % count) for i in range(count)]))
+    else:
+        turn = (pix - jnp.arange(count)) % count
+        blocks = lax.all_to_all(
+            back[0].reshape(count, cap, VIS, width)[turn], "pix", split_axis=0, concat_axis=0, tiled=True
+        )
+        returned = [blocks[(pix + jnp.arange(count)) % count].reshape(count * cap, VIS, width)]
     spread = pl.pallas_call(
         chunk_sum_kernel,
-        out_shape=jax.ShapeDtypeStruct((half, chunk, 128), BF),
-        in_specs=[vmem],
-        out_specs=vmem,
-        compiler_params=params,
+        out_shape=piece,
+        in_specs=[anywhere],
+        out_specs=anywhere,
+        scratch_shapes=[line, pltpu.VMEM((chunk, 128), BF), pltpu.SemaphoreType.DMA((half,))],
+        compiler_params=pltpu.CompilerParams(vmem_limit_bytes=4 * MIB),
         name="chunk_sum",
     )(exchange(paired))
+    spread, *returned = lax.optimization_barrier((spread, *returned))
     summed = exchange(spread).reshape(half * chunk, 128)
     other = lax.ppermute(summed, axes, swap)
-    gain, bias, qkv, out, up, bup, down, bdown, mask, pos = pl.pallas_call(
+    small = ((4, width), (4, width), b_up.shape, b_down.shape, (1, width), pos_table.shape)
+    large = tuple(w.shape for w in (w_qkv, w_out, w_up, w_down))
+    gain, bias, bup, bdown, mask, pos, qkv, out, up, down = pl.pallas_call(
         functools.partial(unpack_kernel, slots),
-        out_shape=tuple(
-            jax.ShapeDtypeStruct(shape, F32)
-            for shape in (
-                (4, width), (4, width), w_qkv.shape, w_out.shape, w_up.shape, b_up.shape, w_down.shape,
-                b_down.shape, (1, width), pos_table.shape,
-            )
-        ),
-        in_specs=[smem, vmem, vmem],
-        out_specs=(vmem,) * 10,
-        scratch_shapes=[pltpu.VMEM((2, half * chunk, 128), BF)],
-        compiler_params=params,
+        out_shape=tuple(jax.ShapeDtypeStruct(shape, F32) for shape in small + large),
+        in_specs=[smem, anywhere, anywhere],
+        out_specs=(vmem,) * 6 + (anywhere,) * 4,
+        scratch_shapes=[pltpu.VMEM(shape, F32) for shape in large]
+        + [pltpu.VMEM((2, half * chunk, 128), BF), pltpu.SemaphoreType.DMA((10,))],
+        compiler_params=pltpu.CompilerParams(vmem_limit_bytes=8 * MIB),
         name="unpack",
     )(core, summed, other)
     grad_tokens = pl.pallas_call(
-        restore_kernel,
+        functools.partial(restore_kernel, cap, len(returned)),
         out_shape=jax.ShapeDtypeStruct((pixels * slots, width), F32),
-        in_specs=[smem, vmem, vmem],
-        out_specs=vmem,
-        scratch_shapes=[pltpu.VMEM((GROUP * VIS, width), F32)],
-        compiler_params=params,
+        in_specs=[smem, vmem] + [anywhere] * len(returned),
+        out_specs=anywhere,
+        scratch_shapes=[
+            pltpu.VMEM((count * cap, VIS, width), BF),
+            pltpu.VMEM((2 * GROUP * VIS, width), F32),
+            pltpu.VMEM((pixels * slots, width), F32),
+            pltpu.SemaphoreType.DMA((len(returned) + 1,)),
+        ],
+        compiler_params=pltpu.CompilerParams(vmem_limit_bytes=8 * MIB),
         name="restore",
-    )(place, pos_rows, returned)
+    )(back_at, pos_rows, *returned)
     return (
         dec,
         grad_tokens.reshape(pixels, slots, width),

time: 136 us -> 123 us (0.904)
  blocking collectives: 57.7 us -> 15 us
  starting transfers between devices: 3.62 us -> 31.9 us
  waiting for transfers between devices: 16 us -> 20.8 us
  Pallas kernels: 53.5 us -> 50.3 us
    all_to_all x1 -> x0, blocking collectives: 23.4 us -> none  [shards(): lax.all_to_all(payload.reshape(count, block, VIS, width), 'pix', split_ax...]
    ppermute x1 -> x8, starting transfers between devices: 0.01 us -> 19.9 us  [the longest x7 19.9 us: shards(): lax.ppermute(back[step], 'pix', [(i, (i - step) % count) for i in range(c...]
    all_to_all x2 -> x1, blocking collectives: 34.3 us -> 15 us  [exchange(): lax.all_to_all(values, axes, split_axis=0, concat_axis=0, axis_index_grou...]
    all_to_all x1 -> x2, starting transfers between devices: 3.59 us -> 12 us  [the longest x1 7.26 us: shards(): lax.all_to_all(payload.reshape(count, block, VIS, width), 'pix', split_ax...]
    ppermute x1 -> x8, waiting for transfers between devices: 2.57 us -> 5.61 us  [the longest x7 3.85 us: shards(): lax.ppermute(back[step], 'pix', [(i, (i - step) % count) for i in range(c...]
    pallas_call x4, Pallas kernels: 47.5 us -> 44.9 us  [the longest x1 39.9 us: main_call(): pl.pallas_call(functools.partial(main_kernel, names, cap, extra, count, o...]
    all_to_all x1 -> x2, waiting for transfers between devices: 13.4 us -> 15.2 us  [the longest x1 15.2 us: shards(): lax.all_to_all(payload.reshape(count, block, VIS, width), 'pix', split_ax...]
    unnamed x9 -> x32, local copies, waits for them, and re-layouts: 3.93 us -> 3.26 us
  transfers between devices with their start and end apart: 3 -> 11, of which waited for: 2 -> 6; matrix products, arithmetic and copies ran while one was open for 0% -> 0% of each run, Pallas kernels for 2% -> 3%
where the time goes in v3:
time: 123 us; the launch traced here: 122 us
  Pallas kernels  50.3 us (41%)
  starting transfers between devices  31.9 us (26%)
  waiting for transfers between devices  20.8 us (17%)
  blocking collectives  15 us (12%)
  local copies, waits for them, and re-layouts  3.26 us (3%)
    pallas_call x1, Pallas kernels, main_call(): pl.pallas_call(functools.partial(main_kernel, names, cap, extra, count, o...  39.9 us
    ppermute x7, starting transfers between devices, shards(): lax.ppermute(back[step], 'pix', [(i, (i - step) % count) for i in range(c...  19.9 us
    all_to_all x1, waiting for transfers between devices, shards(): lax.all_to_all(payload.reshape(count, block, VIS, width), 'pix', split_ax...  15.2 us
    all_to_all x1, blocking collectives, exchange(): lax.all_to_all(values, axes, split_axis=0, concat_axis=0, axis_index_grou...  15 us
    all_to_all x1, starting transfers between devices, shards(): lax.all_to_all(payload.reshape(count, block, VIS, width), 'pix', split_ax...  7.26 us
    all_to_all x1, starting transfers between devices, exchange(): lax.all_to_all(values, axes, split_axis=0, concat_axis=0, axis_index_grou...  4.71 us
    ppermute x7, waiting for transfers between devices, shards(): lax.ppermute(back[step], 'pix', [(i, (i - step) % count) for i in range(c...  3.85 us
    unnamed x32, local copies, waits for them, and re-layouts  3.26 us
  transfers between devices with their start and end apart: 11, of which 6 were waited for; matrix products, arithmetic and copies ran while one was open for 0% of the time, Pallas kernels for 3%

profile of v3, /device:TPU:0, one launch (start us, length us, event | category | flops | bytes accessed | tf_op | source)
XLA Modules:
  0.0 122.4 jit_solution(11769305445559866873)
XLA Ops:
  0.7 0.0 copy-start
  0.7 0.0 copy-start.1
  0.7 1.2 copy-done.1
  1.9 0.7 copy-done.7
  2.6 0.7 copy-done.11
  3.2 0.7 copy-done.13
  3.9 0.0 copy-start.6
  3.9 0.0 copy-start.8
  3.9 0.0 copy-start.9
  3.9 0.0 copy-start.10
  4.0 3.1 %prep.1 = (bf16[272,8,128]{2,1,0:T(8,128)(2,1)}, f32[8,128]{1,0:T(8,128)S(1)}, s32[128]{0:T(128)S(1)}, s32[128]{0:T(128)S(1)}) custom-call(s32[1]{0:T(128)} %bitcast.1.me_ref, s32[128]{0:T(128)S(1)} %copy-done.11, bf16[3072,128]{1,0:T(8,128)(2,1)S(1)} %bitcast.21, s32[1,128]{1,0:T(1,128)S(1)} %bitcast.28, s32[24,128]{1,0:T(8,128)S(1)} %bitcast.24, ...), custom_call_target="tpu_custom_call" | custom-call | tf_op jit(solution)/shard_map/prep/pallas_call | solution.py:212
  7.1 7.3 %all-to-all-start = ((bf16[8,34,8,128]{3,2,1,0:T(8,128)(2,1)}), bf16[8,34,8,128]{3,2,1,0:T(8,128)(2,1)S(1)}, u32[]{:S(2)}, u32[]{:S(2)}) async-start(bf16[8,34,8,128]{3,2,1,0:T(8,128)(2,1)} %bitcast.6), calls=%async_computation | async-start | bytes 1114112 | tf_op jit(solution)/shard_map/all_to_all | solution.py:1119
  14.4 15.2 %all-to-all-done = bf16[8,34,8,128]{3,2,1,0:T(8,128)(2,1)S(1)} async-done(((bf16[8,34,8,128]{3,2,1,0:T(8,128)(2,1)}), bf16[8,34,8,128]{3,2,1,0:T(8,128)(2,1)S(1)}, u32[]{:S(2)}, u32[]{:S(2)}) %all-to-all-start) | async-done | bytes 557088 | tf_op jit(solution)/shard_map/all_to_all | solution.py:1119
  29.6 0.0 copy-done.4
  29.6 0.0 copy-done.5
  29.6 0.0 copy-done.6
  29.6 0.0 copy-done.8
  29.6 0.0 copy-done.9
  29.6 0.0 copy-done.10
  29.6 0.0 copy-done.12
  29.6 0.0 copy-done.14
  29.6 0.0 copy-done.15
  29.6 39.9 %layers.1 = (f32[128,24,128]{2,1,0:T(8,128)}, bf16[1664,128]{1,0:T(8,128)(2,1)S(1)}, bf16[1664,128]{1,0:T(8,128)(2,1)S(1)}, bf16[32,8,128]{2,1,0:T(8,128)(2,1)S(...) custom-call(s32[1]{0:T(128)} %bitcast.refs_0_, ...), custom_call_target="tpu_custom_call" | custom-call | tf_op jit(solution)/shard_map/layers/pallas_call | solution.py:978
  69.6 0.1 collective-permute-start
  69.7 1.8 %collective-permute-done = bf16[1664,128]{1,0:T(8,128)(2,1)S(1)} collective-permute-done((bf16[1664,128]{1,0:T(8,128)(2,1)S(1)}, bf16[1664,128]{1,0:T(8,128)(2,1)S(1)}, u32[]{:S(2)}, u32[]{:S(2)}) %collective-permute-start) | collective-permute-done | bytes 426016 | tf_op jit(solution)/shard_map/ppermute | solution.py:1146
  71.4 1.3 %pair_sum.1 = bf16[16,104,128]{2,1,0:T(8,128)(2,1)} custom-call(bf16[16,104,128]{2,1,0:T(8,128)(2,1)S(1)} %bitcast.22, bf16[16,104,128]{2,1,0:T(8,128)(2,1)S(1)} %bitcast.23), custom_call_target="tpu_custom_call" | custom-call | tf_op jit(solution)/shard_map/pair_sum/pallas_call | solution.py:1149
  72.7 4.7 %all-to-all-start.1 = ((bf16[16,104,128]{2,1,0:T(8,128)(2,1)}), bf16[16,104,128]{2,1,0:T(8,128)(2,1)S(1)}, u32[]{:S(2)}, u32[]{:S(2)}) async-start(bf16[16,104,128]{2,1,0:T(8,128)(2,1)} %pair_sum.1), calls=%async_computation.1 | async-start | bytes 851968 | tf_op jit(solution)/shard_map/all_to_all | solution.py:1142
  77.5 4.6 %collective-permute-start.1 = (bf16[32,8,128]{2,1,0:T(8,128)(2,1)S(1)}, bf16[32,8,128]{2,1,0:T(8,128)(2,1)S(1)}, u32[]{:S(2)}, u32[]{:S(2)}) collective-permute-start(bf16[32,8,128]{2,1,0:T(8,128)(2,1)S(1)} %get-tuple-element.54), channel_id=1, source_target_pairs={{0,28},{4,0},{8,4},{12,8},{16,12},{20,16},{24,20},{28,24},{1,29},{... | collective-permute-start | bytes 196616 | tf_op jit(solution)/shard_map/ppermute | solution.py:1161
  82.1 0.6 collective-permute-start.2
  82.7 0.0 collective-permute-start.3
  82.7 2.9 %collective-permute-start.4 = (bf16[32,8,128]{2,1,0:T(8,128)(2,1)S(1)}, bf16[32,8,128]{2,1,0:T(8,128)(2,1)S(1)}, u32[]{:S(2)}, u32[]{:S(2)}) collective-permute-start(bf16[32,8,128]{2,1,0:T(8,128)(2,1)S(1)} %get-tuple-element.57), channel_id=1, source_target_pairs={{0,16},{4,20},{8,24},{12,28},{16,0},{20,4},{24,8},{28,12},{1,17},{... | collective-permute-start | bytes 196616 | tf_op jit(solution)/shard_map/ppermute | solution.py:1161
  85.6 0.0 collective-permute-start.5
  85.6 1.3 %collective-permute-done.1.refs_1_ = bf16[32,8,128]{2,1,0:T(8,128)(2,1)S(1)} collective-permute-done((bf16[32,8,128]{2,1,0:T(8,128)(2,1)S(1)}, bf16[32,8,128]{2,1,0:T(8,128)(2,1)S(1)}, u32[]{:S(2)}, u32[]{:S(2)}) %collective-permute-start.1) | collective-permute-done | bytes 65568 | tf_op jit(solution)/shard_map/ppermute | solution.py:1161
  86.9 1.1 collective-permute-start.6
  88.0 1.5 %collective-permute-done.2.refs_2_ = bf16[32,8,128]{2,1,0:T(8,128)(2,1)S(1)} collective-permute-done((bf16[32,8,128]{2,1,0:T(8,128)(2,1)S(1)}, bf16[32,8,128]{2,1,0:T(8,128)(2,1)S(1)}, u32[]{:S(2)}, u32[]{:S(2)}) %collective-permute-start.2) | collective-permute-done | bytes 65568 | tf_op jit(solution)/shard_map/ppermute | solution.py:1161
  89.4 10.7 %collective-permute-start.7 = (bf16[32,8,128]{2,1,0:T(8,128)(2,1)S(1)}, bf16[32,8,128]{2,1,0:T(8,128)(2,1)S(1)}, u32[]{:S(2)}, u32[]{:S(2)}) collective-permute-start(bf16[32,8,128]{2,1,0:T(8,128)(2,1)S(1)} %get-tuple-element.60), channel_id=1, source_target_pairs={{0,4},{4,8},{8,12},{12,16},{16,20},{20,24},{24,28},{28,0},{1,5},{5... | collective-permute-start | bytes 196616 | tf_op jit(solution)/shard_map/ppermute | solution.py:1161
  100.1 0.0 all-to-all-done.1.parts_ref
  100.1 1.0 chunk_sum.1
  101.1 0.0 collective-permute-done.3.refs_3_
  101.1 0.2 collective-permute-done.4.refs_4_
  101.3 0.9 collective-permute-done.5.refs_5_
  102.2 0.0 collective-permute-done.6.refs_6_
  102.2 0.0 collective-permute-done.7.refs_7_
  102.2 15.0 %all_to_all.15 = bf16[16,104,128]{2,1,0:T(8,128)(2,1)S(1)} all-to-all(bf16[16,104,128]{2,1,0:T(8,128)(2,1)S(1)} %chunk_sum.1), channel_id=1, replica_groups={{0,2,4,6,8,10,12,14,16,18,20,22,24,26,28,30},{1,3,5,7,9,11,13,15,17,19,..., dimensions={0} | all-to-all | bytes 851968 | tf_op jit(solution)/shard_map/all_to_all | solution.py:1142
  117.2 0.0 collective-permute-start.8
  117.2 2.6 %restore.1 = f32[3072,128]{1,0:T(8,128)} custom-call(s32[128]{0:T(128)S(1)} %get-tuple-element.47.refs_2_.place_ref, f32[8,128]{1,0:T(8,128)S(1)} %get-tuple-element.50.pos_ref, bf16[32,8,128]{2,1,0:T(8,128)(2,1)S(1)} %get-tuple-element.61.refs_0_, bf16[32,8,128]{2,1,0:T(8,128)(2,1)S(1)} %collective-permute-done.1.refs_1_, ...), custom_call_target="tpu_custom_call" | custom-call | tf_op jit(solution)/shard_map/restore/pallas_call | solution.py:1192
  119.9 0.0 collective-permute-done.8.refs_2_
  119.9 2.3 %unpack.1 = (f32[4,128]{1,0:T(4,128)}, f32[4,128]{1,0:T(4,128)}, f32[2,512]{1,0:T(2,128)}, f32[2,128]{1,0:T(2,128)}, f32[1,128]{1,0:T(1,128)}, /*index=5*/f32[24...) custom-call(s32[1]{0:T(128)} %bitcast.refs_0_, ...), custom_call_target="tpu_custom_call" | custom-call | tf_op jit(solution)/shard_map/unpack/pallas_call | solution.py:1182
  (13 shorter events, 0.0 us)
Async XLA Ops:
  0.7 28.9 %copy-start = (bf16[128,24,128]{2,1,0:T(8,128)(2,1)S(1)}, bf16[128,24,128]{2,1,0:T(8,128)(2,1)}, u32[]{:S(2)}) copy-start(bf16[128,24,128]{2,1,0:T(8,128)(2,1)} %refs_5_.1) | copy-start | bytes 2359300
  0.7 1.2 copy-start.1
  1.9 0.7 copy-start.7
  2.6 0.7 copy-start.11
  3.2 0.7 copy-start.13
  3.9 25.7 %copy-start.2 = (bf16[2,128,512]{2,1,0:T(8,128)(2,1)S(1)}, bf16[2,128,512]{2,1,0:T(8,128)(2,1)}, u32[]{:S(2)}) copy-start(bf16[2,128,512]{2,1,0:T(8,128)(2,1)} %refs_8_.1) | copy-start | bytes 786436
  3.9 25.7 %copy-start.3 = (bf16[2,512,128]{2,1,0:T(8,128)(2,1)S(1)}, bf16[2,512,128]{2,1,0:T(8,128)(2,1)}, u32[]{:S(2)}) copy-start(bf16[2,512,128]{2,1,0:T(8,128)(2,1)} %refs_9_.1) | copy-start | bytes 786436
  3.9 25.7 %copy-start.4 = (bf16[2,128,384]{2,1,0:T(8,128)(2,1)S(1)}, bf16[2,128,384]{2,1,0:T(8,128)(2,1)}, u32[]{:S(2)}) copy-start(bf16[2,128,384]{2,1,0:T(8,128)(2,1)} %refs_6_.1) | copy-start | bytes 589828
  3.9 25.7 %copy-start.5 = (bf16[2,128,128]{2,1,0:T(8,128)(2,1)S(1)}, bf16[2,128,128]{2,1,0:T(8,128)(2,1)}, u32[]{:S(2)}) copy-start(bf16[2,128,128]{2,1,0:T(8,128)(2,1)} %refs_7_.1) | copy-start | bytes 196612
  3.9 25.7 %copy-start.6 = (f32[24,128]{1,0:T(8,128)S(1)}, f32[24,128]{1,0:T(8,128)}, u32[]{:S(2)}) copy-start(f32[24,128]{1,0:T(8,128)} %refs_15_.1) | copy-start | bytes 36868
  3.9 25.7 %copy-start.8 = (f32[2,512]{1,0:T(2,128)S(1)}, f32[2,512]{1,0:T(2,128)}, u32[]{:S(2)}) copy-start(f32[2,512]{1,0:T(2,128)} %refs_10_.1) | copy-start | bytes 12292
  3.9 25.7 %copy-start.9 = (f32[2,2,128]{2,1,0:T(2,128)S(1)}, f32[2,2,128]{2,1,0:T(2,128)}, u32[]{:S(2)}) copy-start(f32[2,2,128]{2,1,0:T(2,128)} %param.21) | copy-start | bytes 6148
  3.9 25.7 %copy-start.10 = (f32[2,2,128]{2,1,0:T(2,128)S(1)}, f32[2,2,128]{2,1,0:T(2,128)}, u32[]{:S(2)}) copy-start(f32[2,2,128]{2,1,0:T(2,128)} %param.22) | copy-start | bytes 6148
  3.9 25.7 %copy-start.12 = (f32[2,128]{1,0:T(2,128)S(1)}, f32[2,128]{1,0:T(2,128)}, u32[]{:S(2)}) copy-start(f32[2,128]{1,0:T(2,128)} %refs_11_.1) | copy-start | bytes 3076
  4.0 25.7 %copy-start.14 = (s32[128]{0:T(128)S(1)}, s32[128]{0:T(128)}, u32[]{:S(2)}) copy-start(s32[128]{0:T(128)} %refs_3_.1) | copy-start | bytes 1540
  4.0 25.7 %copy-start.15 = (f32[128]{0:T(128)S(1)}, f32[128]{0:T(128)}, u32[]{:S(2)}) copy-start(f32[128]{0:T(128)} %param.29) | copy-start | bytes 1540
  7.1 22.5 %all-to-all-start = ((bf16[8,34,8,128]{3,2,1,0:T(8,128)(2,1)}), bf16[8,34,8,128]{3,2,1,0:T(8,128)(2,1)S(1)}, u32[]{:S(2)}, u32[]{:S(2)}) async-start(bf16[8,34,8,128]{3,2,1,0:T(8,128)(2,1)} %bitcast.6), calls=%async_computation | async-start | bytes 1114112 | tf_op jit(solution)/shard_map/all_to_all | solution.py:1119
  69.6 1.8 %collective-permute-start = (bf16[1664,128]{1,0:T(8,128)(2,1)S(1)}, bf16[1664,128]{1,0:T(8,128)(2,1)S(1)}, u32[]{:S(2)}, u32[]{:S(2)}) collective-permute-start(bf16[1664,128]{1,0:T(8,128)(2,1)S(1)} %get-tuple-element.52), channel_id=1, source_target_pairs={{0,1},{1,0},{2,3},{3,2},{4,5},{5,4},{6,7},{7,6},{8,9},{9,8},{10,11... | collective-permute-start | bytes 1277960 | tf_op jit(solution)/shard_map/ppermute | solution.py:1146
  72.7 27.4 %all-to-all-start.1 = ((bf16[16,104,128]{2,1,0:T(8,128)(2,1)}), bf16[16,104,128]{2,1,0:T(8,128)(2,1)S(1)}, u32[]{:S(2)}, u32[]{:S(2)}) async-start(bf16[16,104,128]{2,1,0:T(8,128)(2,1)} %pair_sum.1), calls=%async_computation.1 | async-start | bytes 851968 | tf_op jit(solution)/shard_map/all_to_all | solution.py:1142
  77.5 9.4 %collective-permute-start.1 = (bf16[32,8,128]{2,1,0:T(8,128)(2,1)S(1)}, bf16[32,8,128]{2,1,0:T(8,128)(2,1)S(1)}, u32[]{:S(2)}, u32[]{:S(2)}) collective-permute-start(bf16[32,8,128]{2,1,0:T(8,128)(2,1)S(1)} %get-tuple-element.54), channel_id=1, source_target_pairs={{0,28},{4,0},{8,4},{12,8},{16,12},{20,16},{24,20},{28,24},{1,29},{... | collective-permute-start | bytes 196616 | tf_op jit(solution)/shard_map/ppermute | solution.py:1161
  82.1 7.3 %collective-permute-start.2 = (bf16[32,8,128]{2,1,0:T(8,128)(2,1)S(1)}, bf16[32,8,128]{2,1,0:T(8,128)(2,1)S(1)}, u32[]{:S(2)}, u32[]{:S(2)}) collective-permute-start(bf16[32,8,128]{2,1,0:T(8,128)(2,1)S(1)} %get-tuple-element.55), channel_id=1, source_target_pairs={{0,24},{4,28},{8,0},{12,4},{16,8},{20,12},{24,16},{28,20},{1,25},{... | collective-permute-start | bytes 196616 | tf_op jit(solution)/shard_map/ppermute | solution.py:1161
  82.7 18.4 %collective-permute-start.3 = (bf16[32,8,128]{2,1,0:T(8,128)(2,1)S(1)}, bf16[32,8,128]{2,1,0:T(8,128)(2,1)S(1)}, u32[]{:S(2)}, u32[]{:S(2)}) collective-permute-start(bf16[32,8,128]{2,1,0:T(8,128)(2,1)S(1)} %get-tuple-element.56), channel_id=1, source_target_pairs={{0,20},{4,24},{8,28},{12,0},{16,4},{20,8},{24,12},{28,16},{1,21},{... | collective-permute-start | bytes 196616 | tf_op jit(solution)/shard_map/ppermute | solution.py:1161
  82.7 18.6 %collective-permute-start.4 = (bf16[32,8,128]{2,1,0:T(8,128)(2,1)S(1)}, bf16[32,8,128]{2,1,0:T(8,128)(2,1)S(1)}, u32[]{:S(2)}, u32[]{:S(2)}) collective-permute-start(bf16[32,8,128]{2,1,0:T(8,128)(2,1)S(1)} %get-tuple-element.57), channel_id=1, source_target_pairs={{0,16},{4,20},{8,24},{12,28},{16,0},{20,4},{24,8},{28,12},{1,17},{... | collective-permute-start | bytes 196616 | tf_op jit(solution)/shard_map/ppermute | solution.py:1161
  85.6 16.6 %collective-permute-start.5 = (bf16[32,8,128]{2,1,0:T(8,128)(2,1)S(1)}, bf16[32,8,128]{2,1,0:T(8,128)(2,1)S(1)}, u32[]{:S(2)}, u32[]{:S(2)}) collective-permute-start(bf16[32,8,128]{2,1,0:T(8,128)(2,1)S(1)} %get-tuple-element.58), channel_id=1, source_target_pairs={{0,12},{4,16},{8,20},{12,24},{16,28},{20,0},{24,4},{28,8},{1,13},{... | collective-permute-start | bytes 196616 | tf_op jit(solution)/shard_map/ppermute | solution.py:1161
  86.9 15.3 %collective-permute-start.6 = (bf16[32,8,128]{2,1,0:T(8,128)(2,1)S(1)}, bf16[32,8,128]{2,1,0:T(8,128)(2,1)S(1)}, u32[]{:S(2)}, u32[]{:S(2)}) collective-permute-start(bf16[32,8,128]{2,1,0:T(8,128)(2,1)S(1)} %get-tuple-element.59), channel_id=1, source_target_pairs={{0,8},{4,12},{8,16},{12,20},{16,24},{20,28},{24,0},{28,4},{1,9},{5... | collective-permute-start | bytes 196616 | tf_op jit(solution)/shard_map/ppermute | solution.py:1161
  89.4 12.8 %collective-permute-start.7 = (bf16[32,8,128]{2,1,0:T(8,128)(2,1)S(1)}, bf16[32,8,128]{2,1,0:T(8,128)(2,1)S(1)}, u32[]{:S(2)}, u32[]{:S(2)}) collective-permute-start(bf16[32,8,128]{2,1,0:T(8,128)(2,1)S(1)} %get-tuple-element.60), channel_id=1, source_target_pairs={{0,4},{4,8},{8,12},{12,16},{16,20},{20,24},{24,28},{28,0},{1,5},{5... | collective-permute-start | bytes 196616 | tf_op jit(solution)/shard_map/ppermute | solution.py:1161
  117.2 2.7 %collective-permute-start.8 = (bf16[1664,128]{1,0:T(8,128)(2,1)S(1)}, bf16[1664,128]{1,0:T(8,128)(2,1)S(1)}, u32[]{:S(2)}, u32[]{:S(2)}) collective-permute-start(bf16[1664,128]{1,0:T(8,128)(2,1)S(1)} %bitcast.19), channel_id=1, source_target_pairs={{0,1},{1,0},{2,3},{3,2},{4,5},{5,4},{6,7},{7,6},{8,9},{9,8},{10,11... | collective-permute-start | bytes 1277960 | tf_op jit(solution)/shard_map/ppermute | solution.py:1179

commit v4 on v3

--- a/solution.py
+++ b/solution.py
@@ -11,8 +11,10 @@
 HEAD_DIM = 16
 FOLD = 4
 BATCH = 16
-PAIRS = 32
-ENC_ROWS = 512
+PAIRS = 16
+ENC_ROWS = 256
+SETS = 2
+PLACES = (0.0, 1.0, 2.0, 3.0, 4.0)
 VIS = 8
 GROUP = 16
 PAD = 32
@@ -49,7 +51,7 @@
     size = jnp.abs(hidden)
     base = 1.0 + size * (0.3275911 * 0.7071067811865476)
     t = 1.0 / base
-    bell = jnp.exp(hidden * hidden * -0.5)
+    bell = jnp.exp2(hidden * hidden * (-0.5 * 1.4426950408889634))
     poly = t * (
         0.5 * 0.254829592
         + t * (0.5 * -0.284496736 + t * (0.5 * 1.421413741 + t * (0.5 * -1.453152027 + t * (0.5 * 1.061405429))))
@@ -115,6 +117,11 @@
 def pair_tn(rows, columns):
     full = tn(jnp.concatenate(rows, axis=0), block_diagonal(*columns))
     return full[:, :128], full[:, 128:]
+
+
+def with_bias(rows, grad):
+    full = nn(jnp.concatenate([rows.T, jnp.ones((16, rows.shape[0]), BF)], axis=0), grad)
+    return full[:-16], full[-8:]
 
 
 def softmax_halves(scores, keep):
@@ -144,9 +151,9 @@
 def ln_bwd(grad, gain, hat, inv, where):
     unit = hat[where]
     inner = grad * gain
-    lean = jnp.mean(inner, axis=-1, keepdims=True)
-    tilt = jnp.mean(inner * unit, axis=-1, keepdims=True)
-    return inv[where] * (inner - lean - unit * tilt), fold_rows(grad * unit), fold_rows(grad)
+    lean = jnp.sum(inner, axis=-1, keepdims=True)
+    tilt = jnp.sum(inner * unit, axis=-1, keepdims=True)
+    return inv[where] * (inner - (lean + unit * tilt) * (1.0 / unit.shape[-1])), fold_rows(grad * unit), fold_rows(grad)
 
 
 def prep_kernel(
@@ -371,18 +378,15 @@
             b.d_down[0] += tn(grad_low, b.e_act[whole])
             b.d_b_down[0] += fold_rows(grad_low.astype(F32))
             v.grad_act = nn(grad_low, b.down_t[0])
-            v.total = None
 
         def unbend(start):
             where = slice(self.base + start, self.base + start + 16)
-            part = (v.grad_act[start : start + 16] * b.e_slope[where]).astype(BF)
-            b.e_gh[where] = part
-            summed = fold_rows(part.astype(F32))
-            v.total = summed if v.total is None else v.total + summed
+            b.e_gh[where] = (v.grad_act[start : start + 16] * b.e_slope[where]).astype(BF)
 
         def end():
-            b.d_b_up[0] += v.total
-            b.d_up[0] += tn(b.e_n2[whole], b.e_gh[whole])
+            weights, bias = with_bias(b.e_n2[whole], b.e_gh[whole])
+            b.d_up[0] += weights
+            b.d_b_up[0] += bias
             b.e_gn2[whole] = nn(b.e_gh[whole], b.up_t[0])
 
         return [back] + [functools.partial(unbend, start) for start in range(0, self.rows, 16)] + [end]
@@ -464,11 +468,10 @@
         return steps
 
 
-def weave(*streams):
-    lists = [list(stream) for stream in streams]
+def weave(timeline):
     order = []
-    for which, steps in enumerate(lists):
-        order += [((index + 0.5) / len(steps), which, step) for index, step in enumerate(steps)]
+    for which, (start, length, steps) in enumerate(timeline):
+        order += [(start + length * (index + 0.5) / len(steps), which, step) for index, step in enumerate(steps)]
     for _, _, step in sorted(order, key=lambda entry: entry[:2]):
         step()
 
@@ -510,8 +513,9 @@
             for start in self.chunks():
                 spot = (iota((CHUNK, 128), 0) + start).astype(F32)
                 d.hot[pl.ds(start, CHUNK)] = jnp.where(spot == target, 1.0, 0.0).astype(BF)
-            v.placed = nn(d.hot[...], b.sent[self.sent_rows])
-            v.shown = nn(d.hot[...], jnp.ones((128, 128), BF))
+            both = jnp.concatenate([b.sent[self.sent_rows], jnp.ones((128, 128), BF)], axis=1)
+            full = nn(d.hot[...], both)
+            v.placed, v.shown = full[:, 0:128], full[:, 128:256]
 
         steps.append(begin)
 
@@ -632,21 +636,18 @@
             b.d_down[1] += tn(d.gl[...], d.act[...])
             b.d_b_down[1] += fold_rows(d.g[...])
             v.grad_act = nn(d.gl[...], b.down_t[1])
-            v.total = None
 
         steps.append(back)
 
         def unbend(start):
-            part = (v.grad_act[start : start + 16] * d.slope[pl.ds(start, 16)]).astype(BF)
-            d.gh[pl.ds(start, 16)] = part
-            summed = fold_rows(part.astype(F32))
-            v.total = summed if v.total is None else v.total + summed
+            d.gh[pl.ds(start, 16)] = (v.grad_act[start : start + 16] * d.slope[pl.ds(start, 16)]).astype(BF)
 
         steps += [functools.partial(unbend, start) for start in range(0, self.rows, 16)]
 
         def end():
-            b.d_b_up[1] += v.total
-            b.d_up[1] += tn(d.n2[...], d.gh[...])
+            weights, bias = with_bias(d.n2[...], d.gh[...])
+            b.d_up[1] += weights
+            b.d_b_up[1] += bias
             d.gn2[...] = nn(d.gh[...], b.up_t[1])
 
         steps.append(end)
@@ -745,32 +746,25 @@
         return steps
 
 
-def decoder_all(b, groups, before, after):
-    first, second = b.sets
-    pairs = groups // 2
-    here = Decoder(b, first, 0)
-    there = Decoder(b, second, 1)
-    weave(before, here.attend())
-    weave(here.bend())
-    weave(here.feed(), there.attend())
-
-    def pair(index, carry):
-        here = Decoder(b, first, 2 * index)
-        there = Decoder(b, second, 2 * index + 1)
-        later = Decoder(b, first, 2 * index + 2)
-        latest = Decoder(b, second, 2 * index + 3)
-        weave(there.bend(), here.retreat())
-        weave(there.feed(), later.attend())
-        weave(later.bend(), there.retreat())
-        weave(later.feed(), latest.attend())
-        return carry
-
-    lax.fori_loop(0, pairs - 1, pair, 0)
-    here = Decoder(b, first, groups - 2)
-    there = Decoder(b, second, groups - 1)
-    weave(there.bend(), here.retreat())
-    weave(there.feed())
-    weave(there.retreat(), after)
+def plan(b, groups, encoders, before_first):
+    timeline = []
+    for index in range(groups):
+        decoder = Decoder(b, b.sets[index % SETS], index)
+        phases = (decoder.attend, decoder.bend, decoder.feed, decoder.retreat)
+        for start, stop, phase in zip(PLACES, PLACES[1:], phases):
+            timeline.append((2 * index + start, stop - start, phase()))
+    timeline.append((-0.01, 0.01, [before_first]))
+    for chunk in encoders:
+        first, last = chunk.base // (GROUP * VIS), (chunk.base + chunk.rows) // (GROUP * VIS) - 1
+        early = 2 * first - (4 if first else 2)
+        room = (2 * first - early) / 2
+        timeline.append((early, room, chunk.attend()))
+        timeline.append((early + room, room, chunk.bend()))
+        late = 2 * last + PLACES[-1]
+        room = 2 if last < groups - 1 else 1
+        timeline.append((late, room, chunk.feed()))
+        timeline.append((late + room, room, chunk.retreat()))
+    return timeline
 
 
 IN_NAMES = (
@@ -786,7 +780,7 @@
 
 def main_kernel(names, cap, extra, count, outs, *refs):
     b = Box()
-    b.sets = (Box(), Box())
+    b.sets = tuple(Box() for _ in range(SETS))
     b.back_out = refs[len(IN_NAMES) + len(OUT_NAMES) : len(IN_NAMES) + len(OUT_NAMES) + outs]
     refs = refs[: len(IN_NAMES) + len(OUT_NAMES)] + refs[len(IN_NAMES) + len(OUT_NAMES) + outs :]
     for name, ref in zip(names, refs, strict=True):
@@ -836,14 +830,7 @@
         b.len_col[where] = jnp.broadcast_to(lens[group : group + 1], (128, 128)).T
 
     encoders = [Encoder(b, base, ENC_ROWS) for base in range(0, pixels * VIS, ENC_ROWS)]
-    weave(encoders[0].attend())
-    for now, later in zip(encoders, encoders[1:]):
-        weave(now.bend(), later.attend())
-    cot_copy.wait()
-    decoder_all(b, groups, encoders[-1].bend(), encoders[0].feed())
-    for now, later in zip(encoders, encoders[1:]):
-        weave(now.retreat(), later.feed())
-    weave(encoders[-1].retreat())
+    weave(plan(b, groups, encoders, cot_copy.wait))
     copies = []
     size = b.back.shape[0] // outs
     for index, ref in enumerate(b.back_out):
@@ -869,7 +856,7 @@
 
     small = [total(b.d_gain, i) for i in range(4)] + [total(b.d_bias, i) for i in range(4)]
     for layer in range(2):
-        row = total(b.d_b_up, layer)
+        row = b.d_b_up[layer, 0:1]
         small += [row[:, start : start + 128] for start in range(0, 512, 128)]
     small += [total(b.d_b_down, layer) for layer in range(2)]
     small.append(jnp.sum(b.d_mask[...], axis=0, keepdims=True))
@@ -970,7 +957,7 @@
         "e_gml": ((enc, 128), BF),
         "e_gqkv": ((enc, 384), BF),
     }
-    for side in range(2):
+    for side in range(SETS):
         for name, entry in decoder_scratch(rows, slots).items():
             scratch[f"{name}@{side}"] = entry
     names = IN_NAMES + OUT_NAMES + tuple(scratch) + ("sems",)

time: 123 us -> 118 us (0.959)
  Pallas kernels: 50.3 us -> 45.8 us
    pallas_call x1, Pallas kernels: 39.9 us -> 35.4 us  [main_call(): pl.pallas_call(functools.partial(main_kernel, names, cap, extra, count, o...]
where the time goes in v4:
time: 118 us
  Pallas kernels  45.8 us (39%)
  starting transfers between devices  31.9 us (27%)
  waiting for transfers between devices  20.8 us (18%)
  blocking collectives  15 us (13%)
  local copies, waits for them, and re-layouts  3.26 us (3%)
    pallas_call x1, Pallas kernels, main_call(): pl.pallas_call(functools.partial(main_kernel, names, cap, extra, count, o...  35.4 us
    ppermute x7, starting transfers between devices, shards(): lax.ppermute(back[step], 'pix', [(i, (i - step) % count) for i in range(c...  19.9 us
    all_to_all x1, waiting for transfers between devices, shards(): lax.all_to_all(payload.reshape(count, block, VIS, width), 'pix', split_ax...  15.2 us
    all_to_all x1, blocking collectives, exchange(): lax.all_to_all(values, axes, split_axis=0, concat_axis=0, axis_index_grou...  15 us
    all_to_all x1, starting transfers between devices, shards(): lax.all_to_all(payload.reshape(count, block, VIS, width), 'pix', split_ax...  7.26 us
    all_to_all x1, starting transfers between devices, exchange(): lax.all_to_all(values, axes, split_axis=0, concat_axis=0, axis_index_grou...  4.71 us
    ppermute x7, waiting for transfers between devices, shards(): lax.ppermute(back[step], 'pix', [(i, (i - step) % count) for i in range(c...  3.85 us
    unnamed x32, local copies, waits for them, and re-layouts  3.26 us
  transfers between devices with their start and end apart: 11, of which 6 were waited for; matrix products, arithmetic and copies ran while one was open for 0% of the time, Pallas kernels for 3%

profile of v4, /device:TPU:0, one launch (start us, length us, event | category | flops | bytes accessed | tf_op | source)
XLA Modules:
  0.0 117.9 jit_solution(4476590107134885770)
XLA Ops:
  0.7 0.0 copy-start
  0.7 0.0 copy-start.1
  0.7 1.2 %copy-done.1 = bf16[128,24,128]{2,1,0:T(8,128)(2,1)S(1)} copy-done((bf16[128,24,128]{2,1,0:T(8,128)(2,1)S(1)}, bf16[128,24,128]{2,1,0:T(8,128)(2,1)}, u32[]{:S(2)}) %copy-start.1) | copy-done | bytes 786456
  1.9 0.7 copy-done.7
  2.6 0.7 copy-done.11
  3.2 0.7 copy-done.13
  3.9 0.0 copy-start.6
  3.9 0.0 copy-start.8
  3.9 0.0 copy-start.9
  3.9 0.0 copy-start.10
  4.0 3.1 %prep.1 = (bf16[272,8,128]{2,1,0:T(8,128)(2,1)}, f32[8,128]{1,0:T(8,128)S(1)}, s32[128]{0:T(128)S(1)}, s32[128]{0:T(128)S(1)}) custom-call(s32[1]{0:T(128)} %bitcast.1.me_ref, s32[128]{0:T(128)S(1)} %copy-done.11, bf16[3072,128]{1,0:T(8,128)(2,1)S(1)} %bitcast.21, s32[1,128]{1,0:T(1,128)S(1)} %bitcast.28, s32[24,128]{1,0:T(8,128)S(1)} %bitcast.24, ...), custom_call_target="tpu_custom_call" | custom-call | tf_op jit(solution)/shard_map/prep/pallas_call | solution.py:219
  7.1 7.3 %all-to-all-start = ((bf16[8,34,8,128]{3,2,1,0:T(8,128)(2,1)}), bf16[8,34,8,128]{3,2,1,0:T(8,128)(2,1)S(1)}, u32[]{:S(2)}, u32[]{:S(2)}) async-start(bf16[8,34,8,128]{3,2,1,0:T(8,128)(2,1)} %bitcast.6), calls=%async_computation | async-start | bytes 1114112 | tf_op jit(solution)/shard_map/all_to_all | solution.py:1106
  14.4 15.2 %all-to-all-done = bf16[8,34,8,128]{3,2,1,0:T(8,128)(2,1)S(1)} async-done(((bf16[8,34,8,128]{3,2,1,0:T(8,128)(2,1)}), bf16[8,34,8,128]{3,2,1,0:T(8,128)(2,1)S(1)}, u32[]{:S(2)}, u32[]{:S(2)}) %all-to-all-start) | async-done | bytes 557088 | tf_op jit(solution)/shard_map/all_to_all | solution.py:1106
  29.6 0.0 copy-done.4
  29.6 0.0 copy-done.5
  29.6 0.0 copy-done.6
  29.6 0.0 copy-done.8
  29.6 0.0 copy-done.9
  29.6 0.0 copy-done.10
  29.6 0.0 copy-done.12
  29.6 0.0 copy-done.14
  29.6 0.0 copy-done.15
  29.6 35.4 %layers.1 = (f32[128,24,128]{2,1,0:T(8,128)}, bf16[1664,128]{1,0:T(8,128)(2,1)S(1)}, bf16[1664,128]{1,0:T(8,128)(2,1)S(1)}, bf16[32,8,128]{2,1,0:T(8,128)(2,1)S(...) custom-call(s32[1]{0:T(128)} %bitcast.refs_0_, ...), custom_call_target="tpu_custom_call" | custom-call | tf_op jit(solution)/shard_map/layers/pallas_call | solution.py:965
  65.1 0.1 collective-permute-start
  65.2 1.8 %collective-permute-done = bf16[1664,128]{1,0:T(8,128)(2,1)S(1)} collective-permute-done((bf16[1664,128]{1,0:T(8,128)(2,1)S(1)}, bf16[1664,128]{1,0:T(8,128)(2,1)S(1)}, u32[]{:S(2)}, u32[]{:S(2)}) %collective-permute-start) | collective-permute-done | bytes 426016 | tf_op jit(solution)/shard_map/ppermute | solution.py:1133
  66.9 1.3 %pair_sum.1 = bf16[16,104,128]{2,1,0:T(8,128)(2,1)} custom-call(bf16[16,104,128]{2,1,0:T(8,128)(2,1)S(1)} %bitcast.22, bf16[16,104,128]{2,1,0:T(8,128)(2,1)S(1)} %bitcast.23), custom_call_target="tpu_custom_call" | custom-call | tf_op jit(solution)/shard_map/pair_sum/pallas_call | solution.py:1136
  68.2 4.7 %all-to-all-start.1 = ((bf16[16,104,128]{2,1,0:T(8,128)(2,1)}), bf16[16,104,128]{2,1,0:T(8,128)(2,1)S(1)}, u32[]{:S(2)}, u32[]{:S(2)}) async-start(bf16[16,104,128]{2,1,0:T(8,128)(2,1)} %pair_sum.1), calls=%async_computation.1 | async-start | bytes 851968 | tf_op jit(solution)/shard_map/all_to_all | solution.py:1129
  73.0 4.6 %collective-permute-start.1 = (bf16[32,8,128]{2,1,0:T(8,128)(2,1)S(1)}, bf16[32,8,128]{2,1,0:T(8,128)(2,1)S(1)}, u32[]{:S(2)}, u32[]{:S(2)}) collective-permute-start(bf16[32,8,128]{2,1,0:T(8,128)(2,1)S(1)} %get-tuple-element.54), channel_id=1, source_target_pairs={{0,28},{4,0},{8,4},{12,8},{16,12},{20,16},{24,20},{28,24},{1,29},{... | collective-permute-start | bytes 196616 | tf_op jit(solution)/shard_map/ppermute | solution.py:1148
  77.6 0.6 collective-permute-start.2
  78.2 0.0 collective-permute-start.3
  78.2 2.9 %collective-permute-start.4 = (bf16[32,8,128]{2,1,0:T(8,128)(2,1)S(1)}, bf16[32,8,128]{2,1,0:T(8,128)(2,1)S(1)}, u32[]{:S(2)}, u32[]{:S(2)}) collective-permute-start(bf16[32,8,128]{2,1,0:T(8,128)(2,1)S(1)} %get-tuple-element.57), channel_id=1, source_target_pairs={{0,16},{4,20},{8,24},{12,28},{16,0},{20,4},{24,8},{28,12},{1,17},{... | collective-permute-start | bytes 196616 | tf_op jit(solution)/shard_map/ppermute | solution.py:1148
  81.1 0.0 collective-permute-start.5
  81.1 1.3 %collective-permute-done.1.refs_1_ = bf16[32,8,128]{2,1,0:T(8,128)(2,1)S(1)} collective-permute-done((bf16[32,8,128]{2,1,0:T(8,128)(2,1)S(1)}, bf16[32,8,128]{2,1,0:T(8,128)(2,1)S(1)}, u32[]{:S(2)}, u32[]{:S(2)}) %collective-permute-start.1) | collective-permute-done | bytes 65568 | tf_op jit(solution)/shard_map/ppermute | solution.py:1148
  82.4 1.1 collective-permute-start.6
  83.4 1.5 %collective-permute-done.2.refs_2_ = bf16[32,8,128]{2,1,0:T(8,128)(2,1)S(1)} collective-permute-done((bf16[32,8,128]{2,1,0:T(8,128)(2,1)S(1)}, bf16[32,8,128]{2,1,0:T(8,128)(2,1)S(1)}, u32[]{:S(2)}, u32[]{:S(2)}) %collective-permute-start.2) | collective-permute-done | bytes 65568 | tf_op jit(solution)/shard_map/ppermute | solution.py:1148
  84.9 10.7 %collective-permute-start.7 = (bf16[32,8,128]{2,1,0:T(8,128)(2,1)S(1)}, bf16[32,8,128]{2,1,0:T(8,128)(2,1)S(1)}, u32[]{:S(2)}, u32[]{:S(2)}) collective-permute-start(bf16[32,8,128]{2,1,0:T(8,128)(2,1)S(1)} %get-tuple-element.60), channel_id=1, source_target_pairs={{0,4},{4,8},{8,12},{12,16},{16,20},{20,24},{24,28},{28,0},{1,5},{5... | collective-permute-start | bytes 196616 | tf_op jit(solution)/shard_map/ppermute | solution.py:1148
  95.6 0.0 all-to-all-done.1.parts_ref
  95.6 1.0 chunk_sum.1
  96.6 0.0 collective-permute-done.3.refs_3_
  96.6 0.2 collective-permute-done.4.refs_4_
  96.8 0.9 collective-permute-done.5.refs_5_
  97.7 0.0 collective-permute-done.6.refs_6_
  97.7 0.0 collective-permute-done.7.refs_7_
  97.7 15.0 %all_to_all.15 = bf16[16,104,128]{2,1,0:T(8,128)(2,1)S(1)} all-to-all(bf16[16,104,128]{2,1,0:T(8,128)(2,1)S(1)} %chunk_sum.1), channel_id=1, replica_groups={{0,2,4,6,8,10,12,14,16,18,20,22,24,26,28,30},{1,3,5,7,9,11,13,15,17,19,..., dimensions={0} | all-to-all | bytes 851968 | tf_op jit(solution)/shard_map/all_to_all | solution.py:1129
  112.7 0.0 collective-permute-start.8
  112.7 2.6 %restore.1 = f32[3072,128]{1,0:T(8,128)} custom-call(s32[128]{0:T(128)S(1)} %get-tuple-element.47.refs_2_.place_ref, f32[8,128]{1,0:T(8,128)S(1)} %get-tuple-element.50.pos_ref, bf16[32,8,128]{2,1,0:T(8,128)(2,1)S(1)} %get-tuple-element.61.refs_0_, bf16[32,8,128]{2,1,0:T(8,128)(2,1)S(1)} %collective-permute-done.1.refs_1_, ...), custom_call_target="tpu_custom_call" | custom-call | tf_op jit(solution)/shard_map/restore/pallas_call | solution.py:1179
  115.4 0.0 collective-permute-done.8.refs_2_
  115.4 2.3 %unpack.1 = (f32[4,128]{1,0:T(4,128)}, f32[4,128]{1,0:T(4,128)}, f32[2,512]{1,0:T(2,128)}, f32[2,128]{1,0:T(2,128)}, f32[1,128]{1,0:T(1,128)}, /*index=5*/f32[24...) custom-call(s32[1]{0:T(128)} %bitcast.refs_0_, ...), custom_call_target="tpu_custom_call" | custom-call | tf_op jit(solution)/shard_map/unpack/pallas_call | solution.py:1169
  (13 shorter events, 0.0 us)
Async XLA Ops:
  0.7 28.9 %copy-start = (bf16[128,24,128]{2,1,0:T(8,128)(2,1)S(1)}, bf16[128,24,128]{2,1,0:T(8,128)(2,1)}, u32[]{:S(2)}) copy-start(bf16[128,24,128]{2,1,0:T(8,128)(2,1)} %refs_5_.1) | copy-start | bytes 2359300
  0.7 1.2 %copy-start.1 = (bf16[128,24,128]{2,1,0:T(8,128)(2,1)S(1)}, bf16[128,24,128]{2,1,0:T(8,128)(2,1)}, u32[]{:S(2)}) copy-start(bf16[128,24,128]{2,1,0:T(8,128)(2,1)} %param.16) | copy-start | bytes 2359300
  1.9 0.7 copy-start.7
  2.6 0.7 copy-start.11
  3.2 0.7 copy-start.13
  3.9 25.7 %copy-start.2 = (bf16[2,128,512]{2,1,0:T(8,128)(2,1)S(1)}, bf16[2,128,512]{2,1,0:T(8,128)(2,1)}, u32[]{:S(2)}) copy-start(bf16[2,128,512]{2,1,0:T(8,128)(2,1)} %refs_8_.1) | copy-start | bytes 786436
  3.9 25.7 %copy-start.3 = (bf16[2,512,128]{2,1,0:T(8,128)(2,1)S(1)}, bf16[2,512,128]{2,1,0:T(8,128)(2,1)}, u32[]{:S(2)}) copy-start(bf16[2,512,128]{2,1,0:T(8,128)(2,1)} %refs_9_.1) | copy-start | bytes 786436
  3.9 25.7 %copy-start.4 = (bf16[2,128,384]{2,1,0:T(8,128)(2,1)S(1)}, bf16[2,128,384]{2,1,0:T(8,128)(2,1)}, u32[]{:S(2)}) copy-start(bf16[2,128,384]{2,1,0:T(8,128)(2,1)} %refs_6_.1) | copy-start | bytes 589828
  3.9 25.7 %copy-start.5 = (bf16[2,128,128]{2,1,0:T(8,128)(2,1)S(1)}, bf16[2,128,128]{2,1,0:T(8,128)(2,1)}, u32[]{:S(2)}) copy-start(bf16[2,128,128]{2,1,0:T(8,128)(2,1)} %refs_7_.1) | copy-start | bytes 196612
  3.9 25.7 %copy-start.6 = (f32[24,128]{1,0:T(8,128)S(1)}, f32[24,128]{1,0:T(8,128)}, u32[]{:S(2)}) copy-start(f32[24,128]{1,0:T(8,128)} %refs_15_.1) | copy-start | bytes 36868
  3.9 25.7 %copy-start.8 = (f32[2,512]{1,0:T(2,128)S(1)}, f32[2,512]{1,0:T(2,128)}, u32[]{:S(2)}) copy-start(f32[2,512]{1,0:T(2,128)} %refs_10_.1) | copy-start | bytes 12292
  3.9 25.7 %copy-start.9 = (f32[2,2,128]{2,1,0:T(2,128)S(1)}, f32[2,2,128]{2,1,0:T(2,128)}, u32[]{:S(2)}) copy-start(f32[2,2,128]{2,1,0:T(2,128)} %param.21) | copy-start | bytes 6148
  3.9 25.7 %copy-start.10 = (f32[2,2,128]{2,1,0:T(2,128)S(1)}, f32[2,2,128]{2,1,0:T(2,128)}, u32[]{:S(2)}) copy-start(f32[2,2,128]{2,1,0:T(2,128)} %param.22) | copy-start | bytes 6148
  3.9 25.7 %copy-start.12 = (f32[2,128]{1,0:T(2,128)S(1)}, f32[2,128]{1,0:T(2,128)}, u32[]{:S(2)}) copy-start(f32[2,128]{1,0:T(2,128)} %refs_11_.1) | copy-start | bytes 3076
  4.0 25.7 %copy-start.14 = (s32[128]{0:T(128)S(1)}, s32[128]{0:T(128)}, u32[]{:S(2)}) copy-start(s32[128]{0:T(128)} %refs_3_.1) | copy-start | bytes 1540
  4.0 25.7 %copy-start.15 = (f32[128]{0:T(128)S(1)}, f32[128]{0:T(128)}, u32[]{:S(2)}) copy-start(f32[128]{0:T(128)} %param.29) | copy-start | bytes 1540
  7.1 22.5 %all-to-all-start = ((bf16[8,34,8,128]{3,2,1,0:T(8,128)(2,1)}), bf16[8,34,8,128]{3,2,1,0:T(8,128)(2,1)S(1)}, u32[]{:S(2)}, u32[]{:S(2)}) async-start(bf16[8,34,8,128]{3,2,1,0:T(8,128)(2,1)} %bitcast.6), calls=%async_computation | async-start | bytes 1114112 | tf_op jit(solution)/shard_map/all_to_all | solution.py:1106
  65.1 1.8 %collective-permute-start = (bf16[1664,128]{1,0:T(8,128)(2,1)S(1)}, bf16[1664,128]{1,0:T(8,128)(2,1)S(1)}, u32[]{:S(2)}, u32[]{:S(2)}) collective-permute-start(bf16[1664,128]{1,0:T(8,128)(2,1)S(1)} %get-tuple-element.52), channel_id=1, source_target_pairs={{0,1},{1,0},{2,3},{3,2},{4,5},{5,4},{6,7},{7,6},{8,9},{9,8},{10,11... | collective-permute-start | bytes 1277960 | tf_op jit(solution)/shard_map/ppermute | solution.py:1133
  68.2 27.4 %all-to-all-start.1 = ((bf16[16,104,128]{2,1,0:T(8,128)(2,1)}), bf16[16,104,128]{2,1,0:T(8,128)(2,1)S(1)}, u32[]{:S(2)}, u32[]{:S(2)}) async-start(bf16[16,104,128]{2,1,0:T(8,128)(2,1)} %pair_sum.1), calls=%async_computation.1 | async-start | bytes 851968 | tf_op jit(solution)/shard_map/all_to_all | solution.py:1129
  73.0 9.4 %collective-permute-start.1 = (bf16[32,8,128]{2,1,0:T(8,128)(2,1)S(1)}, bf16[32,8,128]{2,1,0:T(8,128)(2,1)S(1)}, u32[]{:S(2)}, u32[]{:S(2)}) collective-permute-start(bf16[32,8,128]{2,1,0:T(8,128)(2,1)S(1)} %get-tuple-element.54), channel_id=1, source_target_pairs={{0,28},{4,0},{8,4},{12,8},{16,12},{20,16},{24,20},{28,24},{1,29},{... | collective-permute-start | bytes 196616 | tf_op jit(solution)/shard_map/ppermute | solution.py:1148
  77.6 7.3 %collective-permute-start.2 = (bf16[32,8,128]{2,1,0:T(8,128)(2,1)S(1)}, bf16[32,8,128]{2,1,0:T(8,128)(2,1)S(1)}, u32[]{:S(2)}, u32[]{:S(2)}) collective-permute-start(bf16[32,8,128]{2,1,0:T(8,128)(2,1)S(1)} %get-tuple-element.55), channel_id=1, source_target_pairs={{0,24},{4,28},{8,0},{12,4},{16,8},{20,12},{24,16},{28,20},{1,25},{... | collective-permute-start | bytes 196616 | tf_op jit(solution)/shard_map/ppermute | solution.py:1148
  78.2 18.4 %collective-permute-start.3 = (bf16[32,8,128]{2,1,0:T(8,128)(2,1)S(1)}, bf16[32,8,128]{2,1,0:T(8,128)(2,1)S(1)}, u32[]{:S(2)}, u32[]{:S(2)}) collective-permute-start(bf16[32,8,128]{2,1,0:T(8,128)(2,1)S(1)} %get-tuple-element.56), channel_id=1, source_target_pairs={{0,20},{4,24},{8,28},{12,0},{16,4},{20,8},{24,12},{28,16},{1,21},{... | collective-permute-start | bytes 196616 | tf_op jit(solution)/shard_map/ppermute | solution.py:1148
  78.2 18.6 %collective-permute-start.4 = (bf16[32,8,128]{2,1,0:T(8,128)(2,1)S(1)}, bf16[32,8,128]{2,1,0:T(8,128)(2,1)S(1)}, u32[]{:S(2)}, u32[]{:S(2)}) collective-permute-start(bf16[32,8,128]{2,1,0:T(8,128)(2,1)S(1)} %get-tuple-element.57), channel_id=1, source_target_pairs={{0,16},{4,20},{8,24},{12,28},{16,0},{20,4},{24,8},{28,12},{1,17},{... | collective-permute-start | bytes 196616 | tf_op jit(solution)/shard_map/ppermute | solution.py:1148
  81.1 16.6 %collective-permute-start.5 = (bf16[32,8,128]{2,1,0:T(8,128)(2,1)S(1)}, bf16[32,8,128]{2,1,0:T(8,128)(2,1)S(1)}, u32[]{:S(2)}, u32[]{:S(2)}) collective-permute-start(bf16[32,8,128]{2,1,0:T(8,128)(2,1)S(1)} %get-tuple-element.58), channel_id=1, source_target_pairs={{0,12},{4,16},{8,20},{12,24},{16,28},{20,0},{24,4},{28,8},{1,13},{... | collective-permute-start | bytes 196616 | tf_op jit(solution)/shard_map/ppermute | solution.py:1148
  82.4 15.3 %collective-permute-start.6 = (bf16[32,8,128]{2,1,0:T(8,128)(2,1)S(1)}, bf16[32,8,128]{2,1,0:T(8,128)(2,1)S(1)}, u32[]{:S(2)}, u32[]{:S(2)}) collective-permute-start(bf16[32,8,128]{2,1,0:T(8,128)(2,1)S(1)} %get-tuple-element.59), channel_id=1, source_target_pairs={{0,8},{4,12},{8,16},{12,20},{16,24},{20,28},{24,0},{28,4},{1,9},{5... | collective-permute-start | bytes 196616 | tf_op jit(solution)/shard_map/ppermute | solution.py:1148
  84.9 12.8 %collective-permute-start.7 = (bf16[32,8,128]{2,1,0:T(8,128)(2,1)S(1)}, bf16[32,8,128]{2,1,0:T(8,128)(2,1)S(1)}, u32[]{:S(2)}, u32[]{:S(2)}) collective-permute-start(bf16[32,8,128]{2,1,0:T(8,128)(2,1)S(1)} %get-tuple-element.60), channel_id=1, source_target_pairs={{0,4},{4,8},{8,12},{12,16},{16,20},{20,24},{24,28},{28,0},{1,5},{5... | collective-permute-start | bytes 196616 | tf_op jit(solution)/shard_map/ppermute | solution.py:1148
  112.7 2.7 %collective-permute-start.8 = (bf16[1664,128]{1,0:T(8,128)(2,1)S(1)}, bf16[1664,128]{1,0:T(8,128)(2,1)S(1)}, u32[]{:S(2)}, u32[]{:S(2)}) collective-permute-start(bf16[1664,128]{1,0:T(8,128)(2,1)S(1)} %bitcast.19), channel_id=1, source_target_pairs={{0,1},{1,0},{2,3},{3,2},{4,5},{5,4},{6,7},{7,6},{8,9},{9,8},{10,11... | collective-permute-start | bytes 1277960 | tf_op jit(solution)/shard_map/ppermute | solution.py:1166

commit v5 on v4

--- a/solution.py
+++ b/solution.py
@@ -19,6 +19,9 @@
 GROUP = 16
 PAD = 32
 CHUNK = 48
+FIRST = (4,)
+MIDDLE = (1, 2, 3, 5, 6, 7)
+LAST = ()
 EPS = 1e-05
 NEG = -1e30
 BF = jnp.bfloat16
@@ -158,7 +161,7 @@
 
 def prep_kernel(
     cap, extra, count, me_ref, dest_ref, tokens_ref, len_ref, masked_ref, dest_row_ref,
-    payload_ref, pos_ref, take_ref, back_ref, tally,
+    payload_ref, pos_ref, route_ref, tally,
 ):
     slots, pixels = masked_ref.shape
     groups = pixels // GROUP
@@ -196,8 +199,7 @@
             rank = tally[dest]
             tally[dest] = rank + 1
             sender = lax.rem(2 * me - dest + 2 * count, count)
-            take_ref[series] = sender * block + rank
-            back_ref[series] = lax.rem(dest - me + count, count) * cap + rank
+            route_ref[series] = sender * 256 + rank
             payload_ref[dest * block + rank] = rows[member_id].astype(BF)
     pos_rows = jnp.concatenate(found, axis=0)
     pos_ref[...] = pos_rows
@@ -222,12 +224,11 @@
             jax.ShapeDtypeStruct((count * (cap + extra), VIS, width), BF),
             jax.ShapeDtypeStruct((pixels // GROUP, GROUP * VIS), F32),
             index,
-            index,
         ),
         in_specs=[smem, smem, vmem, vmem, vmem, vmem],
-        out_specs=(vmem, vmem, smem, smem),
+        out_specs=(vmem, vmem, smem),
         scratch_shapes=[pltpu.SMEM((count,), jnp.int32)],
-        compiler_params=pltpu.CompilerParams(vmem_limit_bytes=6 * MIB),
+        compiler_params=pltpu.CompilerParams(vmem_limit_bytes=56 * MIB),
         name="prep",
     )(
         me, route_dev, tokens.reshape(pixels * slots, width), lengths.reshape(1, pixels), masked.T,
@@ -237,6 +238,10 @@
 
 class Box:
     pass
+
+
+def offset_place(route, me, count, cap):
+    return lax.rem(me - (route >> 8) + count, count) * cap + (route & 255)
 
 
 def gelu_stage(hidden, b_up, act, slope, base, rows):
@@ -285,7 +290,7 @@
         same = iota((16, 128), 0) // VIS == (iota((16, 128), 1) % 16) // VIS
 
         def load(series):
-            b.e_x[series * VIS : (series + 1) * VIS] = b.recv[b.take[series]].astype(F32)
+            b.e_x[series * VIS : (series + 1) * VIS] = b.recv[b.take(series)].astype(F32)
 
         steps = [functools.partial(load, series) for series in range(self.base // VIS, (self.base + self.rows) // VIS)]
 
@@ -462,7 +467,7 @@
             grad = grad + b.e_gm[where]
             for series in range(where.start // VIS, where.stop // VIS):
                 at = series * VIS - where.start
-                b.back[b.back_at[series]] = grad[at : at + VIS].astype(BF)
+                b.back[b.back_at(series)] = grad[at : at + VIS].astype(BF)
 
         steps += [functools.partial(first_norm, where) for where in self.chunks()]
         return steps
@@ -768,7 +773,7 @@
 
 
 IN_NAMES = (
-    "core", "take", "back_at", "slot", "recv_in", "cot_in", "w_qkv", "w_out", "w_up", "w_down", "b_up", "b_down",
+    "core", "me", "route", "slot", "recv_in", "cot_in", "w_qkv", "w_out", "w_up", "w_down", "b_up", "b_down",
     "gain", "bias", "mask", "pos",
 )
 OUT_NAMES = ("dec_out", "keep", "send")
@@ -795,6 +800,8 @@
     pixels = b.cot.shape[0]
     groups = pixels // GROUP
     block = cap + extra
+    b.take = lambda series: (b.route[series] >> 8) * block + (b.route[series] & 255)
+    b.back_at = lambda series: offset_place(b.route[series], b.me[0], count, cap)
     recv_copy = pltpu.make_async_copy(b.recv_in, b.recv, b.sems.at[0])
     recv_copy.start()
     cot_copy = pltpu.make_async_copy(b.cot_in, b.cot, b.sems.at[2])
@@ -982,7 +989,15 @@
     return copies
 
 
-def pair_sum_kernel(mine_ref, theirs_ref, out_ref, mine, theirs, sems):
+def pair_sum_kernel(spot_ref, mine_ref, theirs_ref, keep_ref, send_ref, mine, theirs, sems):
+    for copy in fetch([(mine_ref, mine), (theirs_ref, theirs)], sems):
+        copy.wait()
+    side = spot_ref[0]
+    for ref, which in ((send_ref, 1 - side), (keep_ref, side)):
+        ref[...] = (mine[:, which].astype(F32) + theirs[:, which].astype(F32)).astype(BF)
+
+
+def quad_sum_kernel(mine_ref, theirs_ref, out_ref, mine, theirs, sems):
     for copy in fetch([(mine_ref, mine), (theirs_ref, theirs)], sems):
         copy.wait()
     out_ref[...] = (mine[...].astype(F32) + theirs[...].astype(F32)).astype(BF)
@@ -996,7 +1011,7 @@
     for part in range(1, count):
         total = total + parts[part].astype(F32)
     low[...] = total.astype(BF)
-    for copy in fetch([(low, out_ref.at[part]) for part in range(count)], sems):
+    for copy in fetch([(low, out_ref.at[part]) for part in range(out_ref.shape[0])], sems):
         copy.wait()
 
 
@@ -1061,7 +1076,7 @@
         copy.wait()
 
 
-def restore_kernel(cap, count, place_ref, pos_ref, *refs):
+def restore_kernel(cap, steps, count, spot_ref, route_ref, pos_ref, *refs):
     blocks, (out_ref, rows, held, out, sems) = refs[:count], refs[count:]
     size = rows.shape[0] // count
     copies = fetch([(ref, rows.at[pl.ds(index * size, size)]) for index, ref in enumerate(blocks)], sems)
@@ -1073,7 +1088,7 @@
         copy.wait()
     for group in range(groups):
         for member in range(GROUP):
-            block = rows[place_ref[group * GROUP + member]]
+            block = rows[offset_place(route_ref[group * GROUP + member], spot_ref[0], steps, cap)]
             held[pl.ds((group % 2) * 128 + member * VIS, VIS)] = block.astype(F32)
         pos_row = pos_ref[group : group + 1]
         target = jnp.where(pos_row > 0, (lane // VIS * slots).astype(F32) + pos_row - 1.0, -1.0)
@@ -1098,10 +1113,9 @@
     vmem = pl.BlockSpec(memory_space=pltpu.VMEM)
     anywhere = pl.BlockSpec(memory_space=pl.ANY)
     pix = lax.axis_index("pix")
-    me = pix.reshape(1).astype(jnp.int32)
-    flat = pix * reps + lax.axis_index("rep")
-    core = (flat % 2).reshape(1).astype(jnp.int32)
-    payload, pos_rows, take, back_at = prep(tokens, lengths, masked, route_dev, count, cap, extra, me)
+    rep = lax.axis_index("rep")
+    core, side, me = (value.reshape(1).astype(jnp.int32) for value in (rep % 2, rep // 2 % 2, pix))
+    payload, pos_rows, route = prep(tokens, lengths, masked, route_dev, count, cap, extra, me)
     block = cap + extra
     recv = lax.all_to_all(
         payload.reshape(count, block, VIS, width), "pix", split_axis=0, concat_axis=0, tiled=True
@@ -1112,7 +1126,7 @@
     direct = count <= 8
     dec, keep, send, *back = main_call(
         (
-            core, take, back_at, route_slot, recv, cotangent, w_qkv, w_out, w_up, w_down, b_up, b_down,
+            core, me, route, route_slot, recv, cotangent, w_qkv, w_out, w_up, w_down, b_up, b_down,
             norm_gain.reshape(4, width), norm_bias.reshape(4, width), mask_token.reshape(1, width), pos_table,
         ),
         cap,
@@ -1131,38 +1145,61 @@
         )
 
     theirs = lax.ppermute(send, axes, swap)
-    piece = jax.ShapeDtypeStruct((half, chunk, 128), BF)
-    line = pltpu.VMEM((half, chunk, 128), BF)
+    quarter = jax.ShapeDtypeStruct((count, chunk, 128), BF)
+    line = pltpu.VMEM((count, 2, chunk, 128), BF)
+    keep, send = pl.pallas_call(
+        pair_sum_kernel,
+        out_shape=(quarter, quarter),
+        in_specs=[smem, anywhere, anywhere],
+        out_specs=(vmem, vmem),
+        scratch_shapes=[line, line, pltpu.SemaphoreType.DMA((2,))],
+        compiler_params=pltpu.CompilerParams(vmem_limit_bytes=4 * MIB),
+        name="pair_sum",
+    )(side, keep.reshape(count, 2, chunk, 128), theirs.reshape(count, 2, chunk, 128))
+    theirs = lax.ppermute(send, axes, [(i, i ^ 2) for i in range(devices)])
+    gone = {}
+
+    def tie(values, steps):
+        tied, *some = lax.optimization_barrier((values, *[gone[step] for step in steps if step in gone]))
+        gone.update(zip([step for step in steps if step in gone], some))
+        return tied
+
+    if direct:
+        for step in range(1, count):
+            gone[step] = lax.ppermute(back[step], "pix", [(i, (i - step) % count) for i in range(count)])
+    theirs = tie(theirs, FIRST)
+    line = pltpu.VMEM((count, chunk, 128), BF)
     paired = pl.pallas_call(
-        pair_sum_kernel,
-        out_shape=piece,
+        quad_sum_kernel,
+        out_shape=quarter,
         in_specs=[anywhere, anywhere],
         out_specs=vmem,
         scratch_shapes=[line, line, pltpu.SemaphoreType.DMA((2,))],
         compiler_params=pltpu.CompilerParams(vmem_limit_bytes=4 * MIB),
-        name="pair_sum",
-    )(keep.reshape(half, chunk, 128), theirs.reshape(half, chunk, 128))
+        name="quad_sum",
+    )(keep, theirs)
     if direct:
-        returned = back[:1]
-        for step in range(1, count):
-            returned.append(lax.ppermute(back[step], "pix", [(i, (i - step) % count) for i in range(count)]))
+        returned = []
     else:
         turn = (pix - jnp.arange(count)) % count
         blocks = lax.all_to_all(
             back[0].reshape(count, cap, VIS, width)[turn], "pix", split_axis=0, concat_axis=0, tiled=True
         )
         returned = [blocks[(pix + jnp.arange(count)) % count].reshape(count * cap, VIS, width)]
+    parts = lax.all_to_all(paired, "pix", split_axis=0, concat_axis=0, tiled=True)
     spread = pl.pallas_call(
         chunk_sum_kernel,
-        out_shape=piece,
+        out_shape=jax.ShapeDtypeStruct((half, chunk, 128), BF),
         in_specs=[anywhere],
         out_specs=anywhere,
         scratch_shapes=[line, pltpu.VMEM((chunk, 128), BF), pltpu.SemaphoreType.DMA((half,))],
         compiler_params=pltpu.CompilerParams(vmem_limit_bytes=4 * MIB),
         name="chunk_sum",
-    )(exchange(paired))
-    spread, *returned = lax.optimization_barrier((spread, *returned))
-    summed = exchange(spread).reshape(half * chunk, 128)
+    )(parts)
+    spread = tie(spread, MIDDLE)
+    summed = tie(exchange(spread).reshape(half * chunk, 128), LAST)
+    if direct:
+        returned = [back[0]] + [gone[step] for step in range(1, count)]
     other = lax.ppermute(summed, axes, swap)
     small = ((4, width), (4, width), b_up.shape, b_down.shape, (1, width), pos_table.shape)
     large = tuple(w.shape for w in (w_qkv, w_out, w_up, w_down))
@@ -1177,9 +1214,9 @@
         name="unpack",
     )(core, summed, other)
     grad_tokens = pl.pallas_call(
-        functools.partial(restore_kernel, cap, len(returned)),
+        functools.partial(restore_kernel, cap, count, len(returned)),
         out_shape=jax.ShapeDtypeStruct((pixels * slots, width), F32),
-        in_specs=[smem, vmem] + [anywhere] * len(returned),
+        in_specs=[smem, smem, vmem] + [anywhere] * len(returned),
         out_specs=anywhere,
         scratch_shapes=[
             pltpu.VMEM((count * cap, VIS, width), BF),
@@ -1189,7 +1226,7 @@
         ],
         compiler_params=pltpu.CompilerParams(vmem_limit_bytes=8 * MIB),
         name="restore",
-    )(back_at, pos_rows, *returned)
+    )(me, route, pos_rows, *returned)
     return (
         dec,
         grad_tokens.reshape(pixels, slots, width),

time: 118 us -> 115 us (0.975)
  starting transfers between devices: 31.9 us -> 22 us
  waiting for transfers between devices: 20.8 us -> 29.6 us
  local copies, waits for them, and re-layouts: 3.26 us -> 0.71 us
    ppermute x7, starting transfers between devices: 19.9 us -> 9.69 us  [shards(): lax.ppermute(back[step], 'pix', [(i, (i - step) % count) for i in range(c...]
    ppermute x7, waiting for transfers between devices: 3.85 us -> 12.7 us  [shards(): lax.ppermute(back[step], 'pix', [(i, (i - step) % count) for i in range(c...]
    unnamed x32 -> x30, local copies, waits for them, and re-layouts: 3.26 us -> 0.71 us
    ppermute x0 -> x1, starting transfers between devices: none -> 1.58 us  [shards(): theirs = lax.ppermute(send, axes, [(i, i ^ 2) for i in range(devices)])]
    all_to_all x1, starting transfers between devices: 4.71 us -> 3.41 us  [shards(): lax.all_to_all(paired, 'pix', split_axis=0, concat_axis=0, tiled=True)]
    pallas_call x3 -> x4, Pallas kernels: 4.94 us -> 5.83 us  [the longest x1 2.98 us: shards(): pl.pallas_call(functools.partial(restore_kernel, cap, count, len(returned...]
  transfers between devices with their start and end apart: 11 -> 12, of which waited for: 6 -> 4; matrix products, arithmetic and copies ran while one was open for 0% -> 0% of each run, Pallas kernels for 3% -> 3%
where the time goes in v5:
time: 115 us
  Pallas kernels  46.8 us (41%)
  waiting for transfers between devices  29.6 us (26%)
  starting transfers between devices  22 us (19%)
  blocking collectives  14.7 us (13%)
    pallas_call x1, Pallas kernels, main_call(): pl.pallas_call(functools.partial(main_kernel, names, cap, extra, count, o...  35.3 us
    all_to_all x1, waiting for transfers between devices, shards(): lax.all_to_all(payload.reshape(count, block, VIS, width), 'pix', split_ax...  15.2 us
    all_to_all x1, blocking collectives, exchange(): lax.all_to_all(values, axes, split_axis=0, concat_axis=0, axis_index_grou...  14.7 us
    ppermute x7, waiting for transfers between devices, shards(): lax.ppermute(back[step], 'pix', [(i, (i - step) % count) for i in range(c...  12.7 us
    ppermute x7, starting transfers between devices, shards(): lax.ppermute(back[step], 'pix', [(i, (i - step) % count) for i in range(c...  9.69 us
    all_to_all x1, starting transfers between devices, shards(): lax.all_to_all(payload.reshape(count, block, VIS, width), 'pix', split_ax...  7.27 us
    pallas_call x1, Pallas kernels, prep(): pl.pallas_call(functools.partial(prep_kernel, cap, extra, count), out_sha...  3.44 us
    all_to_all x1, starting transfers between devices, shards(): lax.all_to_all(paired, 'pix', split_axis=0, concat_axis=0, tiled=True)  3.41 us
  transfers between devices with their start and end apart: 12, of which 4 were waited for; matrix products, arithmetic and copies ran while one was open for 0% of the time, Pallas kernels for 3%

profile of v5, /device:TPU:0, one launch (start us, length us, event | category | flops | bytes accessed | tf_op | source)
XLA Modules:
  0.0 115.0 jit_solution(2303448164797683654)
XLA Ops:
  0.7 0.0 copy-start
  0.7 0.0 copy-start.5
  0.7 0.0 copy-start.14
  0.7 0.0 copy-start.12
  0.7 0.0 copy-start.2
  0.7 0.0 copy-start.6
  0.7 0.0 copy-start.1
  0.7 0.0 copy-start.4
  0.7 0.0 copy-start.3
  0.7 0.0 copy-start.9
  0.8 0.0 copy-start.8
  0.8 0.0 copy-start.13
  0.8 3.4 %prep.1 = (bf16[272,8,128]{2,1,0:T(8,128)(2,1)}, f32[8,128]{1,0:T(8,128)}, s32[128]{0:T(128)}) custom-call(s32[1]{0:T(128)} %bitcast.1.me_ref.refs_1_.spot_ref, s32[128]{0:T(128)} %dest_ref.1, bf16[3072,128]{1,0:T(8,128)(2,1)} %bitcast.28, s32[1,128]{1,0:T(1,128)} %bitcast.32, s32[24,128]{1,0:T(8,128)} %bitcast.30, s32[1,128]{1,0:T(1,128)} %bitcast.31), custom_call_target="tpu_custom_call" | custom-call | tf_op jit(solution)/shard_map/prep/pallas_call | solution.py:221
  4.2 7.3 %all-to-all-start = ((bf16[8,34,8,128]{3,2,1,0:T(8,128)(2,1)}), bf16[8,34,8,128]{3,2,1,0:T(8,128)(2,1)S(1)}, u32[]{:S(2)}, u32[]{:S(2)}) async-start(bf16[8,34,8,128]{3,2,1,0:T(8,128)(2,1)} %bitcast.29), calls=%async_computation | async-start | bytes 1114112 | tf_op jit(solution)/shard_map/all_to_all | solution.py:1120
  11.5 15.2 %all-to-all-done = bf16[8,34,8,128]{3,2,1,0:T(8,128)(2,1)S(1)} async-done(((bf16[8,34,8,128]{3,2,1,0:T(8,128)(2,1)}), bf16[8,34,8,128]{3,2,1,0:T(8,128)(2,1)S(1)}, u32[]{:S(2)}, u32[]{:S(2)}) %all-to-all-start) | async-done | bytes 557088 | tf_op jit(solution)/shard_map/all_to_all | solution.py:1120
  26.7 0.0 copy-done
  26.8 0.0 copy-start.10
  26.8 0.6 copy-done.10
  27.4 35.3 %layers.1 = (f32[128,24,128]{2,1,0:T(8,128)}, bf16[1664,128]{1,0:T(8,128)(2,1)S(1)}, bf16[1664,128]{1,0:T(8,128)(2,1)S(1)}, bf16[32,8,128]{2,1,0:T(8,128)(2,1)S(...) custom-call(s32[1]{0:T(128)} %bitcast.refs_0_, ...), custom_call_target="tpu_custom_call" | custom-call | tf_op jit(solution)/shard_map/layers/pallas_call | solution.py:972
  62.7 0.1 collective-permute-start
  62.8 1.7 %collective-permute-done = bf16[1664,128]{1,0:T(8,128)(2,1)S(1)} collective-permute-done((bf16[1664,128]{1,0:T(8,128)(2,1)S(1)}, bf16[1664,128]{1,0:T(8,128)(2,1)S(1)}, u32[]{:S(2)}, u32[]{:S(2)}) %collective-permute-start) | collective-permute-done | bytes 426016 | tf_op jit(solution)/shard_map/ppermute | solution.py:1147
  64.5 0.6 pair_sum.1
  65.1 1.6 %collective-permute-start.1 = (bf16[8,104,128]{2,1,0:T(8,128)(2,1)S(1)}, bf16[8,104,128]{2,1,0:T(8,128)(2,1)S(1)}, u32[]{:S(2)}, u32[]{:S(2)}) collective-permute-start(bf16[8,104,128]{2,1,0:T(8,128)(2,1)S(1)} %get-tuple-element.55), channel_id=1, source_target_pairs={{0,2},{1,3},{2,0},{3,1},{4,6},{5,7},{6,4},{7,5},{8,10},{9,11},{10,... | collective-permute-start | bytes 638984 | tf_op jit(solution)/shard_map/ppermute | solution.py:1159
  66.7 0.1 collective-permute-start.2
  66.8 6.1 %collective-permute-done.2.refs_4_ = bf16[32,8,128]{2,1,0:T(8,128)(2,1)S(1)} collective-permute-done((bf16[32,8,128]{2,1,0:T(8,128)(2,1)S(1)}, bf16[32,8,128]{2,1,0:T(8,128)(2,1)S(1)}, u32[]{:S(2)}, u32[]{:S(2)}) %collective-permute-start.2) | collective-permute-done | bytes 65568 | tf_op jit(solution)/shard_map/ppermute | solution.py:1169
  72.9 0.0 collective-permute-done.1.theirs_ref
  72.9 1.3 %quad_sum.1 = bf16[8,104,128]{2,1,0:T(8,128)(2,1)} custom-call(bf16[8,104,128]{2,1,0:T(8,128)(2,1)S(1)} %get-tuple-element.54.mine_ref, bf16[8,104,128]{2,1,0:T(8,128)(2,1)S(1)} %collective-permute-done.1.theirs_ref), custom_call_target="tpu_custom_call" | custom-call | tf_op jit(solution)/shard_map/quad_sum/pallas_call | solution.py:1172
  74.2 3.4 %all-to-all-start.1 = ((bf16[8,104,128]{2,1,0:T(8,128)(2,1)}), bf16[8,104,128]{2,1,0:T(8,128)(2,1)S(1)}, u32[]{:S(2)}, u32[]{:S(2)}) async-start(bf16[8,104,128]{2,1,0:T(8,128)(2,1)} %quad_sum.1), calls=%async_computation.1 | async-start | bytes 425984 | tf_op jit(solution)/shard_map/all_to_all | solution.py:1189
  77.6 4.7 %collective-permute-start.3 = (bf16[32,8,128]{2,1,0:T(8,128)(2,1)S(1)}, bf16[32,8,128]{2,1,0:T(8,128)(2,1)S(1)}, u32[]{:S(2)}, u32[]{:S(2)}) collective-permute-start(bf16[32,8,128]{2,1,0:T(8,128)(2,1)S(1)} %get-tuple-element.58), channel_id=1, source_target_pairs={{0,28},{4,0},{8,4},{12,8},{16,12},{20,16},{24,20},{28,24},{1,29},{... | collective-permute-start | bytes 196616 | tf_op jit(solution)/shard_map/ppermute | solution.py:1169
  82.2 0.6 collective-permute-start.4
  82.8 0.0 collective-permute-start.5
  82.8 2.9 %collective-permute-start.6 = (bf16[32,8,128]{2,1,0:T(8,128)(2,1)S(1)}, bf16[32,8,128]{2,1,0:T(8,128)(2,1)S(1)}, u32[]{:S(2)}, u32[]{:S(2)}) collective-permute-start(bf16[32,8,128]{2,1,0:T(8,128)(2,1)S(1)} %get-tuple-element.61), channel_id=1, source_target_pairs={{0,12},{4,16},{8,20},{12,24},{16,28},{20,0},{24,4},{28,8},{1,13},{... | collective-permute-start | bytes 196616 | tf_op jit(solution)/shard_map/ppermute | solution.py:1169
  85.7 1.5 %collective-permute-start.7 = (bf16[32,8,128]{2,1,0:T(8,128)(2,1)S(1)}, bf16[32,8,128]{2,1,0:T(8,128)(2,1)S(1)}, u32[]{:S(2)}, u32[]{:S(2)}) collective-permute-start(bf16[32,8,128]{2,1,0:T(8,128)(2,1)S(1)} %get-tuple-element.62), channel_id=1, source_target_pairs={{0,8},{4,12},{8,16},{12,20},{16,24},{20,28},{24,0},{28,4},{1,9},{5... | collective-permute-start | bytes 196616 | tf_op jit(solution)/shard_map/ppermute | solution.py:1169
  87.2 0.0 collective-permute-done.3.refs_1_
  87.2 0.0 collective-permute-start.8
  87.2 0.0 all-to-all-done.1.parts_ref
  87.2 1.0 chunk_sum.1
  88.2 0.0 collective-permute-done.4.refs_2_
  88.2 0.0 collective-permute-done.5.refs_3_
  88.2 6.6 %collective-permute-done.6.refs_5_ = bf16[32,8,128]{2,1,0:T(8,128)(2,1)S(1)} collective-permute-done((bf16[32,8,128]{2,1,0:T(8,128)(2,1)S(1)}, bf16[32,8,128]{2,1,0:T(8,128)(2,1)S(1)}, u32[]{:S(2)}, u32[]{:S(2)}) %collective-permute-start.6) | collective-permute-done | bytes 65568 | tf_op jit(solution)/shard_map/ppermute | solution.py:1169
  94.8 0.0 collective-permute-done.7.refs_6_
  94.8 0.0 collective-permute-done.8.refs_7_
  94.8 14.7 %all_to_all.15 = bf16[16,104,128]{2,1,0:T(8,128)(2,1)S(1)} all-to-all(bf16[16,104,128]{2,1,0:T(8,128)(2,1)S(1)} %chunk_sum.1), channel_id=1, replica_groups={{0,2,4,6,8,10,12,14,16,18,20,22,24,26,28,30},{1,3,5,7,9,11,13,15,17,19,..., dimensions={0} | all-to-all | bytes 851968 | tf_op jit(solution)/shard_map/all_to_all | solution.py:1143
  109.5 0.0 collective-permute-start.9
  109.5 0.0 copy-done.7
  109.5 3.0 %restore.1 = f32[3072,128]{1,0:T(8,128)} custom-call(s32[1]{0:T(128)} %bitcast.1.me_ref.refs_1_.spot_ref, s32[128]{0:T(128)S(1)} %copy-done.11, f32[8,128]{1,0:T(8,128)S(1)} %copy-done.7, bf16[32,8,128]{2,1,0:T(8,128)(2,1)S(1)} %get-tuple-element.51.refs_0_, bf16[32,8,128]{2,1,0:T(8,128)(2,1)S(1)} %collective-permute-done.3.refs_1_, ...), custom_call_target="tpu_custom_call" | custom-call | tf_op jit(solution)/shard_map/restore/pallas_call | solution.py:1216
  112.5 0.0 collective-permute-done.9.refs_2_
  112.5 2.3 %unpack.1 = (f32[4,128]{1,0:T(4,128)}, f32[4,128]{1,0:T(4,128)}, f32[2,512]{1,0:T(2,128)}, f32[2,128]{1,0:T(2,128)}, f32[1,128]{1,0:T(1,128)}, /*index=5*/f32[24...) custom-call(s32[1]{0:T(128)} %bitcast.refs_0_, ...), custom_call_target="tpu_custom_call" | custom-call | tf_op jit(solution)/shard_map/unpack/pallas_call | solution.py:1206
  (14 shorter events, 0.0 us)
Async XLA Ops:
  0.7 26.0 %copy-start = (bf16[128,24,128]{2,1,0:T(8,128)(2,1)S(1)}, bf16[128,24,128]{2,1,0:T(8,128)(2,1)}, u32[]{:S(2)}) copy-start(bf16[128,24,128]{2,1,0:T(8,128)(2,1)} %refs_5_.1) | copy-start | bytes 2359300
  0.7 26.0 %copy-start.5 = (f32[24,128]{1,0:T(8,128)S(1)}, f32[24,128]{1,0:T(8,128)}, u32[]{:S(2)}) copy-start(f32[24,128]{1,0:T(8,128)} %refs_15_.1) | copy-start | bytes 36868
  0.7 26.0 %copy-start.14 = (f32[128]{0:T(128)S(1)}, f32[128]{0:T(128)}, u32[]{:S(2)}) copy-start(f32[128]{0:T(128)} %param.29) | copy-start | bytes 1540
  0.7 26.0 %copy-start.12 = (f32[2,128]{1,0:T(2,128)S(1)}, f32[2,128]{1,0:T(2,128)}, u32[]{:S(2)}) copy-start(f32[2,128]{1,0:T(2,128)} %refs_11_.1) | copy-start | bytes 3076
  0.7 26.0 %copy-start.2 = (bf16[2,512,128]{2,1,0:T(8,128)(2,1)S(1)}, bf16[2,512,128]{2,1,0:T(8,128)(2,1)}, u32[]{:S(2)}) copy-start(bf16[2,512,128]{2,1,0:T(8,128)(2,1)} %refs_9_.1) | copy-start | bytes 786436
  0.7 26.0 %copy-start.6 = (f32[2,512]{1,0:T(2,128)S(1)}, f32[2,512]{1,0:T(2,128)}, u32[]{:S(2)}) copy-start(f32[2,512]{1,0:T(2,128)} %refs_10_.1) | copy-start | bytes 12292
  0.7 26.0 %copy-start.1 = (bf16[2,128,512]{2,1,0:T(8,128)(2,1)S(1)}, bf16[2,128,512]{2,1,0:T(8,128)(2,1)}, u32[]{:S(2)}) copy-start(bf16[2,128,512]{2,1,0:T(8,128)(2,1)} %refs_8_.1) | copy-start | bytes 786436
  0.7 26.0 %copy-start.4 = (bf16[2,128,128]{2,1,0:T(8,128)(2,1)S(1)}, bf16[2,128,128]{2,1,0:T(8,128)(2,1)}, u32[]{:S(2)}) copy-start(bf16[2,128,128]{2,1,0:T(8,128)(2,1)} %refs_7_.1) | copy-start | bytes 196612
  0.7 26.0 %copy-start.3 = (bf16[2,128,384]{2,1,0:T(8,128)(2,1)S(1)}, bf16[2,128,384]{2,1,0:T(8,128)(2,1)}, u32[]{:S(2)}) copy-start(bf16[2,128,384]{2,1,0:T(8,128)(2,1)} %refs_6_.1) | copy-start | bytes 589828
  0.7 26.0 %copy-start.9 = (f32[2,2,128]{2,1,0:T(2,128)S(1)}, f32[2,2,128]{2,1,0:T(2,128)}, u32[]{:S(2)}) copy-start(f32[2,2,128]{2,1,0:T(2,128)} %param.22) | copy-start | bytes 6148
  0.8 26.0 %copy-start.8 = (f32[2,2,128]{2,1,0:T(2,128)S(1)}, f32[2,2,128]{2,1,0:T(2,128)}, u32[]{:S(2)}) copy-start(f32[2,2,128]{2,1,0:T(2,128)} %param.21) | copy-start | bytes 6148
  0.8 26.0 %copy-start.13 = (s32[128]{0:T(128)S(1)}, s32[128]{0:T(128)}, u32[]{:S(2)}) copy-start(s32[128]{0:T(128)} %refs_3_.1) | copy-start | bytes 1540
  4.2 22.5 %all-to-all-start = ((bf16[8,34,8,128]{3,2,1,0:T(8,128)(2,1)}), bf16[8,34,8,128]{3,2,1,0:T(8,128)(2,1)S(1)}, u32[]{:S(2)}, u32[]{:S(2)}) async-start(bf16[8,34,8,128]{3,2,1,0:T(8,128)(2,1)} %bitcast.29), calls=%async_computation | async-start | bytes 1114112 | tf_op jit(solution)/shard_map/all_to_all | solution.py:1120
  26.8 0.7 copy-start.10
  62.7 1.8 %collective-permute-start = (bf16[1664,128]{1,0:T(8,128)(2,1)S(1)}, bf16[1664,128]{1,0:T(8,128)(2,1)S(1)}, u32[]{:S(2)}, u32[]{:S(2)}) collective-permute-start(bf16[1664,128]{1,0:T(8,128)(2,1)S(1)} %get-tuple-element.53), channel_id=1, source_target_pairs={{0,1},{1,0},{2,3},{3,2},{4,5},{5,4},{6,7},{7,6},{8,9},{9,8},{10,11... | collective-permute-start | bytes 1277960 | tf_op jit(solution)/shard_map/ppermute | solution.py:1147
  64.5 45.0 %copy-start.7 = (f32[8,128]{1,0:T(8,128)S(1)}, f32[8,128]{1,0:T(8,128)}, u32[]{:S(2)}) copy-start(f32[8,128]{1,0:T(8,128)} %get-tuple-element.50.pos_ref) | copy-start | bytes 12292
  64.5 45.0 %copy-start.11 = (s32[128]{0:T(128)S(1)}, s32[128]{0:T(128)}, u32[]{:S(2)}) copy-start(s32[128]{0:T(128)} %get-tuple-element.47.refs_2_.route_ref) | copy-start | bytes 1540
  65.1 7.7 %collective-permute-start.1 = (bf16[8,104,128]{2,1,0:T(8,128)(2,1)S(1)}, bf16[8,104,128]{2,1,0:T(8,128)(2,1)S(1)}, u32[]{:S(2)}, u32[]{:S(2)}) collective-permute-start(bf16[8,104,128]{2,1,0:T(8,128)(2,1)S(1)} %get-tuple-element.55), channel_id=1, source_target_pairs={{0,2},{1,3},{2,0},{3,1},{4,6},{5,7},{6,4},{7,5},{8,10},{9,11},{10,... | collective-permute-start | bytes 638984 | tf_op jit(solution)/shard_map/ppermute | solution.py:1159
  66.7 6.2 %collective-permute-start.2 = (bf16[32,8,128]{2,1,0:T(8,128)(2,1)S(1)}, bf16[32,8,128]{2,1,0:T(8,128)(2,1)S(1)}, u32[]{:S(2)}, u32[]{:S(2)}) collective-permute-start(bf16[32,8,128]{2,1,0:T(8,128)(2,1)S(1)} %get-tuple-element.56), channel_id=1, source_target_pairs={{0,16},{4,20},{8,24},{12,28},{16,0},{20,4},{24,8},{28,12},{1,17},{... | collective-permute-start | bytes 196616 | tf_op jit(solution)/shard_map/ppermute | solution.py:1169
  74.2 13.1 %all-to-all-start.1 = ((bf16[8,104,128]{2,1,0:T(8,128)(2,1)}), bf16[8,104,128]{2,1,0:T(8,128)(2,1)S(1)}, u32[]{:S(2)}, u32[]{:S(2)}) async-start(bf16[8,104,128]{2,1,0:T(8,128)(2,1)} %quad_sum.1), calls=%async_computation.1 | async-start | bytes 425984 | tf_op jit(solution)/shard_map/all_to_all | solution.py:1189
  77.6 9.6 %collective-permute-start.3 = (bf16[32,8,128]{2,1,0:T(8,128)(2,1)S(1)}, bf16[32,8,128]{2,1,0:T(8,128)(2,1)S(1)}, u32[]{:S(2)}, u32[]{:S(2)}) collective-permute-start(bf16[32,8,128]{2,1,0:T(8,128)(2,1)S(1)} %get-tuple-element.58), channel_id=1, source_target_pairs={{0,28},{4,0},{8,4},{12,8},{16,12},{20,16},{24,20},{28,24},{1,29},{... | collective-permute-start | bytes 196616 | tf_op jit(solution)/shard_map/ppermute | solution.py:1169
  82.2 6.0 %collective-permute-start.4 = (bf16[32,8,128]{2,1,0:T(8,128)(2,1)S(1)}, bf16[32,8,128]{2,1,0:T(8,128)(2,1)S(1)}, u32[]{:S(2)}, u32[]{:S(2)}) collective-permute-start(bf16[32,8,128]{2,1,0:T(8,128)(2,1)S(1)} %get-tuple-element.59), channel_id=1, source_target_pairs={{0,24},{4,28},{8,0},{12,4},{16,8},{20,12},{24,16},{28,20},{1,25},{... | collective-permute-start | bytes 196616 | tf_op jit(solution)/shard_map/ppermute | solution.py:1169
  82.8 5.4 %collective-permute-start.5 = (bf16[32,8,128]{2,1,0:T(8,128)(2,1)S(1)}, bf16[32,8,128]{2,1,0:T(8,128)(2,1)S(1)}, u32[]{:S(2)}, u32[]{:S(2)}) collective-permute-start(bf16[32,8,128]{2,1,0:T(8,128)(2,1)S(1)} %get-tuple-element.60), channel_id=1, source_target_pairs={{0,20},{4,24},{8,28},{12,0},{16,4},{20,8},{24,12},{28,16},{1,21},{... | collective-permute-start | bytes 196616 | tf_op jit(solution)/shard_map/ppermute | solution.py:1169
  82.8 12.0 %collective-permute-start.6 = (bf16[32,8,128]{2,1,0:T(8,128)(2,1)S(1)}, bf16[32,8,128]{2,1,0:T(8,128)(2,1)S(1)}, u32[]{:S(2)}, u32[]{:S(2)}) collective-permute-start(bf16[32,8,128]{2,1,0:T(8,128)(2,1)S(1)} %get-tuple-element.61), channel_id=1, source_target_pairs={{0,12},{4,16},{8,20},{12,24},{16,28},{20,0},{24,4},{28,8},{1,13},{... | collective-permute-start | bytes 196616 | tf_op jit(solution)/shard_map/ppermute | solution.py:1169
  85.7 9.1 %collective-permute-start.7 = (bf16[32,8,128]{2,1,0:T(8,128)(2,1)S(1)}, bf16[32,8,128]{2,1,0:T(8,128)(2,1)S(1)}, u32[]{:S(2)}, u32[]{:S(2)}) collective-permute-start(bf16[32,8,128]{2,1,0:T(8,128)(2,1)S(1)} %get-tuple-element.62), channel_id=1, source_target_pairs={{0,8},{4,12},{8,16},{12,20},{16,24},{20,28},{24,0},{28,4},{1,9},{5... | collective-permute-start | bytes 196616 | tf_op jit(solution)/shard_map/ppermute | solution.py:1169
  87.2 7.6 %collective-permute-start.8 = (bf16[32,8,128]{2,1,0:T(8,128)(2,1)S(1)}, bf16[32,8,128]{2,1,0:T(8,128)(2,1)S(1)}, u32[]{:S(2)}, u32[]{:S(2)}) collective-permute-start(bf16[32,8,128]{2,1,0:T(8,128)(2,1)S(1)} %get-tuple-element.63), channel_id=1, source_target_pairs={{0,4},{4,8},{8,12},{12,16},{16,20},{20,24},{24,28},{28,0},{1,5},{5... | collective-permute-start | bytes 196616 | tf_op jit(solution)/shard_map/ppermute | solution.py:1169
  109.5 3.0 %collective-permute-start.9 = (bf16[1664,128]{1,0:T(8,128)(2,1)S(1)}, bf16[1664,128]{1,0:T(8,128)(2,1)S(1)}, u32[]{:S(2)}, u32[]{:S(2)}) collective-permute-start(bf16[1664,128]{1,0:T(8,128)(2,1)S(1)} %bitcast.20), channel_id=1, source_target_pairs={{0,1},{1,0},{2,3},{3,2},{4,5},{5,4},{6,7},{7,6},{8,9},{9,8},{10,11... | collective-permute-start | bytes 1277960 | tf_op jit(solution)/shard_map/ppermute | solution.py:1203

commit v6 on v5

--- a/solution.py
+++ b/solution.py
@@ -638,24 +638,29 @@
         steps += [functools.partial(low, start) for start in self.chunks()]
 
         def back():
+            v.grad_act = nn(d.gl[...], b.down_t[1])
+
+        def weights_down():
             b.d_down[1] += tn(d.gl[...], d.act[...])
             b.d_b_down[1] += fold_rows(d.g[...])
-            v.grad_act = nn(d.gl[...], b.down_t[1])
 
         steps.append(back)
 
         def unbend(start):
             d.gh[pl.ds(start, 16)] = (v.grad_act[start : start + 16] * d.slope[pl.ds(start, 16)]).astype(BF)
 
-        steps += [functools.partial(unbend, start) for start in range(0, self.rows, 16)]
+        bends = [functools.partial(unbend, start) for start in range(0, self.rows, 16)]
+        steps += bends[:4] + [weights_down] + bends[4:]
 
         def end():
+            d.gn2[...] = nn(d.gh[...], b.up_t[1])
+
+        def weights_up():
             weights, bias = with_bias(d.n2[...], d.gh[...])
             b.d_up[1] += weights
             b.d_b_up[1] += bias
-            d.gn2[...] = nn(d.gh[...], b.up_t[1])
-
-        steps.append(end)
+
+        steps += [end, weights_up]
         return steps
 
     def retreat(self):
@@ -674,8 +679,10 @@
 
         steps += [functools.partial(norm, start) for start in self.chunks()]
 
+        def weights_out():
+            b.d_out[1] += tn(d.att[...], d.gl[...])
+
         def out():
-            b.d_out[1] += tn(d.att[...], d.gl[...])
             v.grad_att = nn(d.gl[...], b.out_t[1])
             v.grad, v.prob, v.grad_p, v.grad_s, v.grad_v, v.grad_k, v.grad_q = ({} for _ in range(7))
 
@@ -714,6 +721,8 @@
         for first in range(0, GROUP, BATCH):
             for stage, stride in ((spread, 2), (values, 2), (soft, 1), (keys, 2), (queries, 2), (gather, 1)):
                 steps += [functools.partial(stage, member) for member in range(first, first + BATCH, stride)]
+                if stage is soft and first == 0:
+                    steps.append(weights_out)
 
         def low(start):
             where = pl.ds(start, CHUNK)
@@ -721,8 +730,10 @@
 
         steps += [functools.partial(low, start) for start in self.chunks()]
 
+        def weights_qkv():
+            b.d_qkv[1] += tn(d.n1[...], d.gqkv[...])
+
         def project():
-            b.d_qkv[1] += tn(d.n1[...], d.gqkv[...])
             v.grad_n1 = nn(d.gqkv[...], b.qkv_t[1])
             v.pos = None
 
@@ -741,6 +752,7 @@
             v.pos = part if v.pos is None else v.pos + part
             b.d_mask[...] += fold_rows(grad * d.unseen[where])
 
+        steps.append(weights_qkv)
         steps += [functools.partial(first_norm, start) for start in self.chunks()]
 
         def end():

time: 115 us -> 115 us (level)
  no operation moved by 1% of the time
where the time goes in v6:
time: 115 us
  Pallas kernels  46.4 us (40%)
  waiting for transfers between devices  29.6 us (26%)
  starting transfers between devices  22 us (19%)
  blocking collectives  14.7 us (13%)
    pallas_call x1, Pallas kernels, main_call(): pl.pallas_call(functools.partial(main_kernel, names, cap, extra, count, o...  34.8 us
    all_to_all x1, waiting for transfers between devices, shards(): lax.all_to_all(payload.reshape(count, block, VIS, width), 'pix', split_ax...  15.2 us
    all_to_all x1, blocking collectives, exchange(): lax.all_to_all(values, axes, split_axis=0, concat_axis=0, axis_index_grou...  14.7 us
    ppermute x7, waiting for transfers between devices, shards(): lax.ppermute(back[step], 'pix', [(i, (i - step) % count) for i in range(c...  12.7 us
    ppermute x7, starting transfers between devices, shards(): lax.ppermute(back[step], 'pix', [(i, (i - step) % count) for i in range(c...  9.7 us
    all_to_all x1, starting transfers between devices, shards(): lax.all_to_all(payload.reshape(count, block, VIS, width), 'pix', split_ax...  7.27 us
    pallas_call x1, Pallas kernels, prep(): pl.pallas_call(functools.partial(prep_kernel, cap, extra, count), out_sha...  3.44 us
    all_to_all x1, starting transfers between devices, shards(): lax.all_to_all(paired, 'pix', split_axis=0, concat_axis=0, tiled=True)  3.41 us
  transfers between devices with their start and end apart: 12, of which 4 were waited for; matrix products, arithmetic and copies ran while one was open for 0% of the time, Pallas kernels for 3%

profile of v6, /device:TPU:0, one launch (start us, length us, event | category | flops | bytes accessed | tf_op | source)
XLA Modules:
  0.0 114.6 jit_solution(536478422201650106)
XLA Ops:
  0.7 0.0 copy-start
  0.7 0.0 copy-start.5
  0.7 0.0 copy-start.14
  0.7 0.0 copy-start.12
  0.7 0.0 copy-start.2
  0.7 0.0 copy-start.6
  0.7 0.0 copy-start.1
  0.7 0.0 copy-start.4
  0.7 0.0 copy-start.3
  0.7 0.0 copy-start.9
  0.8 0.0 copy-start.8
  0.8 0.0 copy-start.13
  0.8 3.4 %prep.1 = (bf16[272,8,128]{2,1,0:T(8,128)(2,1)}, f32[8,128]{1,0:T(8,128)}, s32[128]{0:T(128)}) custom-call(s32[1]{0:T(128)} %bitcast.1.me_ref.refs_1_.spot_ref, s32[128]{0:T(128)} %dest_ref.1, bf16[3072,128]{1,0:T(8,128)(2,1)} %bitcast.28, s32[1,128]{1,0:T(1,128)} %bitcast.32, s32[24,128]{1,0:T(8,128)} %bitcast.30, s32[1,128]{1,0:T(1,128)} %bitcast.31), custom_call_target="tpu_custom_call" | custom-call | tf_op jit(solution)/shard_map/prep/pallas_call | solution.py:221
  4.2 7.3 %all-to-all-start = ((bf16[8,34,8,128]{3,2,1,0:T(8,128)(2,1)}), bf16[8,34,8,128]{3,2,1,0:T(8,128)(2,1)S(1)}, u32[]{:S(2)}, u32[]{:S(2)}) async-start(bf16[8,34,8,128]{3,2,1,0:T(8,128)(2,1)} %bitcast.29), calls=%async_computation | async-start | bytes 1114112 | tf_op jit(solution)/shard_map/all_to_all | solution.py:1132
  11.5 15.2 %all-to-all-done = bf16[8,34,8,128]{3,2,1,0:T(8,128)(2,1)S(1)} async-done(((bf16[8,34,8,128]{3,2,1,0:T(8,128)(2,1)}), bf16[8,34,8,128]{3,2,1,0:T(8,128)(2,1)S(1)}, u32[]{:S(2)}, u32[]{:S(2)}) %all-to-all-start) | async-done | bytes 557088 | tf_op jit(solution)/shard_map/all_to_all | solution.py:1132
  26.7 0.0 copy-done
  26.7 0.0 copy-done.5
  26.8 0.0 copy-start.10
  26.8 0.6 copy-done.10
  27.4 34.8 %layers.1 = (f32[128,24,128]{2,1,0:T(8,128)}, bf16[1664,128]{1,0:T(8,128)(2,1)S(1)}, bf16[1664,128]{1,0:T(8,128)(2,1)S(1)}, bf16[32,8,128]{2,1,0:T(8,128)(2,1)S(...) custom-call(s32[1]{0:T(128)} %bitcast.refs_0_, ...), custom_call_target="tpu_custom_call" | custom-call | tf_op jit(solution)/shard_map/layers/pallas_call | solution.py:984
  62.2 0.1 collective-permute-start
  62.3 1.7 %collective-permute-done = bf16[1664,128]{1,0:T(8,128)(2,1)S(1)} collective-permute-done((bf16[1664,128]{1,0:T(8,128)(2,1)S(1)}, bf16[1664,128]{1,0:T(8,128)(2,1)S(1)}, u32[]{:S(2)}, u32[]{:S(2)}) %collective-permute-start) | collective-permute-done | bytes 426016 | tf_op jit(solution)/shard_map/ppermute | solution.py:1159
  64.1 0.6 pair_sum.1
  64.6 1.6 %collective-permute-start.1 = (bf16[8,104,128]{2,1,0:T(8,128)(2,1)S(1)}, bf16[8,104,128]{2,1,0:T(8,128)(2,1)S(1)}, u32[]{:S(2)}, u32[]{:S(2)}) collective-permute-start(bf16[8,104,128]{2,1,0:T(8,128)(2,1)S(1)} %get-tuple-element.55), channel_id=1, source_target_pairs={{0,2},{1,3},{2,0},{3,1},{4,6},{5,7},{6,4},{7,5},{8,10},{9,11},{10,... | collective-permute-start | bytes 638984 | tf_op jit(solution)/shard_map/ppermute | solution.py:1171
  66.2 0.1 collective-permute-start.2
  66.3 6.1 %collective-permute-done.2.refs_4_ = bf16[32,8,128]{2,1,0:T(8,128)(2,1)S(1)} collective-permute-done((bf16[32,8,128]{2,1,0:T(8,128)(2,1)S(1)}, bf16[32,8,128]{2,1,0:T(8,128)(2,1)S(1)}, u32[]{:S(2)}, u32[]{:S(2)}) %collective-permute-start.2) | collective-permute-done | bytes 65568 | tf_op jit(solution)/shard_map/ppermute | solution.py:1181
  72.4 0.0 collective-permute-done.1.theirs_ref
  72.4 1.3 %quad_sum.1 = bf16[8,104,128]{2,1,0:T(8,128)(2,1)} custom-call(bf16[8,104,128]{2,1,0:T(8,128)(2,1)S(1)} %get-tuple-element.54.mine_ref, bf16[8,104,128]{2,1,0:T(8,128)(2,1)S(1)} %collective-permute-done.1.theirs_ref), custom_call_target="tpu_custom_call" | custom-call | tf_op jit(solution)/shard_map/quad_sum/pallas_call | solution.py:1184
  73.7 3.4 %all-to-all-start.1 = ((bf16[8,104,128]{2,1,0:T(8,128)(2,1)}), bf16[8,104,128]{2,1,0:T(8,128)(2,1)S(1)}, u32[]{:S(2)}, u32[]{:S(2)}) async-start(bf16[8,104,128]{2,1,0:T(8,128)(2,1)} %quad_sum.1), calls=%async_computation.1 | async-start | bytes 425984 | tf_op jit(solution)/shard_map/all_to_all | solution.py:1201
  77.1 4.7 %collective-permute-start.3 = (bf16[32,8,128]{2,1,0:T(8,128)(2,1)S(1)}, bf16[32,8,128]{2,1,0:T(8,128)(2,1)S(1)}, u32[]{:S(2)}, u32[]{:S(2)}) collective-permute-start(bf16[32,8,128]{2,1,0:T(8,128)(2,1)S(1)} %get-tuple-element.58), channel_id=1, source_target_pairs={{0,28},{4,0},{8,4},{12,8},{16,12},{20,16},{24,20},{28,24},{1,29},{... | collective-permute-start | bytes 196616 | tf_op jit(solution)/shard_map/ppermute | solution.py:1181
  81.8 0.6 collective-permute-start.4
  82.3 0.0 collective-permute-start.5
  82.3 2.9 %collective-permute-start.6 = (bf16[32,8,128]{2,1,0:T(8,128)(2,1)S(1)}, bf16[32,8,128]{2,1,0:T(8,128)(2,1)S(1)}, u32[]{:S(2)}, u32[]{:S(2)}) collective-permute-start(bf16[32,8,128]{2,1,0:T(8,128)(2,1)S(1)} %get-tuple-element.61), channel_id=1, source_target_pairs={{0,12},{4,16},{8,20},{12,24},{16,28},{20,0},{24,4},{28,8},{1,13},{... | collective-permute-start | bytes 196616 | tf_op jit(solution)/shard_map/ppermute | solution.py:1181
  85.3 1.5 %collective-permute-start.7 = (bf16[32,8,128]{2,1,0:T(8,128)(2,1)S(1)}, bf16[32,8,128]{2,1,0:T(8,128)(2,1)S(1)}, u32[]{:S(2)}, u32[]{:S(2)}) collective-permute-start(bf16[32,8,128]{2,1,0:T(8,128)(2,1)S(1)} %get-tuple-element.62), channel_id=1, source_target_pairs={{0,8},{4,12},{8,16},{12,20},{16,24},{20,28},{24,0},{28,4},{1,9},{5... | collective-permute-start | bytes 196616 | tf_op jit(solution)/shard_map/ppermute | solution.py:1181
  86.7 0.0 collective-permute-done.3.refs_1_
  86.7 0.0 collective-permute-start.8
  86.7 0.0 all-to-all-done.1.parts_ref
  86.7 1.0 chunk_sum.1
  87.7 0.0 collective-permute-done.4.refs_2_
  87.8 0.0 collective-permute-done.5.refs_3_
  87.8 6.6 %collective-permute-done.6.refs_5_ = bf16[32,8,128]{2,1,0:T(8,128)(2,1)S(1)} collective-permute-done((bf16[32,8,128]{2,1,0:T(8,128)(2,1)S(1)}, bf16[32,8,128]{2,1,0:T(8,128)(2,1)S(1)}, u32[]{:S(2)}, u32[]{:S(2)}) %collective-permute-start.6) | collective-permute-done | bytes 65568 | tf_op jit(solution)/shard_map/ppermute | solution.py:1181
  94.4 0.0 collective-permute-done.7.refs_6_
  94.4 0.0 collective-permute-done.8.refs_7_
  94.4 14.7 %all_to_all.15 = bf16[16,104,128]{2,1,0:T(8,128)(2,1)S(1)} all-to-all(bf16[16,104,128]{2,1,0:T(8,128)(2,1)S(1)} %chunk_sum.1), channel_id=1, replica_groups={{0,2,4,6,8,10,12,14,16,18,20,22,24,26,28,30},{1,3,5,7,9,11,13,15,17,19,..., dimensions={0} | all-to-all | bytes 851968 | tf_op jit(solution)/shard_map/all_to_all | solution.py:1155
  109.1 0.0 collective-permute-start.9
  109.1 3.0 %restore.1 = f32[3072,128]{1,0:T(8,128)} custom-call(s32[1]{0:T(128)} %bitcast.1.me_ref.refs_1_.spot_ref, s32[128]{0:T(128)S(1)} %copy-done.11, f32[8,128]{1,0:T(8,128)S(1)} %copy-done.7, bf16[32,8,128]{2,1,0:T(8,128)(2,1)S(1)} %get-tuple-element.51.refs_0_, bf16[32,8,128]{2,1,0:T(8,128)(2,1)S(1)} %collective-permute-done.3.refs_1_, ...), custom_call_target="tpu_custom_call" | custom-call | tf_op jit(solution)/shard_map/restore/pallas_call | solution.py:1228
  112.1 0.0 collective-permute-done.9.refs_2_
  112.1 2.3 %unpack.1 = (f32[4,128]{1,0:T(4,128)}, f32[4,128]{1,0:T(4,128)}, f32[2,512]{1,0:T(2,128)}, f32[2,128]{1,0:T(2,128)}, f32[1,128]{1,0:T(1,128)}, /*index=5*/f32[24...) custom-call(s32[1]{0:T(128)} %bitcast.refs_0_, ...), custom_call_target="tpu_custom_call" | custom-call | tf_op jit(solution)/shard_map/unpack/pallas_call | solution.py:1218
  (14 shorter events, 0.0 us)
Async XLA Ops:
  0.7 26.0 %copy-start = (bf16[128,24,128]{2,1,0:T(8,128)(2,1)S(1)}, bf16[128,24,128]{2,1,0:T(8,128)(2,1)}, u32[]{:S(2)}) copy-start(bf16[128,24,128]{2,1,0:T(8,128)(2,1)} %refs_5_.1) | copy-start | bytes 2359300
  0.7 26.0 %copy-start.5 = (f32[24,128]{1,0:T(8,128)S(1)}, f32[24,128]{1,0:T(8,128)}, u32[]{:S(2)}) copy-start(f32[24,128]{1,0:T(8,128)} %refs_15_.1) | copy-start | bytes 36868
  0.7 26.0 %copy-start.14 = (f32[128]{0:T(128)S(1)}, f32[128]{0:T(128)}, u32[]{:S(2)}) copy-start(f32[128]{0:T(128)} %param.29) | copy-start | bytes 1540
  0.7 26.0 %copy-start.12 = (f32[2,128]{1,0:T(2,128)S(1)}, f32[2,128]{1,0:T(2,128)}, u32[]{:S(2)}) copy-start(f32[2,128]{1,0:T(2,128)} %refs_11_.1) | copy-start | bytes 3076
  0.7 26.0 %copy-start.2 = (bf16[2,512,128]{2,1,0:T(8,128)(2,1)S(1)}, bf16[2,512,128]{2,1,0:T(8,128)(2,1)}, u32[]{:S(2)}) copy-start(bf16[2,512,128]{2,1,0:T(8,128)(2,1)} %refs_9_.1) | copy-start | bytes 786436
  0.7 26.0 %copy-start.6 = (f32[2,512]{1,0:T(2,128)S(1)}, f32[2,512]{1,0:T(2,128)}, u32[]{:S(2)}) copy-start(f32[2,512]{1,0:T(2,128)} %refs_10_.1) | copy-start | bytes 12292
  0.7 26.0 %copy-start.1 = (bf16[2,128,512]{2,1,0:T(8,128)(2,1)S(1)}, bf16[2,128,512]{2,1,0:T(8,128)(2,1)}, u32[]{:S(2)}) copy-start(bf16[2,128,512]{2,1,0:T(8,128)(2,1)} %refs_8_.1) | copy-start | bytes 786436
  0.7 26.0 %copy-start.4 = (bf16[2,128,128]{2,1,0:T(8,128)(2,1)S(1)}, bf16[2,128,128]{2,1,0:T(8,128)(2,1)}, u32[]{:S(2)}) copy-start(bf16[2,128,128]{2,1,0:T(8,128)(2,1)} %refs_7_.1) | copy-start | bytes 196612
  0.7 26.0 %copy-start.3 = (bf16[2,128,384]{2,1,0:T(8,128)(2,1)S(1)}, bf16[2,128,384]{2,1,0:T(8,128)(2,1)}, u32[]{:S(2)}) copy-start(bf16[2,128,384]{2,1,0:T(8,128)(2,1)} %refs_6_.1) | copy-start | bytes 589828
  0.7 26.0 %copy-start.9 = (f32[2,2,128]{2,1,0:T(2,128)S(1)}, f32[2,2,128]{2,1,0:T(2,128)}, u32[]{:S(2)}) copy-start(f32[2,2,128]{2,1,0:T(2,128)} %param.22) | copy-start | bytes 6148
  0.8 26.0 %copy-start.8 = (f32[2,2,128]{2,1,0:T(2,128)S(1)}, f32[2,2,128]{2,1,0:T(2,128)}, u32[]{:S(2)}) copy-start(f32[2,2,128]{2,1,0:T(2,128)} %param.21) | copy-start | bytes 6148
  0.8 26.0 %copy-start.13 = (s32[128]{0:T(128)S(1)}, s32[128]{0:T(128)}, u32[]{:S(2)}) copy-start(s32[128]{0:T(128)} %refs_3_.1) | copy-start | bytes 1540
  4.2 22.5 %all-to-all-start = ((bf16[8,34,8,128]{3,2,1,0:T(8,128)(2,1)}), bf16[8,34,8,128]{3,2,1,0:T(8,128)(2,1)S(1)}, u32[]{:S(2)}, u32[]{:S(2)}) async-start(bf16[8,34,8,128]{3,2,1,0:T(8,128)(2,1)} %bitcast.29), calls=%async_computation | async-start | bytes 1114112 | tf_op jit(solution)/shard_map/all_to_all | solution.py:1132
  26.8 0.7 copy-start.10
  62.2 1.8 %collective-permute-start = (bf16[1664,128]{1,0:T(8,128)(2,1)S(1)}, bf16[1664,128]{1,0:T(8,128)(2,1)S(1)}, u32[]{:S(2)}, u32[]{:S(2)}) collective-permute-start(bf16[1664,128]{1,0:T(8,128)(2,1)S(1)} %get-tuple-element.53), channel_id=1, source_target_pairs={{0,1},{1,0},{2,3},{3,2},{4,5},{5,4},{6,7},{7,6},{8,9},{9,8},{10,11... | collective-permute-start | bytes 1277960 | tf_op jit(solution)/shard_map/ppermute | solution.py:1159
  64.1 45.0 %copy-start.7 = (f32[8,128]{1,0:T(8,128)S(1)}, f32[8,128]{1,0:T(8,128)}, u32[]{:S(2)}) copy-start(f32[8,128]{1,0:T(8,128)} %get-tuple-element.50.pos_ref) | copy-start | bytes 12292
  64.1 45.0 %copy-start.11 = (s32[128]{0:T(128)S(1)}, s32[128]{0:T(128)}, u32[]{:S(2)}) copy-start(s32[128]{0:T(128)} %get-tuple-element.47.refs_2_.route_ref) | copy-start | bytes 1540
  64.6 7.7 %collective-permute-start.1 = (bf16[8,104,128]{2,1,0:T(8,128)(2,1)S(1)}, bf16[8,104,128]{2,1,0:T(8,128)(2,1)S(1)}, u32[]{:S(2)}, u32[]{:S(2)}) collective-permute-start(bf16[8,104,128]{2,1,0:T(8,128)(2,1)S(1)} %get-tuple-element.55), channel_id=1, source_target_pairs={{0,2},{1,3},{2,0},{3,1},{4,6},{5,7},{6,4},{7,5},{8,10},{9,11},{10,... | collective-permute-start | bytes 638984 | tf_op jit(solution)/shard_map/ppermute | solution.py:1171
  66.2 6.2 %collective-permute-start.2 = (bf16[32,8,128]{2,1,0:T(8,128)(2,1)S(1)}, bf16[32,8,128]{2,1,0:T(8,128)(2,1)S(1)}, u32[]{:S(2)}, u32[]{:S(2)}) collective-permute-start(bf16[32,8,128]{2,1,0:T(8,128)(2,1)S(1)} %get-tuple-element.56), channel_id=1, source_target_pairs={{0,16},{4,20},{8,24},{12,28},{16,0},{20,4},{24,8},{28,12},{1,17},{... | collective-permute-start | bytes 196616 | tf_op jit(solution)/shard_map/ppermute | solution.py:1181
  73.7 13.1 %all-to-all-start.1 = ((bf16[8,104,128]{2,1,0:T(8,128)(2,1)}), bf16[8,104,128]{2,1,0:T(8,128)(2,1)S(1)}, u32[]{:S(2)}, u32[]{:S(2)}) async-start(bf16[8,104,128]{2,1,0:T(8,128)(2,1)} %quad_sum.1), calls=%async_computation.1 | async-start | bytes 425984 | tf_op jit(solution)/shard_map/all_to_all | solution.py:1201
  77.1 9.6 %collective-permute-start.3 = (bf16[32,8,128]{2,1,0:T(8,128)(2,1)S(1)}, bf16[32,8,128]{2,1,0:T(8,128)(2,1)S(1)}, u32[]{:S(2)}, u32[]{:S(2)}) collective-permute-start(bf16[32,8,128]{2,1,0:T(8,128)(2,1)S(1)} %get-tuple-element.58), channel_id=1, source_target_pairs={{0,28},{4,0},{8,4},{12,8},{16,12},{20,16},{24,20},{28,24},{1,29},{... | collective-permute-start | bytes 196616 | tf_op jit(solution)/shard_map/ppermute | solution.py:1181
  81.8 6.0 %collective-permute-start.4 = (bf16[32,8,128]{2,1,0:T(8,128)(2,1)S(1)}, bf16[32,8,128]{2,1,0:T(8,128)(2,1)S(1)}, u32[]{:S(2)}, u32[]{:S(2)}) collective-permute-start(bf16[32,8,128]{2,1,0:T(8,128)(2,1)S(1)} %get-tuple-element.59), channel_id=1, source_target_pairs={{0,24},{4,28},{8,0},{12,4},{16,8},{20,12},{24,16},{28,20},{1,25},{... | collective-permute-start | bytes 196616 | tf_op jit(solution)/shard_map/ppermute | solution.py:1181
  82.3 5.4 %collective-permute-start.5 = (bf16[32,8,128]{2,1,0:T(8,128)(2,1)S(1)}, bf16[32,8,128]{2,1,0:T(8,128)(2,1)S(1)}, u32[]{:S(2)}, u32[]{:S(2)}) collective-permute-start(bf16[32,8,128]{2,1,0:T(8,128)(2,1)S(1)} %get-tuple-element.60), channel_id=1, source_target_pairs={{0,20},{4,24},{8,28},{12,0},{16,4},{20,8},{24,12},{28,16},{1,21},{... | collective-permute-start | bytes 196616 | tf_op jit(solution)/shard_map/ppermute | solution.py:1181
  82.3 12.0 %collective-permute-start.6 = (bf16[32,8,128]{2,1,0:T(8,128)(2,1)S(1)}, bf16[32,8,128]{2,1,0:T(8,128)(2,1)S(1)}, u32[]{:S(2)}, u32[]{:S(2)}) collective-permute-start(bf16[32,8,128]{2,1,0:T(8,128)(2,1)S(1)} %get-tuple-element.61), channel_id=1, source_target_pairs={{0,12},{4,16},{8,20},{12,24},{16,28},{20,0},{24,4},{28,8},{1,13},{... | collective-permute-start | bytes 196616 | tf_op jit(solution)/shard_map/ppermute | solution.py:1181
  85.3 9.1 %collective-permute-start.7 = (bf16[32,8,128]{2,1,0:T(8,128)(2,1)S(1)}, bf16[32,8,128]{2,1,0:T(8,128)(2,1)S(1)}, u32[]{:S(2)}, u32[]{:S(2)}) collective-permute-start(bf16[32,8,128]{2,1,0:T(8,128)(2,1)S(1)} %get-tuple-element.62), channel_id=1, source_target_pairs={{0,8},{4,12},{8,16},{12,20},{16,24},{20,28},{24,0},{28,4},{1,9},{5... | collective-permute-start | bytes 196616 | tf_op jit(solution)/shard_map/ppermute | solution.py:1181
  86.7 7.6 %collective-permute-start.8 = (bf16[32,8,128]{2,1,0:T(8,128)(2,1)S(1)}, bf16[32,8,128]{2,1,0:T(8,128)(2,1)S(1)}, u32[]{:S(2)}, u32[]{:S(2)}) collective-permute-start(bf16[32,8,128]{2,1,0:T(8,128)(2,1)S(1)} %get-tuple-element.63), channel_id=1, source_target_pairs={{0,4},{4,8},{8,12},{12,16},{16,20},{20,24},{24,28},{28,0},{1,5},{5... | collective-permute-start | bytes 196616 | tf_op jit(solution)/shard_map/ppermute | solution.py:1181
  109.1 3.0 %collective-permute-start.9 = (bf16[1664,128]{1,0:T(8,128)(2,1)S(1)}, bf16[1664,128]{1,0:T(8,128)(2,1)S(1)}, u32[]{:S(2)}, u32[]{:S(2)}) collective-permute-start(bf16[1664,128]{1,0:T(8,128)(2,1)S(1)} %bitcast.20), channel_id=1, source_target_pairs={{0,1},{1,0},{2,3},{3,2},{4,5},{5,4},{6,7},{7,6},{8,9},{9,8},{10,11... | collective-permute-start | bytes 1277960 | tf_op jit(solution)/shard_map/ppermute | solution.py:1215
